TPU v7x, 128 devices: a whole 4x4x4 slice. The times are simulated.
128 devices in a mesh: dp: 8 (over z, core), expert: 16 (over x, y).
Axes of the slice: x: 4, y: 4, z: 4, core: 2. Of those that a mesh axis runs over, the one named last changes fastest.
Arguments:
- tokens_in: bfloat16 [16384, 4096], P(('dp', 'expert')), may hold values from -6 to 6
- out_grad: bfloat16 [16384, 4096], P(('dp', 'expert')), may hold values from -6 to 6
- expert_ids: int32 [16384, 2], P(('dp', 'expert')), may hold values from 0 to 15, as said below
- router_codes: int32 [16384, 2], P(('dp', 'expert')), may hold values from 1 to 64
- amax_history: int32 [16, 4], replicated, may hold values from -2 to 2
- w_gate: bfloat16 [16, 4096, 768], P('expert'), may hold values from -0.09375 to 0.09375
- w_up: bfloat16 [16, 4096, 768], P('expert'), may hold values from -0.09375 to 0.09375
- w_down: bfloat16 [16, 768, 4096], P('expert'), may hold values from -0.21875 to 0.21875
Outputs:
- grad_tokens: bfloat16 [16384, 4096], P(('dp', 'expert'))
- grad_gate: bfloat16 [16, 4096, 768], P('expert', 'dp')
- grad_up: bfloat16 [16, 4096, 768], P('expert', 'dp')
- grad_down: bfloat16 [16, 768, 4096], P('expert', None, 'dp')
Inputs may be any that keep to these rules, and one draw needn't show every extreme that they name: `expert_ids`: each row names 2 different experts. Among the 128 rows of one device no expert is named more than 32 times; in each data group one expert is named exactly 32 times by every device of the group.
All inputs are finite; a program needn't handle non-finite values.
Results may differ from a plain program's by a relative error of at most 0.017.
Values may be sent and summed in bfloat16 or wider, within the bound.
No kernel may reach another device: no remote copies, remote signals or barrier semaphores. Data moves between devices by JAX's collectives and lax.ppermute only.
A program may use at most 128 MiB of HBM per device.

v0:
```python
import jax
import jax.numpy as jnp
from jax import lax
from jax.sharding import PartitionSpec as P

saturation = 2.0
weight_factor = 1.0 / 64.0


def scales_of(history):
    return jnp.exp2(-jnp.max(history, axis=1).astype(jnp.float32))


def slots_of(ids, experts, cap):
    flat = ids.reshape(-1)
    marks = (flat[:, None] == jnp.arange(experts, dtype=jnp.int32)[None, :]).astype(jnp.int32)
    before = jnp.cumsum(marks, axis=0) - marks
    slot = jnp.sum(before * marks, axis=1)
    return flat * cap + slot


def quantize(grad, codes, ids, scales):
    experts = scales.shape[0]
    marks = ids[:, :, None] == jnp.arange(experts, dtype=jnp.int32)[None, None, :]
    chosen = jnp.sum(jnp.where(marks, scales[None, None, :], 0.0), axis=2)
    factor = codes.astype(jnp.float32) / 64.0 * chosen
    values = grad.astype(jnp.float32)[:, None, :] * factor[:, :, None]
    return jnp.clip(values, -saturation, saturation).astype(jnp.bfloat16)


def backward_rows(rows_x, rows_q, scale, wg, wu, wd):
    gate = jnp.dot(rows_x, wg, preferred_element_type=jnp.float32)
    up = jnp.dot(rows_x, wu, preferred_element_type=jnp.float32)
    sig = jax.nn.sigmoid(gate)
    act = gate * sig
    hidden = (act * up).astype(jnp.bfloat16)
    unscaled = (rows_q.astype(jnp.float32) / scale).astype(jnp.bfloat16)
    d_hidden = lax.dot_general(
        unscaled, wd, (((1,), (1,)), ((), ())), preferred_element_type=jnp.float32
    )
    d_gate = (d_hidden * up * sig * (1.0 + gate * (1.0 - sig))).astype(jnp.bfloat16)
    d_up = (d_hidden * act).astype(jnp.bfloat16)
    return (d_gate, d_up, hidden, unscaled)


def input_rows(d_gate, d_up, wg, wu):
    first = lax.dot_general(
        d_gate, wg, (((1,), (1,)), ((), ())), preferred_element_type=jnp.float32
    )
    second = lax.dot_general(d_up, wu, (((1,), (1,)), ((), ())), preferred_element_type=jnp.float32)
    return (first + second).astype(jnp.bfloat16)


def inner_rows(left, right):
    return lax.dot_general(
        left, right, (((0,), (0,)), ((), ())), preferred_element_type=jnp.float32
    )


def shards(tokens_in, out_grad, expert_ids, router_codes, amax_history, w_gate, w_up, w_down):
    peers = lax.axis_size("expert")
    experts = amax_history.shape[0]
    width = tokens_in.shape[1]
    topk = expert_ids.shape[1]
    cap = tokens_in.shape[0] * topk * 2 // experts
    scales = scales_of(amax_history)
    dest = slots_of(expert_ids, experts, cap)
    quant = quantize(out_grad, router_codes, expert_ids, scales).reshape(-1, width)
    repeated = jnp.repeat(tokens_in, topk, axis=0)
    xbuf = (
        jnp.zeros((experts * cap, width), jnp.bfloat16)
        .at[dest]
        .set(repeated)
        .reshape(experts, cap, width)
    )
    qbuf = (
        jnp.zeros((experts * cap, width), jnp.bfloat16)
        .at[dest]
        .set(quant)
        .reshape(experts, cap, width)
    )
    rows_x, rows_q = (
        lax.all_to_all(xbuf, "expert", split_axis=0, concat_axis=0, tiled=True),
        lax.all_to_all(qbuf, "expert", split_axis=0, concat_axis=0, tiled=True),
    )
    rows_x = rows_x.reshape(peers * cap, width)
    rows_q = rows_q.reshape(peers * cap, width)
    own_scale = scales[lax.axis_index("expert")]
    wg = w_gate[0]
    wu = w_up[0]
    wd = w_down[0]
    d_gate, d_up, hidden, unscaled = backward_rows(rows_x, rows_q, own_scale, wg, wu, wd)
    full_gate = inner_rows(rows_x, d_gate)
    full_up = inner_rows(rows_x, d_up)
    gate_part = lax.psum_scatter(
        full_gate.astype(jnp.bfloat16), "dp", scatter_dimension=0, tiled=True
    ).astype(jnp.float32)
    up_part = lax.psum_scatter(
        full_up.astype(jnp.bfloat16), "dp", scatter_dimension=0, tiled=True
    ).astype(jnp.float32)
    full_down = inner_rows(hidden, unscaled)
    down_part = lax.psum_scatter(
        full_down.astype(jnp.bfloat16), "dp", scatter_dimension=1, tiled=True
    ).astype(jnp.float32)
    grad_gate = (gate_part * weight_factor).astype(jnp.bfloat16)
    grad_up = (up_part * weight_factor).astype(jnp.bfloat16)
    grad_down = (down_part * weight_factor).astype(jnp.bfloat16)
    back_rows = input_rows(d_gate, d_up, wg, wu).reshape(peers, cap, width)
    returned = lax.all_to_all(back_rows, "expert", split_axis=0, concat_axis=0, tiled=True)
    picked = returned.reshape(experts * cap, width)[dest]
    summed = jnp.sum(picked.astype(jnp.float32).reshape(-1, topk, width), axis=1)
    grad_tokens = summed.astype(jnp.bfloat16)
    return (grad_tokens, grad_gate[None], grad_up[None], grad_down[None])


def solution(mesh):
    return jax.shard_map(
        shards,
        mesh=mesh,
        in_specs=(
            P(("dp", "expert"), None),
            P(("dp", "expert"), None),
            P(("dp", "expert"), None),
            P(("dp", "expert"), None),
            P(),
            P("expert", None, None),
            P("expert", None, None),
            P("expert", None, None),
        ),
        out_specs=(
            P(("dp", "expert"), None),
            P("expert", "dp", None),
            P("expert", "dp", None),
            P("expert", None, "dp"),
        ),
        check_vma=False,
    )
```

profile of v0, /device:TPU:1, one launch (start us, length us, event | category | flops | bytes accessed | tf_op | source)
XLA Modules:
  0.0 309.8 jit_solution(8403294706465874309)
XLA Ops:
  7.2 0.7 broadcast_multiply_fusion
  7.8 0.8 copy.20
  8.6 0.1 eq.42
  8.8 0.1 eq.38
  8.9 0.1 copy.19
  9.0 0.1 mul.75
  9.2 0.6 reduce-window.6
  9.8 0.2 slice_reduce_fusion
  10.0 3.3 %broadcast_in_dim.35 = bf16[128,2,4096]{2,1,0:T(2,128)(2,1)S(1)} broadcast(bf16[128,4096]{1,0:T(8,128)(2,1)} %param.8), dimensions={0,2} | broadcast | bytes 3145728 | tf_op jit(solution)/shard_map/broadcast_in_dim | solution.py:69
  13.3 2.2 reshape.120
  15.6 0.1 fusion.26
  15.7 7.0 %scatter_custom_fusion.1 = bf16[512,4096]{1,0:T(8,128)(2,1)} fusion(s32[256]{0:T(256)S(1)} %bitcast.68, bf16[256,4096]{1,0:T(8,128)(2,1)} %reshape.120, bf16[]{:T(256)} %constant.13.clone.1), kind=kCustom, calls=%fused_computation.23 | custom fusion | bytes 4194816 | tf_op jit(solution)/shard_map/scatter | solution.py:73
  22.7 0.0 copy-start.3
  22.7 0.0 copy-start.2
  22.7 0.0 copy-start.1
  22.7 8.1 %all-to-all-start.1 = ((bf16[16,32,4096]{2,1,0:T(8,128)(2,1)}), bf16[16,32,4096]{2,1,0:T(8,128)(2,1)}, u32[]{:S(2)}, u32[]{:S(2)}) async-start(bf16[16,32,4096]{2,1,0:T(8,128)(2,1)} %bitcast.64), calls=%async_computation.1 | async-start | bytes 8388608 | tf_op jit(solution)/shard_map/all_to_all | solution.py:83
  30.8 0.0 copy-done.3
  30.9 0.0 copy-done.2
  30.9 0.1 select_reduce_fusion
  31.0 0.0 copy-done.4
  31.0 0.1 copy.23
  31.1 0.1 mul.80
  31.2 0.0 copy-done.1
  31.2 4.1 %mul.77 = f32[128,2,4096]{2,1,0:T(2,128)} broadcast(bf16[128,4096]{1,0:T(8,128)(2,1)S(1)} %copy-done.1), dimensions={0,2} | broadcast | bytes 5242880 | tf_op jit(solution)/shard_map/mul | solution.py:27
  35.3 6.0 %mul.78 = f32[256,4096]{1,0:T(8,128)} reshape(f32[128,2,4096]{2,1,0:T(2,128)} %mul.77) | data formatting | bytes 8388608 | tf_op jit(solution)/shard_map/mul | solution.py:27
  41.3 7.9 %scatter_custom_fusion = bf16[512,4096]{1,0:T(8,128)(2,1)} fusion(s32[256]{0:T(256)S(1)} %bitcast.69, f32[256,4096]{1,0:T(8,128)} %mul.78, f32[]{:T(128)} %constant.10.clone.1, f32[256]{0:T(256)S(1)} %mul.80, f32[]{:T(128)} %constant.17.clone.1, bf16[]{:T(256)} %constant.13.clone.1), kind=kCustom, calls=%fused_computation.19 | custom fusion | flops 2097152 | bytes 8389642 | tf_op jit(solution)/shard_map/scatter | solution.py:79
  49.3 42.3 %all-to-all-done.1 = bf16[16,32,4096]{2,1,0:T(8,128)(2,1)} async-done(((bf16[16,32,4096]{2,1,0:T(8,128)(2,1)}), bf16[16,32,4096]{2,1,0:T(8,128)(2,1)}, u32[]{:S(2)}, u32[]{:S(2)}) %all-to-all-start.1) | async-done | bytes 4194336 | tf_op jit(solution)/shard_map/all_to_all | solution.py:83
  91.6 10.8 %all-to-all-start = ((bf16[16,32,4096]{2,1,0:T(8,128)(2,1)}), bf16[16,32,4096]{2,1,0:T(8,128)(2,1)}, u32[]{:S(2)}, u32[]{:S(2)}) async-start(bf16[16,32,4096]{2,1,0:T(8,128)(2,1)} %bitcast.63), calls=%async_computation | async-start | bytes 8388608 | tf_op jit(solution)/shard_map/all_to_all | solution.py:84
  102.4 0.6 reduce-scatter.8.cloned.1.call-start
  103.0 0.6 dynamic_slice.3
  103.6 7.0 %fusion.2 = f32[512,768]{1,0:T(8,128)S(1)} fusion(bf16[512,4096]{1,0:T(8,128)(2,1)} %bitcast.8, bf16[1,4096,768]{2,1,0:T(8,128)(2,1)} %param.13), kind=kOutput, calls=%fused_computation.10 | convolution fusion | flops 3221225472 | bytes 12058624 | tf_op jit(solution)/shard_map/dot_general | solution.py:32
  110.6 0.0 copy-start.6
  110.6 9.3 %fusion.6 = f32[512,768]{1,0:T(8,128)} fusion(bf16[512,4096]{1,0:T(8,128)(2,1)} %bitcast.8, bf16[1,4096,768]{2,1,0:T(8,128)(2,1)} %param.14), kind=kOutput, calls=%fused_computation.14 | convolution fusion | flops 3221225472 | bytes 12058624 | tf_op jit(solution)/shard_map/dot_general | solution.py:33
  119.9 33.8 %all-to-all-done = bf16[16,32,4096]{2,1,0:T(8,128)(2,1)} async-done(((bf16[16,32,4096]{2,1,0:T(8,128)(2,1)}), bf16[16,32,4096]{2,1,0:T(8,128)(2,1)}, u32[]{:S(2)}, u32[]{:S(2)}) %all-to-all-start) | async-done | bytes 4194336 | tf_op jit(solution)/shard_map/all_to_all | solution.py:84
  153.6 3.8 %divide_convert_fusion = bf16[16,32,4096]{2,1,0:T(8,128)(2,1)S(1)} fusion(bf16[16,32,4096]{2,1,0:T(8,128)(2,1)} %all-to-all-done, f32[]{:T(128)} %bitcast.4), kind=kLoop, calls=%fused_computation.4 | loop fusion | flops 6291456 | bytes 8388612 | tf_op jit(solution)/shard_map/convert_element_type | solution.py:37
  157.4 0.0 copy-start
  157.4 0.0 copy-done.6
  157.4 2.0 copy-done
  159.5 0.0 copy-done.7
  159.5 5.5 %convolution_convert_fusion = bf16[768,4096]{1,0:T(8,128)(2,1)} fusion(bf16[512,4096]{1,0:T(8,128)(2,1)S(1)} %bitcast.65, f32[512,768]{1,0:T(8,128)S(1)} %copy-done.7, f32[512,768]{1,0:T(8,128)S(1)} %fusion.2), kind=kOutput, calls=%fused_computation.5 | convolution fusion | flops 3226730496 | bytes 13631488 | tf_op jit(solution)/shard_map/dot_general | solution.py:55
  165.0 0.0 reduce-scatter.8.cloned.1.call-update
  165.0 0.2 reduce-scatter.6.cloned.1.call-start
  165.2 8.7 %multiply_convert_fusion.4 = (bf16[512,768]{1,0:T(8,128)(2,1)S(1)}, bf16[512,768]{1,0:T(8,128)(2,1)S(1)}) fusion(f32[512,768]{1,0:T(8,128)} %copy-done.6, f32[512,768]{1,0:T(8,128)} %fusion.6, bf16[512,4096]{1,0:T(8,128)(2,1)} %bitcast.66, bf16[1,768,4096]{2,1,0:T(8,128)(2,1)} %param.15), kind=kOutput, calls=%fused_computation.30 | convolution fusion | flops 3226337280 | bytes 15204352 | tf_op jit(solution)/shard_map/dot_general | solution.py:38
  173.9 0.0 copy-start.5
  173.9 8.6 %convolution_convert_fusion.1 = bf16[4096,768]{1,0:T(8,128)(2,1)} fusion(bf16[512,4096]{1,0:T(8,128)(2,1)} %bitcast.8, bf16[512,768]{1,0:T(8,128)(2,1)S(1)} %get-tuple-element.4), kind=kOutput, calls=%fused_computation.6 | convolution fusion | flops 3224371200 | bytes 11272192 | tf_op jit(solution)/shard_map/dot_general | solution.py:55
  182.5 0.0 reduce-scatter.6.cloned.1.call-update
  182.5 0.3 reduce-scatter.4.cloned.1.call-start
  182.8 0.0 copy-done.5
  182.8 8.4 %convolution_convert_fusion.2 = bf16[4096,768]{1,0:T(8,128)(2,1)} fusion(bf16[512,4096]{1,0:T(8,128)(2,1)} %bitcast.8, bf16[512,768]{1,0:T(8,128)(2,1)S(1)} %get-tuple-element.5), kind=kOutput, calls=%fused_computation.7 | convolution fusion | flops 3224371200 | bytes 11272192 | tf_op jit(solution)/shard_map/dot_general | solution.py:55
  191.2 0.0 reduce-scatter.4.cloned.1.call-update
  191.3 0.0 slice-start.1
  191.3 6.0 %fusion = f32[512,4096]{1,0:T(8,128)S(1)} fusion(bf16[512,768]{1,0:T(8,128)(2,1)} %copy-done.5, bf16[1,4096,768]{2,1,0:T(8,128)(2,1)} %param.13), kind=kOutput, calls=%fused_computation.8 | convolution fusion | flops 3221225472 | bytes 15466496 | tf_op jit(solution)/shard_map/dot_general | solution.py:47
  197.3 0.0 slice-done
  197.3 0.0 slice-done.1
  197.3 5.1 %add_convert_fusion = bf16[512,4096]{1,0:T(8,128)(2,1)} fusion(f32[512,4096]{1,0:T(8,128)S(1)} %fusion, bf16[512,768]{1,0:T(8,128)(2,1)S(1)} %get-tuple-element.4, bf16[1,4096,768]{2,1,0:T(8,128)(2,1)S(1)} %bitcast.73), kind=kOutput, calls=%fused_computation.3 | convolution fusion | flops 3225419776 | bytes 19660800 | tf_op jit(solution)/shard_map/dot_general | solution.py:50
  202.5 5.2 %all-to-all-start.2 = ((bf16[16,32,4096]{2,1,0:T(8,128)(2,1)}), bf16[16,32,4096]{2,1,0:T(8,128)(2,1)}, u32[]{:S(2)}, u32[]{:S(2)}) async-start(bf16[16,32,4096]{2,1,0:T(8,128)(2,1)} %bitcast.67), calls=%async_computation.2 | async-start | bytes 8388608 | tf_op jit(solution)/shard_map/all_to_all | solution.py:109
  207.7 48.2 %all-to-all-done.2 = bf16[16,32,4096]{2,1,0:T(8,128)(2,1)} async-done(((bf16[16,32,4096]{2,1,0:T(8,128)(2,1)}), bf16[16,32,4096]{2,1,0:T(8,128)(2,1)}, u32[]{:S(2)}, u32[]{:S(2)}) %all-to-all-start.2) | async-done | bytes 4194336 | tf_op jit(solution)/shard_map/all_to_all | solution.py:109
  255.9 6.6 %gather_fusion = bf16[256,4096]{1,0:T(8,128)(2,1)S(1)} fusion(bf16[512,4096]{1,0:T(8,128)(2,1)} %bitcast.12, s32[1024]{0:T(1024)S(1)} %pad_clamp_fusion), kind=kCustom, calls=%fused_computation | custom fusion | bytes 4195328 | tf_op jit(solution)/shard_map/gather | solution.py:110
  262.5 2.7 gather.6
  265.2 7.7 %reduce_sum.35 = bf16[128,4096]{1,0:T(8,128)(2,1)} reduce(bf16[128,2,4096]{2,1,0:T(2,128)(2,1)} %gather.6, bf16[]{:T(256)} %constant.13.clone.1), dimensions={1}, to_apply=%region_7.8 | reduce | flops 524288 | bytes 3145730 | tf_op jit(solution)/shard_map/reduce_sum | solution.py:111
  272.9 2.2 fusion.22
  275.1 2.2 fusion.21
  277.2 23.6 %reduce-scatter.4.cloned.1.call-done = bf16[512,768]{1,0:T(8,128)(2,1)} async-done(((bf16[4096,768]{1,0:T(8,128)(2,1)}), bf16[512,768]{1,0:T(8,128)(2,1)}) %reduce-scatter.4.cloned.1.call-update) | async-done | bytes 786448 | tf_op jit(solution)/shard_map/reduce_scatter | solution.py:95
  300.8 2.1 fusion.20
  (14 shorter events, 0.1 us)
Async XLA Ops:
  22.7 8.1 %copy-start.3 = (s32[16,4]{0,1:T(4,128)S(1)}, s32[16,4]{0,1:T(4,128)}, u32[]{:S(2)}) copy-start(s32[16,4]{0,1:T(4,128)} %param.12) | copy-start | bytes 772
  22.7 8.1 %copy-start.2 = (s32[128,2]{0,1:T(2,128)S(1)}, s32[128,2]{0,1:T(2,128)}, u32[]{:S(2)}) copy-start(s32[128,2]{0,1:T(2,128)} %param.10) | copy-start | bytes 3076
  22.7 8.2 %copy-start.4 = (s32[128,2]{0,1:T(2,128)S(1)}, s32[128,2]{0,1:T(2,128)}, u32[]{:S(2)}) copy-start(s32[128,2]{0,1:T(2,128)} %param.11) | copy-start | bytes 3076
  22.7 8.5 %copy-start.1 = (bf16[128,4096]{1,0:T(8,128)(2,1)S(1)}, bf16[128,4096]{1,0:T(8,128)(2,1)}, u32[]{:S(2)}) copy-start(bf16[128,4096]{1,0:T(8,128)(2,1)} %param.9) | copy-start | bytes 3145732
  22.7 68.9 %all-to-all-start.1 = ((bf16[16,32,4096]{2,1,0:T(8,128)(2,1)}), bf16[16,32,4096]{2,1,0:T(8,128)(2,1)}, u32[]{:S(2)}, u32[]{:S(2)}) async-start(bf16[16,32,4096]{2,1,0:T(8,128)(2,1)} %bitcast.64), calls=%async_computation.1 | async-start | bytes 8388608 | tf_op jit(solution)/shard_map/all_to_all | solution.py:83
  91.6 62.0 %all-to-all-start = ((bf16[16,32,4096]{2,1,0:T(8,128)(2,1)}), bf16[16,32,4096]{2,1,0:T(8,128)(2,1)}, u32[]{:S(2)}, u32[]{:S(2)}) async-start(bf16[16,32,4096]{2,1,0:T(8,128)(2,1)} %bitcast.63), calls=%async_computation | async-start | bytes 8388608 | tf_op jit(solution)/shard_map/all_to_all | solution.py:84
  102.4 170.5 %reduce-scatter.8.cloned.1.call-start = ((), (), s32[]{:S(2)}) async-start(), calls=%async_computation.8 | async-start | bytes 7077888 | tf_op jit(solution)/shard_map/reduce_scatter | solution.py:102
  110.6 46.8 %copy-start.6 = (f32[512,768]{1,0:T(8,128)}, f32[512,768]{1,0:T(8,128)S(1)}, u32[]{:S(2)}) copy-start(f32[512,768]{1,0:T(8,128)S(1)} %fusion.2) | copy-start | bytes 4718596
  153.6 5.8 %copy-start.7 = (f32[512,768]{1,0:T(8,128)S(1)}, f32[512,768]{1,0:T(8,128)}, u32[]{:S(2)}) copy-start(f32[512,768]{1,0:T(8,128)} %fusion.6) | copy-start | bytes 4718596
  157.4 2.0 copy-start
  165.0 110.1 %reduce-scatter.6.cloned.1.call-start = ((), (), s32[]{:S(2)}) async-start(), calls=%async_computation.7 | async-start | bytes 7077888 | tf_op jit(solution)/shard_map/reduce_scatter | solution.py:98
  173.9 8.9 %copy-start.5 = (bf16[512,768]{1,0:T(8,128)(2,1)}, bf16[512,768]{1,0:T(8,128)(2,1)S(1)}, u32[]{:S(2)}) copy-start(bf16[512,768]{1,0:T(8,128)(2,1)S(1)} %get-tuple-element.5) | copy-start | bytes 2359300
  182.5 118.3 %reduce-scatter.4.cloned.1.call-start = ((), (), s32[]{:S(2)}) async-start(), calls=%async_computation.6 | async-start | bytes 7077888 | tf_op jit(solution)/shard_map/reduce_scatter | solution.py:95
  191.2 6.1 %slice-start = ((s8[6291456]{0:T(1024)(128)(4,1)}), s8[2097152]{0:T(1024)(128)(4,1)S(1)}, s32[]{:S(2)}) async-start(s8[6291456]{0:T(1024)(128)(4,1)} %bitcast.72), calls=%async_computation.9 | async-start | bytes 4194304
  191.3 6.0 %slice-start.1 = ((s8[6291456]{0:T(1024)(128)(4,1)}), s8[4194304]{0:T(1024)(128)(4,1)S(1)}, s32[]{:S(2)}) async-start(s8[6291456]{0:T(1024)(128)(4,1)} %bitcast.72), calls=%async_computation.10 | async-start | bytes 8388608
  202.5 53.4 %all-to-all-start.2 = ((bf16[16,32,4096]{2,1,0:T(8,128)(2,1)}), bf16[16,32,4096]{2,1,0:T(8,128)(2,1)}, u32[]{:S(2)}, u32[]{:S(2)}) async-start(bf16[16,32,4096]{2,1,0:T(8,128)(2,1)} %bitcast.67), calls=%async_computation.2 | async-start | bytes 8388608 | tf_op jit(solution)/shard_map/all_to_all | solution.py:109
Sparse Core Ops, SparseCore 0:
  165.1 45.6 reduce-scatter.7
  213.2 42.2 reduce-scatter.5
  257.9 42.8 reduce-scatter.3
where the time goes:
time: 316 us; the launch traced here: 310 us
  waiting for transfers between devices  148 us (47%)
  matrix products  58.7 us (19%)
  local copies, waits for them, and re-layouts  36.4 us (12%)
  other arithmetic  27.4 us (9%)
  starting transfers between devices  25.1 us (8%)
  between operations  14.2 us (4%)
    all_to_all x1, waiting for transfers between devices, shards(): lax.all_to_all(back_rows, 'expert', split_axis=0, concat_axis=0, tiled=True)  48.2 us
    all_to_all x1, waiting for transfers between devices, shards(): lax.all_to_all(xbuf, 'expert', split_axis=0, concat_axis=0, tiled=True)  42.3 us
    all_to_all x1, waiting for transfers between devices, shards(): lax.all_to_all(qbuf, 'expert', split_axis=0, concat_axis=0, tiled=True)  33.8 us
    reduce_scatter x1, waiting for transfers between devices, shards(): lax.psum_scatter(full_gate.astype(jnp.bfloat16), 'dp', scatter_dimension=...  23.6 us
    dot_general x3, matrix products, inner_rows(): lax.dot_general(left, right, (((0,), (0,)), ((), ())), preferred_element_...  22.5 us
    all_to_all x1, starting transfers between devices, shards(): lax.all_to_all(qbuf, 'expert', split_axis=0, concat_axis=0, tiled=True)  10.8 us
    mul x3, local copies, waits for them, and re-layouts, quantize(): values = grad.astype(jnp.float32)[:, None, :] * factor[:, :, None]  10.2 us
    gather x2, local copies, waits for them, and re-layouts, shards(): picked = returned.reshape(experts * cap, width)[dest]  9.28 us
  transfers between devices with their start and end apart: 6, of which 4 were waited for; matrix products, arithmetic and copies ran while one was open for 30% of the time, Pallas kernels for 0%

commit v1 on v0

v1 whole, which is shorter than its diff:
```python
import jax
import jax.numpy as jnp
from jax import lax
from jax.experimental import pallas as pl
from jax.experimental.pallas import tpu as pltpu
from jax.sharding import PartitionSpec as P

saturation = 2.0
weight_factor = 1.0 / 64.0
MIB = 1024 * 1024


def params(limit):
    return pltpu.CompilerParams(vmem_limit_bytes=limit * MIB)


def cost(flops, nbytes):
    return pl.CostEstimate(flops=int(flops), bytes_accessed=int(nbytes), transcendentals=0)


def dot_nn(a, b):
    return lax.dot_general(a, b, (((1,), (0,)), ((), ())), preferred_element_type=jnp.float32)


def dot_nt(a, b):
    return lax.dot_general(a, b, (((1,), (1,)), ((), ())), preferred_element_type=jnp.float32)


def dot_tn(a, b):
    return lax.dot_general(a, b, (((0,), (0,)), ((), ())), preferred_element_type=jnp.float32)


def pack(tokens, grad, ids, codes, history, n_dp):
    tok, width = tokens.shape
    experts = history.shape[0]
    cap = tok * 2 * 2 // experts
    slots = experts * cap
    part = width // n_dp
    half = part // 2
    step = 4 * half
    nx = width // step
    nq = width // 2 // step

    def body(ids_ref, codes_ref, hist_ref, x_ref, g_ref, first_ref, second_ref, sel_ref, fac_ref):
        j = pl.program_id(0)

        @pl.when(j == 0)
        def _():
            rows = lax.broadcasted_iota(jnp.int32, (tok, tok), 0)
            cols = lax.broadcasted_iota(jnp.int32, (tok, tok), 1)
            eye = rows == cols

            def as_row(column):
                wide = jnp.broadcast_to(column.astype(jnp.float32), (tok, tok))
                return jnp.sum(jnp.where(eye, wide, 0.0), axis=0, keepdims=True)

            earlier = (rows < cols).astype(jnp.bfloat16)
            expert = lax.broadcasted_iota(jnp.int32, (experts, tok), 0)
            magnitude = jnp.max(hist_ref[...], axis=1, keepdims=True)
            scale = jnp.zeros((experts, 1), jnp.float32)
            inverse = jnp.zeros((experts, 1), jnp.float32)
            for value in range(-2, 3):
                scale = jnp.where(magnitude == value, 2.0**-value, scale)
                inverse = jnp.where(magnitude == value, 2.0**value, inverse)
            id_rows = [as_row(ids_ref[:, k : k + 1]).astype(jnp.int32) for k in range(2)]
            marks = [expert == row for row in id_rows]
            count = (marks[0] | marks[1]).astype(jnp.float32)
            before = dot_nn(count.astype(jnp.bfloat16), earlier)
            slot = lax.broadcasted_iota(jnp.int32, (slots, tok), 0)
            select = jnp.zeros((slots, tok), jnp.float32)
            factor = jnp.zeros((slots, tok), jnp.float32)
            unscale = jnp.zeros((slots, tok), jnp.float32)
            for k in range(2):
                place = jnp.sum(jnp.where(marks[k], before, 0.0), axis=0, keepdims=True)
                dest = id_rows[k] * cap + place.astype(jnp.int32)
                chosen = jnp.sum(jnp.where(marks[k], scale, 0.0), axis=0, keepdims=True)
                back = jnp.sum(jnp.where(marks[k], inverse, 0.0), axis=0, keepdims=True)
                weight = as_row(codes_ref[:, k : k + 1]) / 64.0 * chosen
                hit = slot == dest
                select = jnp.where(hit, 1.0, select)
                factor = jnp.where(hit, weight, factor)
                unscale = jnp.where(hit, back, unscale)
            sel_ref[...] = select.astype(jnp.bfloat16)
            fac_ref[0] = jnp.sum(factor, axis=1, keepdims=True)
            fac_ref[1] = jnp.sum(unscale, axis=1, keepdims=True)

        @pl.when(j < nx)
        def _():
            first_ref[...] = dot_nn(sel_ref[...], x_ref[...]).astype(jnp.bfloat16)

        def gradient(base, out_ref):
            for r in range(4):
                start = pl.multiple_of(base + r * part, half)
                picked = dot_nn(sel_ref[...], g_ref[:, pl.ds(start, half)])
                clipped = jnp.clip(picked * fac_ref[0], -saturation, saturation)
                rounded = clipped.astype(jnp.bfloat16).astype(jnp.float32)
                out_ref[:, r * half : (r + 1) * half] = (rounded * fac_ref[1]).astype(jnp.bfloat16)

        @pl.when((j >= nx) & (j < nx + nq))
        def _():
            gradient((j - nx) * 4 * part, first_ref)

        @pl.when(j >= nx + nq)
        def _():
            gradient((j - nx - nq) * 4 * part + half, second_ref)

    whole = lambda shape: pl.BlockSpec(shape, lambda j: (0,) * len(shape))
    return pl.pallas_call(
        body,
        grid=(nx + 2 * nq,),
        in_specs=[
            whole(ids.shape),
            whole(codes.shape),
            whole(history.shape),
            pl.BlockSpec((tok, step), lambda j: (0, jnp.minimum(j, nx - 1))),
            whole(grad.shape),
        ],
        out_specs=[
            pl.BlockSpec((slots, step), lambda j: (0, jnp.minimum(j, nx + nq - 1))),
            pl.BlockSpec((slots, step), lambda j: (0, jnp.maximum(j - nx - nq, 0))),
            whole((slots, tok)),
        ],
        out_shape=[
            jax.ShapeDtypeStruct((slots, width + width // 2), jnp.bfloat16),
            jax.ShapeDtypeStruct((slots, width // 2), jnp.bfloat16),
            jax.ShapeDtypeStruct((slots, tok), jnp.bfloat16),
        ],
        scratch_shapes=[pltpu.VMEM((2, slots, 1), jnp.float32)],
        compiler_params=params(32),
        cost_estimate=cost(4 * slots * tok * width, 12 * slots * width // 3),
        name="pack",
    )(ids, codes, history, tokens, grad)


def forward(first, w_gate, w_up):
    rows = first.shape[0]
    width, units = w_gate.shape[1:]
    block = 256

    def body(x_ref, wg_ref, wu_ref, hidden_ref, for_gate_ref, for_up_ref):
        gate = dot_nn(x_ref[...], wg_ref[...])
        up = dot_nn(x_ref[...], wu_ref[...])
        sig = jax.nn.sigmoid(gate)
        act = gate * sig
        hidden_ref[...] = (act * up).astype(jnp.bfloat16)
        for_gate_ref[...] = up * sig * (1.0 + gate * (1.0 - sig))
        for_up_ref[...] = act

    out = pl.BlockSpec((rows, block), lambda j: (0, j))
    weight = pl.BlockSpec((None, width, block), lambda j: (0, 0, j))
    return pl.pallas_call(
        body,
        grid=(units // block,),
        in_specs=[pl.BlockSpec((rows, width), lambda j: (0, 0)), weight, weight],
        out_specs=[out, out, out],
        out_shape=[
            jax.ShapeDtypeStruct((rows, units), jnp.bfloat16),
            jax.ShapeDtypeStruct((rows, units), jnp.float32),
            jax.ShapeDtypeStruct((rows, units), jnp.float32),
        ],
        compiler_params=params(40),
        cost_estimate=cost(4 * rows * width * units, 4 * width * units + 2 * rows * width),
        name="forward",
    )(first, w_gate, w_up)


def hidden_grad(buf, offset, w_down, which, n_dp, more=None):
    rows = buf.shape[0]
    units, width = w_down.shape[1:]
    part = width // n_dp
    half = part // 2
    block = 256

    def body(q_ref, wd_ref, *refs):
        total = None
        for i in range(n_dp):
            start = i * part + which * half
            term = dot_nt(q_ref[:, i * half : (i + 1) * half], wd_ref[:, start : start + half])
            total = term if total is None else total + term
        if more is None:
            refs[0][...] = total
        else:
            total = total + refs[0][...]
            refs[3][...] = (total * refs[1][...]).astype(jnp.bfloat16)
            refs[4][...] = (total * refs[2][...]).astype(jnp.bfloat16)

    tile = pl.BlockSpec((rows, block), lambda j: (0, j))
    extra = [] if more is None else list(more)
    outs = (
        [jax.ShapeDtypeStruct((rows, units), jnp.float32)]
        if more is None
        else [jax.ShapeDtypeStruct((rows, units), jnp.bfloat16)] * 2
    )
    return pl.pallas_call(
        body,
        grid=(units // block,),
        in_specs=[
            pl.BlockSpec((rows, width // 2), lambda j: (0, offset)),
            pl.BlockSpec((None, block, width), lambda j: (0, j, 0)),
        ]
        + [tile] * len(extra),
        out_specs=[tile] * len(outs),
        out_shape=outs,
        compiler_params=params(32),
        cost_estimate=cost(rows * width * units, 2 * width * units + rows * width),
        name="hidden_grad",
    )(buf, w_down, *extra)


def weight_part(kind, buf, base, width, other, places, received=None):
    rows = buf.shape[0]
    units = other.shape[1]
    shape = (width, units) if kind == "rows" else (units, width)
    half = shape[0] // 2

    def product(buf_ref, other_ref):
        if kind == "rows":
            return dot_tn(buf_ref[...], other_ref[...])
        return dot_tn(other_ref[...], buf_ref[...])

    def plain(places_ref, buf_ref, other_ref, out_ref):
        out_ref[...] = product(buf_ref, other_ref).astype(jnp.bfloat16)

    def summed(places_ref, buf_ref, other_ref, in_ref, fwd_ref, bwd_ref, keep1_ref, keep3_ref, own_ref):
        j = pl.program_id(0)
        total = product(buf_ref, other_ref) + in_ref[...].astype(jnp.float32)
        total = total.astype(jnp.bfloat16)
        low, high = total[:half], total[half:]

        @pl.when(j == 0)
        def _():
            fwd_ref[0] = low
            bwd_ref[0] = high

        @pl.when(j == 1)
        def _():
            keep1_ref[...] = low
            fwd_ref[1] = high

        @pl.when(j == 2)
        def _():
            bwd_ref[1] = low
            keep3_ref[...] = high

        @pl.when(j == 3)
        def _():
            own_ref[...] = total

    ins = [
        pl.BlockSpec((rows, width), lambda j, at: (0, base + at[j])),
        pl.BlockSpec((rows, units), lambda j, at: (0, 0)),
    ]
    flat = jnp.bfloat16
    if received is None:
        outs = pl.BlockSpec((None,) + shape, lambda j, at: (j, 0, 0))
        out_shape = jax.ShapeDtypeStruct((4,) + shape, flat)
        args = (buf, other)
    else:
        ins.append(pl.BlockSpec((None,) + shape, lambda j, at: (j, 0, 0)))
        shapes = [(2, half, shape[1])] * 2 + [(half, shape[1])] * 2 + [shape]
        outs = [pl.BlockSpec(s, lambda j, at, n=len(s): (0,) * n) for s in shapes]
        out_shape = [jax.ShapeDtypeStruct(s, flat) for s in shapes]
        args = (buf, other, received)
    return pl.pallas_call(
        plain if received is None else summed,
        grid_spec=pltpu.PrefetchScalarGridSpec(
            num_scalar_prefetch=1, grid=(4,), in_specs=ins, out_specs=outs
        ),
        out_shape=out_shape,
        compiler_params=params(32),
        cost_estimate=cost(8 * rows * width * units, 12 * width * units + 8 * rows * width),
        name="weight_part",
    )(places, *args)


def input_rows(d_gate, d_up, w_gate, w_up):
    rows, units = d_gate.shape
    width = w_gate.shape[1]
    block = 512

    def body(dg_ref, du_ref, wg_ref, wu_ref, out_ref):
        total = dot_nt(dg_ref[...], wg_ref[...]) + dot_nt(du_ref[...], wu_ref[...])
        out_ref[...] = total.astype(jnp.bfloat16)

    whole = pl.BlockSpec((rows, units), lambda j: (0, 0))
    weight = pl.BlockSpec((None, block, units), lambda j: (0, j, 0))
    return pl.pallas_call(
        body,
        grid=(width // block,),
        in_specs=[whole, whole, weight, weight],
        out_specs=pl.BlockSpec((rows, block), lambda j: (0, j)),
        out_shape=jax.ShapeDtypeStruct((rows, width), jnp.bfloat16),
        compiler_params=params(32),
        cost_estimate=cost(4 * rows * width * units, 4 * width * units + 2 * rows * width),
        name="input_rows",
    )(d_gate, d_up, w_gate, w_up)


def combine(select, returned):
    slots, tok = select.shape
    width = returned.shape[1]
    block = 1024

    def body(sel_ref, in_ref, out_ref):
        out_ref[...] = dot_tn(sel_ref[...], in_ref[...]).astype(jnp.bfloat16)

    return pl.pallas_call(
        body,
        grid=(width // block,),
        in_specs=[
            pl.BlockSpec((slots, tok), lambda j: (0, 0)),
            pl.BlockSpec((slots, block), lambda j: (0, j)),
        ],
        out_specs=pl.BlockSpec((tok, block), lambda j: (0, j)),
        out_shape=jax.ShapeDtypeStruct((tok, width), jnp.bfloat16),
        compiler_params=params(32),
        cost_estimate=cost(2 * slots * tok * width, 2 * slots * width),
        name="combine",
    )(select, returned)


def shards(tokens_in, out_grad, expert_ids, router_codes, amax_history, w_gate, w_up, w_down):
    n_dp = lax.axis_size("dp")
    peers = lax.axis_size("expert")
    width = tokens_in.shape[1]
    experts = amax_history.shape[0]
    part = width // n_dp
    half = part // 2
    place = lax.axis_index("dp")
    z, core = place // 2, place % 2
    n_z = n_dp // 2
    order = (z + jnp.array([2, 1, 3, 0], jnp.int32)) % n_z * 2
    theirs = order + (1 - core)
    ours = order + core

    swap = [(i, i ^ 1) for i in range(n_dp)]
    ahead = [(i, (i + 2) % n_dp) for i in range(n_dp)]
    behind = [(i, (i - 2) % n_dp) for i in range(n_dp)]

    def exchange(buf):
        blocks = buf.reshape(peers, -1, buf.shape[1])
        out = lax.all_to_all(blocks, "expert", split_axis=0, concat_axis=0, tiled=True)
        return out.reshape(buf.shape)

    def wide(value):
        return value.astype(jnp.float32)

    def reduced(kind, buf, base, cut, other):
        mine = weight_part(kind, buf, base, cut, other, theirs)
        got = lax.ppermute(mine, "dp", swap)
        fwd, bwd, keep1, keep3, own = weight_part(kind, buf, base, cut, other, ours, got)
        from_behind = lax.ppermute(fwd, "dp", ahead)
        from_ahead = lax.ppermute(bwd, "dp", behind)
        fwd2 = (wide(keep1) + wide(from_behind[0])).astype(jnp.bfloat16)
        bwd2 = (wide(keep3) + wide(from_ahead[0])).astype(jnp.bfloat16)
        low = lax.ppermute(fwd2, "dp", ahead)
        high = lax.ppermute(bwd2, "dp", behind)
        cut_at = own.shape[0] // 2
        first = wide(own[:cut_at]) + wide(from_ahead[1]) + wide(low)
        second = wide(own[cut_at:]) + wide(from_behind[1]) + wide(high)
        total = jnp.concatenate([first, second], axis=0)
        return (total * weight_factor).astype(jnp.bfloat16)

    first, second, select = pack(
        tokens_in, out_grad, expert_ids, router_codes, amax_history, n_dp
    )
    first = exchange(first)
    second = exchange(second)
    hidden, for_gate, for_up = forward(first, w_gate, w_up)
    down_a = reduced("columns", first, width // half, half, hidden)
    (d_hidden,) = hidden_grad(first, 2, w_down, 0, n_dp)
    down_b = reduced("columns", second, 0, half, hidden)
    d_gate, d_up = hidden_grad(second, 0, w_down, 1, n_dp, (d_hidden, for_gate, for_up))
    grad_gate = reduced("rows", first, 0, part, d_gate)
    grad_up = reduced("rows", first, 0, part, d_up)
    back = exchange(input_rows(d_gate, d_up, w_gate, w_up))
    grad_tokens = combine(select, back)
    grad_down = jnp.concatenate([down_a, down_b], axis=1)
    return (grad_tokens, grad_gate[None], grad_up[None], grad_down[None])


def solution(mesh):
    return jax.shard_map(
        shards,
        mesh=mesh,
        in_specs=(
            P(("dp", "expert"), None),
            P(("dp", "expert"), None),
            P(("dp", "expert"), None),
            P(("dp", "expert"), None),
            P(),
            P("expert", None, None),
            P("expert", None, None),
            P("expert", None, None),
        ),
        out_specs=(
            P(("dp", "expert"), None),
            P("expert", "dp", None),
            P("expert", "dp", None),
            P("expert", None, "dp"),
        ),
        check_vma=False,
    )
```

time: 316 us -> 265 us (0.84)
  waiting for transfers between devices: 148 us -> 39.9 us
  blocking collectives: 0 us -> 79.5 us
  Pallas kernels: 0 us -> 71.4 us
  matrix products: 58.7 us -> 0 us
  other arithmetic: 27.4 us -> 8.49 us
  between operations: 14.2 us -> 1 us
  local copies, waits for them, and re-layouts: 36.4 us -> 26 us
  starting transfers between devices: 25.1 us -> 34.3 us
    all_to_all x3 -> x2, waiting for transfers between devices: 124 us -> 4.17 us  [exchange(): lax.all_to_all(blocks, 'expert', split_axis=0, concat_axis=0, tiled=True)]
    all_to_all x0 -> x1, blocking collectives: none -> 79.5 us  [exchange(): lax.all_to_all(blocks, 'expert', split_axis=0, concat_axis=0, tiled=True)]
    pallas_call x0 -> x14, Pallas kernels: none -> 71.4 us  [the longest x8 36 us: weight_part(): pl.pallas_call(plain if received is None else summed, grid_spec=pltpu.Pre...]
    dot_general x8 -> x0, matrix products: 58.7 us -> none  [the longest x3 22.5 us: inner_rows(): lax.dot_general(left, right, (((0,), (0,)), ((), ())), preferred_element_...]
    ppermute x0 -> x20, waiting for transfers between devices: none -> 35.7 us  [the longest x4 22.5 us: reduced(): from_ahead = lax.ppermute(bwd, 'dp', behind)]
    ppermute x0 -> x20, starting transfers between devices: none -> 25 us  [the longest x4 11.3 us: reduced(): from_ahead = lax.ppermute(bwd, 'dp', behind)]
    reduce_scatter x3 -> x0, waiting for transfers between devices: 23.6 us -> none  [the longest x1 23.6 us: shards(): lax.psum_scatter(full_gate.astype(jnp.bfloat16), 'dp', scatter_dimension=...]
    unnamed x21 -> x61, local copies, waits for them, and re-layouts: 2.84 us -> 26 us
  transfers between devices with their start and end apart: 6 -> 22, of which waited for: 4 -> 10; matrix products, arithmetic and copies ran while one was open for 30% -> 2% of each run, Pallas kernels for 0% -> 22%
where the time goes in v1:
time: 265 us; the launch traced here: 261 us
  blocking collectives  79.5 us (30%)
  Pallas kernels  71.4 us (27%)
  waiting for transfers between devices  39.9 us (15%)
  starting transfers between devices  34.3 us (13%)
  local copies, waits for them, and re-layouts  26 us (10%)
  other arithmetic  8.49 us (3%)
    all_to_all x1, blocking collectives, exchange(): lax.all_to_all(blocks, 'expert', split_axis=0, concat_axis=0, tiled=True)  79.5 us
    pallas_call x8, Pallas kernels, weight_part(): pl.pallas_call(plain if received is None else summed, grid_spec=pltpu.Pre...  36 us
    unnamed x61, local copies, waits for them, and re-layouts  26 us
    ppermute x4, waiting for transfers between devices, reduced(): from_ahead = lax.ppermute(bwd, 'dp', behind)  22.5 us
    ppermute x4, starting transfers between devices, reduced(): from_ahead = lax.ppermute(bwd, 'dp', behind)  11.3 us
    pallas_call x1, Pallas kernels, forward(): pl.pallas_call(body, grid=(units // block,), in_specs=[pl.BlockSpec((rows...  9.72 us
    all_to_all x2, starting transfers between devices, exchange(): lax.all_to_all(blocks, 'expert', split_axis=0, concat_axis=0, tiled=True)  9.3 us
    pallas_call x1, Pallas kernels, input_rows(): pl.pallas_call(body, grid=(width // block,), in_specs=[whole, whole, weig...  8.35 us
  transfers between devices with their start and end apart: 22, of which 10 were waited for; matrix products, arithmetic and copies ran while one was open for 2% of the time, Pallas kernels for 22%

profile of v1, /device:TPU:1, one launch (start us, length us, event | category | flops | bytes accessed | tf_op | source)
XLA Modules:
  0.0 260.6 jit_solution(5597476670810876246)
XLA Ops:
  0.6 0.8 copy.13.ids_ref
  1.4 0.8 copy.14.codes_ref
  2.2 0.8 copy.15.hist_ref
  3.0 1.2 copy-done.12
  4.2 1.2 copy-done.13
  5.4 5.8 %pack.1 = (bf16[512,6144]{1,0:T(8,128)(2,1)S(1)}, bf16[512,2048]{1,0:T(8,128)(2,1)S(1)}, bf16[512,128]{1,0:T(8,128)(2,1)S(1)}) custom-call(s32[128,2]{1,0:T(8,128)S(1)} %copy.13.ids_ref, s32[128,2]{1,0:T(8,128)S(1)} %copy.14.codes_ref, s32[16,4]{1,0:T(8,128)S(1)} %copy.15.hist_ref, bf16[128,4096]{1,0:T(8,128)(2,1)S(1)} %copy-done.12, ...), custom_call_target="tpu_custom_call" | custom-call | flops 1073741824 | bytes 8388608 | tf_op jit(solution)/shard_map/pack/pallas_call | solution.py:108
  11.3 79.5 %all_to_all.15 = bf16[16,32,6144]{2,1,0:T(8,128)(2,1)} all-to-all(bf16[16,32,6144]{2,1,0:T(8,128)(2,1)S(1)} %bitcast.108), channel_id=1, replica_groups=mesh['dp'=8,'expert'=16] {'expert'}, dimensions={0} | all-to-all | bytes 12582912 | tf_op jit(solution)/shard_map/all_to_all | solution.py:342
  90.8 4.8 %all-to-all-start = ((bf16[16,32,2048]{2,1,0:T(8,128)(2,1)}), bf16[16,32,2048]{2,1,0:T(8,128)(2,1)}, u32[]{:S(2)}, u32[]{:S(2)}) async-start(bf16[16,32,2048]{2,1,0:T(8,128)(2,1)} %bitcast.110), calls=%async_computation | async-start | bytes 4194304 | tf_op jit(solution)/shard_map/all_to_all | solution.py:342
  95.6 2.8 %copy-done = bf16[16,32,6144]{2,1,0:T(8,128)(2,1)S(1)} copy-done((bf16[16,32,6144]{2,1,0:T(8,128)(2,1)S(1)}, bf16[16,32,6144]{2,1,0:T(8,128)(2,1)}, u32[]{:S(2)}) %copy-start) | copy-done | bytes 6291480
  98.4 2.8 %copy-done.2 = bf16[1,768,4096]{2,1,0:T(8,128)(2,1)S(1)} copy-done((bf16[1,768,4096]{2,1,0:T(8,128)(2,1)S(1)}, bf16[1,768,4096]{2,1,0:T(8,128)(2,1)}, u32[]{:S(2)}) %copy-start.2) | copy-done | bytes 6291480
  101.1 2.5 hidden_grad.2.refs_0_
  103.6 1.1 copy-done.4
  104.8 9.7 %forward.1 = (bf16[512,768]{1,0:T(8,128)(2,1)S(1)}, f32[512,768]{1,0:T(8,128)S(1)}, f32[512,768]{1,0:T(8,128)S(1)}) custom-call(bf16[512,6144]{1,0:T(8,128)(2,1)S(1)} %bitcast.99, bf16[1,4096,768]{2,1,0:T(8,128)(2,1)} %wg_ref.3, bf16[1,4096,768]{2,1,0:T(8,128)(2,1)} %wu_ref.3), custom_call_target="tpu_custom_call" | custom-call | flops 6442450944 | bytes 16777216 | tf_op jit(solution)/shard_map/forward/pallas_call | solution.py:151
  114.5 1.2 copy-done.8
  115.7 1.2 copy-done.10
  116.9 4.2 %all-to-all-done = bf16[16,32,2048]{2,1,0:T(8,128)(2,1)} async-done(((bf16[16,32,2048]{2,1,0:T(8,128)(2,1)}), bf16[16,32,2048]{2,1,0:T(8,128)(2,1)}, u32[]{:S(2)}, u32[]{:S(2)}) %all-to-all-start) | async-done | bytes 2097184 | tf_op jit(solution)/shard_map/all_to_all | solution.py:342
  121.0 2.9 %copy-done.3 = bf16[1,768,4096]{2,1,0:T(8,128)(2,1)S(1)} copy-done((bf16[1,768,4096]{2,1,0:T(8,128)(2,1)S(1)}, bf16[1,768,4096]{2,1,0:T(8,128)(2,1)}, u32[]{:S(2)}) %copy-start.3) | copy-done | bytes 6291480
  124.0 1.5 copy-done.5
  125.5 1.4 copy-done.9
  126.9 1.4 copy-done.11
  128.3 4.3 %hidden_grad.3 = (bf16[512,768]{1,0:T(8,128)(2,1)S(1)}, bf16[512,768]{1,0:T(8,128)(2,1)S(1)}) custom-call(bf16[512,2048]{1,0:T(8,128)(2,1)} %bitcast.1.q_ref.buf_ref, bf16[1,768,4096]{2,1,0:T(8,128)(2,1)S(1)} %copy-done.3, f32[512,768]{1,0:T(8,128)S(1)} %copy-done.5, f32[512,768]{1,0:T(8,128)S(1)} %copy-done.9, f32[512,768]{1,0:T(8,128)S(1)} %copy-done.11), custom_call_target="tpu_custom_call" | custom-call | flops 1610612736 | bytes 8388608 | tf_op jit(solution)/shard_map/hidden_grad/pallas_call | solution.py:194
  132.7 4.4 %weight_part.10 = bf16[4,512,768]{2,1,0:T(8,128)(2,1)} custom-call(s32[4]{0:T(128)S(1)} %get-tuple-element.60.places_ref, bf16[512,6144]{1,0:T(8,128)(2,1)S(1)} %bitcast.102, bf16[512,768]{1,0:T(8,128)(2,1)S(1)} %get-tuple-element.38.du_ref.other_ref), custom_call_target="tpu_custom_call" | custom-call | flops 1610612736 | bytes 6815744 | tf_op jit(solution)/shard_map/weight_part/pallas_call | solution.py:264
  137.1 5.3 %collective-permute-start.5 = (bf16[4,512,768]{2,1,0:T(8,128)(2,1)}, bf16[4,512,768]{2,1,0:T(8,128)(2,1)}, u32[]{:S(2)}, u32[]{:S(2)}) collective-permute-start(bf16[4,512,768]{2,1,0:T(8,128)(2,1)} %weight_part.10), channel_id=1, source_target_pairs={{0,16},{16,0},{32,48},{48,32},{64,80},{80,64},{96,112},{112,96},{1... | collective-permute-start | bytes 9437192 | tf_op jit(solution)/shard_map/ppermute | solution.py:350
  142.3 5.1 %weight_part.14 = bf16[4,768,256]{2,1,0:T(8,128)(2,1)} custom-call(s32[4]{0:T(128)S(1)} %get-tuple-element.60.places_ref, bf16[512,2048]{1,0:T(8,128)(2,1)} %bitcast.1.q_ref.buf_ref, bf16[512,768]{1,0:T(8,128)(2,1)S(1)} %get-tuple-element.49.other_ref), custom_call_target="tpu_custom_call" | custom-call | flops 805306368 | bytes 3407872 | tf_op jit(solution)/shard_map/weight_part/pallas_call | solution.py:264
  147.5 4.4 %weight_part.8 = bf16[4,512,768]{2,1,0:T(8,128)(2,1)} custom-call(s32[4]{0:T(128)S(1)} %get-tuple-element.60.places_ref, bf16[512,6144]{1,0:T(8,128)(2,1)S(1)} %bitcast.103, bf16[512,768]{1,0:T(8,128)(2,1)S(1)} %get-tuple-element.37.dg_ref.other_ref), custom_call_target="tpu_custom_call" | custom-call | flops 1610612736 | bytes 6815744 | tf_op jit(solution)/shard_map/weight_part/pallas_call | solution.py:264
  151.9 0.5 collective-permute-start
  152.4 3.4 %weight_part.12 = bf16[4,768,256]{2,1,0:T(8,128)(2,1)} custom-call(s32[4]{0:T(128)S(1)} %get-tuple-element.60.places_ref, bf16[512,6144]{1,0:T(8,128)(2,1)S(1)} %bitcast.104, bf16[512,768]{1,0:T(8,128)(2,1)S(1)} %get-tuple-element.49.other_ref), custom_call_target="tpu_custom_call" | custom-call | flops 805306368 | bytes 3407872 | tf_op jit(solution)/shard_map/weight_part/pallas_call | solution.py:264
  155.9 8.3 %input_rows.1 = bf16[512,4096]{1,0:T(8,128)(2,1)S(1)} custom-call(bf16[512,768]{1,0:T(8,128)(2,1)S(1)} %get-tuple-element.37.dg_ref.other_ref, bf16[512,768]{1,0:T(8,128)(2,1)S(1)} %get-tuple-element.38.du_ref.other_ref, bf16[1,4096,768]{2,1,0:T(8,128)(2,1)S(1)} %bitcast.112, bf16[1,4096,768]{2,1,0:T(8,128)(2,1)S(1)} %bitcast.114), custom_call_target="tpu_custom_call" | custom-call | flops 6442450944 | bytes 16777216 | tf_op jit(solution)/shard_map/input_rows/pallas_call | solution.py:287
  164.3 2.0 copy-done.6
  166.3 4.5 %all-to-all-start.2 = ((bf16[16,32,4096]{2,1,0:T(8,128)(2,1)}), bf16[16,32,4096]{2,1,0:T(8,128)(2,1)}, u32[]{:S(2)}, u32[]{:S(2)}) async-start(bf16[16,32,4096]{2,1,0:T(8,128)(2,1)} %bitcast.109), calls=%async_computation.2 | async-start | bytes 8388608 | tf_op jit(solution)/shard_map/all_to_all | solution.py:342
  170.8 4.2 %weight_part.15 = (bf16[2,384,256]{2,1,0:T(8,128)(2,1)S(1)}, bf16[2,384,256]{2,1,0:T(8,128)(2,1)S(1)}, bf16[384,256]{1,0:T(8,128)(2,1)S(1)}, bf16[384,256]{1,0:T(8,128)(2,1)S(1)}, bf16[768,256]{1,0:T(8,128)(2,1)S(1)}) custom-call(s32[4]{0:T(128)S(1)} %broadcast_add_fusion.1.places_ref, bf16[512,2048]{1,0:T(8,128)(2,1)} %bitcast.1.q_ref.buf_ref, ...), custom_call_target="tpu_custom_call" | custom-call | flops 805306368 | bytes 3407872 | tf_op jit(solution)/shard_map/weight_part/pallas_call | solution.py:264
  175.0 3.8 %collective-permute-start.16 = (bf16[2,384,256]{2,1,0:T(8,128)(2,1)S(1)}, bf16[2,384,256]{2,1,0:T(8,128)(2,1)S(1)}, u32[]{:S(2)}, u32[]{:S(2)}) collective-permute-start(bf16[2,384,256]{2,1,0:T(8,128)(2,1)S(1)} %get-tuple-element.56), channel_id=1, source_target_pairs={{0,96},{16,112},{32,0},{48,16},{64,32},{80,48},{96,64},{112,80},{1... | collective-permute-start | bytes 1179656 | tf_op jit(solution)/shard_map/ppermute | solution.py:353
  178.9 2.8 %copy-done.1 = bf16[16,32,6144]{2,1,0:T(8,128)(2,1)S(1)} copy-done((bf16[16,32,6144]{2,1,0:T(8,128)(2,1)S(1)}, bf16[16,32,6144]{2,1,0:T(8,128)(2,1)}, u32[]{:S(2)}) %copy-start.1) | copy-done | bytes 6291480
  181.7 4.1 %weight_part.13 = (bf16[2,384,256]{2,1,0:T(8,128)(2,1)S(1)}, bf16[2,384,256]{2,1,0:T(8,128)(2,1)S(1)}, bf16[384,256]{1,0:T(8,128)(2,1)S(1)}, bf16[384,256]{1,0:T(8,128)(2,1)S(1)}, bf16[768,256]{1,0:T(8,128)(2,1)S(1)}) custom-call(s32[4]{0:T(128)S(1)} %broadcast_add_fusion.1.places_ref, bf16[512,6144]{1,0:T(8,128)(2,1)S(1)} %bitcast.105, ...), custom_call_target="tpu_custom_call" | custom-call | flops 805306368 | bytes 3407872 | tf_op jit(solution)/shard_map/weight_part/pallas_call | solution.py:264
  185.8 2.7 %collective-permute-start.11 = (bf16[2,384,256]{2,1,0:T(8,128)(2,1)S(1)}, bf16[2,384,256]{2,1,0:T(8,128)(2,1)S(1)}, u32[]{:S(2)}, u32[]{:S(2)}) collective-permute-start(bf16[2,384,256]{2,1,0:T(8,128)(2,1)S(1)} %get-tuple-element.51), channel_id=1, source_target_pairs={{0,96},{16,112},{32,0},{48,16},{64,32},{80,48},{96,64},{112,80},{1... | collective-permute-start | bytes 1179656 | tf_op jit(solution)/shard_map/ppermute | solution.py:353
  188.6 1.5 collective-permute-done.17
  190.1 1.3 collective-permute-start.19
  191.4 4.5 %collective-permute-done.11 = bf16[2,384,256]{2,1,0:T(8,128)(2,1)S(1)} collective-permute-done((bf16[2,384,256]{2,1,0:T(8,128)(2,1)S(1)}, bf16[2,384,256]{2,1,0:T(8,128)(2,1)S(1)}, u32[]{:S(2)}, u32[]{:S(2)}) %collective-permute-start.11) | collective-permute-done | bytes 393248 | tf_op jit(solution)/shard_map/ppermute | solution.py:353
  195.9 3.2 %collective-permute-done.12 = bf16[2,384,256]{2,1,0:T(8,128)(2,1)S(1)} collective-permute-done((bf16[2,384,256]{2,1,0:T(8,128)(2,1)S(1)}, bf16[2,384,256]{2,1,0:T(8,128)(2,1)S(1)}, u32[]{:S(2)}, u32[]{:S(2)}) %collective-permute-start.12) | collective-permute-done | bytes 393248 | tf_op jit(solution)/shard_map/ppermute | solution.py:352
  199.1 0.8 collective-permute-start.14
  199.9 0.8 collective-permute-start.13
  200.7 5.2 %weight_part.11 = (bf16[2,256,768]{2,1,0:T(8,128)(2,1)S(1)}, bf16[2,256,768]{2,1,0:T(8,128)(2,1)S(1)}, bf16[256,768]{1,0:T(8,128)(2,1)S(1)}, bf16[256,768]{1,0:T(8,128)(2,1)S(1)}, bf16[512,768]{1,0:T(8,128)(2,1)S(1)}) custom-call(s32[4]{0:T(128)S(1)} %broadcast_add_fusion.1.places_ref, bf16[512,6144]{1,0:T(8,128)(2,1)S(1)} %bitcast.106, ...), custom_call_target="tpu_custom_call" | custom-call | flops 1610612736 | bytes 6815744 | tf_op jit(solution)/shard_map/weight_part/pallas_call | solution.py:264
  205.9 2.0 collective-permute-start.6
  207.9 0.1 fusion.19
  208.1 5.2 %weight_part.9 = (bf16[2,256,768]{2,1,0:T(8,128)(2,1)S(1)}, bf16[2,256,768]{2,1,0:T(8,128)(2,1)S(1)}, bf16[256,768]{1,0:T(8,128)(2,1)S(1)}, bf16[256,768]{1,0:T(8,128)(2,1)S(1)}, bf16[512,768]{1,0:T(8,128)(2,1)S(1)}) custom-call(s32[4]{0:T(128)S(1)} %broadcast_add_fusion.1.places_ref, bf16[512,6144]{1,0:T(8,128)(2,1)S(1)} %bitcast.107, ...), custom_call_target="tpu_custom_call" | custom-call | flops 1610612736 | bytes 6815744 | tf_op jit(solution)/shard_map/weight_part/pallas_call | solution.py:264
  213.3 2.7 %collective-permute-start.1 = (bf16[2,256,768]{2,1,0:T(8,128)(2,1)S(1)}, bf16[2,256,768]{2,1,0:T(8,128)(2,1)S(1)}, u32[]{:S(2)}, u32[]{:S(2)}) collective-permute-start(bf16[2,256,768]{2,1,0:T(8,128)(2,1)S(1)} %get-tuple-element.40), channel_id=1, source_target_pairs={{0,96},{16,112},{32,0},{48,16},{64,32},{80,48},{96,64},{112,80},{1... | collective-permute-start | bytes 2359304 | tf_op jit(solution)/shard_map/ppermute | solution.py:353
  216.0 0.2 fusion.23
  216.2 0.2 fusion.2
  216.5 0.9 maximum_bitcast_fusion
  217.4 4.8 %collective-permute-done.6 = bf16[2,256,768]{2,1,0:T(8,128)(2,1)S(1)} collective-permute-done((bf16[2,256,768]{2,1,0:T(8,128)(2,1)S(1)}, bf16[2,256,768]{2,1,0:T(8,128)(2,1)S(1)}, u32[]{:S(2)}, u32[]{:S(2)}) %collective-permute-start.6) | collective-permute-done | bytes 786464 | tf_op jit(solution)/shard_map/ppermute | solution.py:353
  222.3 2.5 collective-permute-start.9
  224.8 1.0 fusion.7
  225.8 13.2 %collective-permute-done.1 = bf16[2,256,768]{2,1,0:T(8,128)(2,1)S(1)} collective-permute-done((bf16[2,256,768]{2,1,0:T(8,128)(2,1)S(1)}, bf16[2,256,768]{2,1,0:T(8,128)(2,1)S(1)}, u32[]{:S(2)}, u32[]{:S(2)}) %collective-permute-start.1) | collective-permute-done | bytes 786464 | tf_op jit(solution)/shard_map/ppermute | solution.py:353
  239.1 2.5 collective-permute-start.4
  241.6 0.9 fusion.13
  242.6 4.7 %combine.1 = bf16[128,4096]{1,0:T(8,128)(2,1)} custom-call(bf16[512,128]{1,0:T(8,128)(2,1)S(1)} %get-tuple-element.32.sel_ref, bf16[512,4096]{1,0:T(8,128)(2,1)} %bitcast.5.in_ref), custom_call_target="tpu_custom_call" | custom-call | flops 536870912 | bytes 4194304 | tf_op jit(solution)/shard_map/combine/pallas_call | solution.py:307
  247.3 0.2 collective-permute-done.9
  247.5 2.2 collective-permute-done.8
  249.7 1.4 fusion.9
  251.1 1.0 fusion.1
  252.1 3.8 %collective-permute-done.4 = bf16[256,768]{1,0:T(8,128)(2,1)} collective-permute-done((bf16[256,768]{1,0:T(8,128)(2,1)S(1)}, bf16[256,768]{1,0:T(8,128)(2,1)}, u32[]{:S(2)}, u32[]{:S(2)}) %collective-permute-start.4) | collective-permute-done | bytes 393248 | tf_op jit(solution)/shard_map/ppermute | solution.py:357
  255.9 2.3 collective-permute-done.3
  258.3 1.4 fusion.15
  259.6 1.0 fusion
  (78 shorter events, 0.8 us)
Async XLA Ops:
  3.0 1.2 copy-start.12
  4.2 1.2 copy-start.13
  11.3 79.5 %copy-start.7 = (bf16[512,2048]{1,0:T(8,128)(2,1)}, bf16[512,2048]{1,0:T(8,128)(2,1)S(1)}, u32[]{:S(2)}) copy-start(bf16[512,2048]{1,0:T(8,128)(2,1)S(1)} %get-tuple-element.33) | copy-start | bytes 6291460
  90.7 4.8 %copy-start.20 = (s32[4]{0:T(128)S(1)}, s32[4]{0:T(128)}, u32[]{:S(2)}) copy-start(s32[4]{0:T(128)} %constant.51.clone) | copy-start | bytes 52
  90.7 14.0 %slice-start = ((s8[6291456]{0:T(1024)(128)(4,1)}), s8[2097152]{0:T(1024)(128)(4,1)S(1)}, s32[]{:S(2)}) async-start(s8[6291456]{0:T(1024)(128)(4,1)} %bitcast.97), calls=%async_computation.3 | async-start | bytes 4194304
  90.8 30.3 %all-to-all-start = ((bf16[16,32,2048]{2,1,0:T(8,128)(2,1)}), bf16[16,32,2048]{2,1,0:T(8,128)(2,1)}, u32[]{:S(2)}, u32[]{:S(2)}) async-start(bf16[16,32,2048]{2,1,0:T(8,128)(2,1)} %bitcast.110), calls=%async_computation | async-start | bytes 4194304 | tf_op jit(solution)/shard_map/all_to_all | solution.py:342
  95.6 2.8 %copy-start = (bf16[16,32,6144]{2,1,0:T(8,128)(2,1)S(1)}, bf16[16,32,6144]{2,1,0:T(8,128)(2,1)}, u32[]{:S(2)}) copy-start(bf16[16,32,6144]{2,1,0:T(8,128)(2,1)} %all_to_all.15) | copy-start | bytes 18874372
  98.4 2.8 %copy-start.2 = (bf16[1,768,4096]{2,1,0:T(8,128)(2,1)S(1)}, bf16[1,768,4096]{2,1,0:T(8,128)(2,1)}, u32[]{:S(2)}) copy-start(bf16[1,768,4096]{2,1,0:T(8,128)(2,1)} %wd_ref.3) | copy-start | bytes 18874372
  101.1 3.6 %slice-start.1 = ((s8[6291456]{0:T(1024)(128)(4,1)}), s8[4194304]{0:T(1024)(128)(4,1)S(1)}, s32[]{:S(2)}) async-start(s8[6291456]{0:T(1024)(128)(4,1)} %bitcast.97), calls=%async_computation.4 | async-start | bytes 8388608
  103.6 1.2 copy-start.4
  114.5 1.2 copy-start.8
  115.7 1.2 copy-start.10
  121.0 11.6 %slice-start.2 = ((s8[6291456]{0:T(1024)(128)(4,1)}), s8[4194304]{0:T(1024)(128)(4,1)S(1)}, s32[]{:S(2)}) async-start(s8[6291456]{0:T(1024)(128)(4,1)} %bitcast.100), calls=%async_computation.5 | async-start | bytes 8388608
  121.0 2.9 %copy-start.3 = (bf16[1,768,4096]{2,1,0:T(8,128)(2,1)S(1)}, bf16[1,768,4096]{2,1,0:T(8,128)(2,1)}, u32[]{:S(2)}) copy-start(bf16[1,768,4096]{2,1,0:T(8,128)(2,1)} %wd_ref.3) | copy-start | bytes 18874372
  124.0 1.5 copy-start.5
  125.5 1.4 copy-start.9
  126.9 1.4 copy-start.11
  128.3 4.3 %slice-start.3 = ((s8[6291456]{0:T(1024)(128)(4,1)}), s8[2097152]{0:T(1024)(128)(4,1)S(1)}, s32[]{:S(2)}) async-start(s8[6291456]{0:T(1024)(128)(4,1)} %bitcast.100), calls=%async_computation.6 | async-start | bytes 4194304
  137.1 62.8 %collective-permute-start.5 = (bf16[4,512,768]{2,1,0:T(8,128)(2,1)}, bf16[4,512,768]{2,1,0:T(8,128)(2,1)}, u32[]{:S(2)}, u32[]{:S(2)}) collective-permute-start(bf16[4,512,768]{2,1,0:T(8,128)(2,1)} %weight_part.10), channel_id=1, source_target_pairs={{0,16},{16,0},{32,48},{48,32},{64,80},{80,64},{96,112},{112,96},{1... | collective-permute-start | bytes 9437192 | tf_op jit(solution)/shard_map/ppermute | solution.py:350
  142.3 13.5 %slice-start.4 = ((s8[6291456]{0:T(1024)(128)(4,1)}), s8[4194304]{0:T(1024)(128)(4,1)S(1)}, s32[]{:S(2)}) async-start(s8[6291456]{0:T(1024)(128)(4,1)} %bitcast.111), calls=%async_computation.7 | async-start | bytes 8388608
  142.3 13.5 %slice-start.6 = ((s8[6291456]{0:T(1024)(128)(4,1)}), s8[2097152]{0:T(1024)(128)(4,1)S(1)}, s32[]{:S(2)}) async-start(s8[6291456]{0:T(1024)(128)(4,1)} %bitcast.113), calls=%async_computation.9 | async-start | bytes 4194304
  147.5 23.4 %collective-permute-start.15 = (bf16[4,768,256]{2,1,0:T(8,128)(2,1)}, bf16[4,768,256]{2,1,0:T(8,128)(2,1)}, u32[]{:S(2)}, u32[]{:S(2)}) collective-permute-start(bf16[4,768,256]{2,1,0:T(8,128)(2,1)} %weight_part.14), channel_id=1, source_target_pairs={{0,16},{16,0},{32,48},{48,32},{64,80},{80,64},{96,112},{112,96},{1... | collective-permute-start | bytes 4718600 | tf_op jit(solution)/shard_map/ppermute | solution.py:350
  147.5 8.4 %slice-start.5 = ((s8[6291456]{0:T(1024)(128)(4,1)}), s8[2097152]{0:T(1024)(128)(4,1)S(1)}, s32[]{:S(2)}) async-start(s8[6291456]{0:T(1024)(128)(4,1)} %bitcast.111), calls=%async_computation.8 | async-start | bytes 4194304
  147.5 8.4 %slice-start.7 = ((s8[6291456]{0:T(1024)(128)(4,1)}), s8[4194304]{0:T(1024)(128)(4,1)S(1)}, s32[]{:S(2)}) async-start(s8[6291456]{0:T(1024)(128)(4,1)} %bitcast.113), calls=%async_computation.10 | async-start | bytes 8388608
  151.9 56.2 %collective-permute-start = (bf16[4,512,768]{2,1,0:T(8,128)(2,1)}, bf16[4,512,768]{2,1,0:T(8,128)(2,1)}, u32[]{:S(2)}, u32[]{:S(2)}) collective-permute-start(bf16[4,512,768]{2,1,0:T(8,128)(2,1)} %weight_part.8), channel_id=1, source_target_pairs={{0,16},{16,0},{32,48},{48,32},{64,80},{80,64},{96,112},{112,96},{1... | collective-permute-start | bytes 9437192 | tf_op jit(solution)/shard_map/ppermute | solution.py:350
  155.8 23.0 %collective-permute-start.10 = (bf16[4,768,256]{2,1,0:T(8,128)(2,1)}, bf16[4,768,256]{2,1,0:T(8,128)(2,1)}, u32[]{:S(2)}, u32[]{:S(2)}) collective-permute-start(bf16[4,768,256]{2,1,0:T(8,128)(2,1)} %weight_part.12), channel_id=1, source_target_pairs={{0,16},{16,0},{32,48},{48,32},{64,80},{80,64},{96,112},{112,96},{1... | collective-permute-start | bytes 4718600 | tf_op jit(solution)/shard_map/ppermute | solution.py:350
  164.2 2.0 copy-start.6
  166.3 76.3 %all-to-all-start.2 = ((bf16[16,32,4096]{2,1,0:T(8,128)(2,1)}), bf16[16,32,4096]{2,1,0:T(8,128)(2,1)}, u32[]{:S(2)}, u32[]{:S(2)}) async-start(bf16[16,32,4096]{2,1,0:T(8,128)(2,1)} %bitcast.109), calls=%async_computation.2 | async-start | bytes 8388608 | tf_op jit(solution)/shard_map/all_to_all | solution.py:342
  175.0 13.5 %collective-permute-start.16 = (bf16[2,384,256]{2,1,0:T(8,128)(2,1)S(1)}, bf16[2,384,256]{2,1,0:T(8,128)(2,1)S(1)}, u32[]{:S(2)}, u32[]{:S(2)}) collective-permute-start(bf16[2,384,256]{2,1,0:T(8,128)(2,1)S(1)} %get-tuple-element.56), channel_id=1, source_target_pairs={{0,96},{16,112},{32,0},{48,16},{64,32},{80,48},{96,64},{112,80},{1... | collective-permute-start | bytes 1179656 | tf_op jit(solution)/shard_map/ppermute | solution.py:353
  178.9 11.2 %collective-permute-start.17 = (bf16[2,384,256]{2,1,0:T(8,128)(2,1)S(1)}, bf16[2,384,256]{2,1,0:T(8,128)(2,1)S(1)}, u32[]{:S(2)}, u32[]{:S(2)}) collective-permute-start(bf16[2,384,256]{2,1,0:T(8,128)(2,1)S(1)} %get-tuple-element.58), channel_id=1, source_target_pairs={{0,32},{16,48},{32,64},{48,80},{64,96},{80,112},{96,0},{112,16},{1... | collective-permute-start | bytes 1179656 | tf_op jit(solution)/shard_map/ppermute | solution.py:352
  178.9 2.8 %copy-start.1 = (bf16[16,32,6144]{2,1,0:T(8,128)(2,1)S(1)}, bf16[16,32,6144]{2,1,0:T(8,128)(2,1)}, u32[]{:S(2)}) copy-start(bf16[16,32,6144]{2,1,0:T(8,128)(2,1)} %all_to_all.15) | copy-start | bytes 18874372
  185.8 10.1 %collective-permute-start.11 = (bf16[2,384,256]{2,1,0:T(8,128)(2,1)S(1)}, bf16[2,384,256]{2,1,0:T(8,128)(2,1)S(1)}, u32[]{:S(2)}, u32[]{:S(2)}) collective-permute-start(bf16[2,384,256]{2,1,0:T(8,128)(2,1)S(1)} %get-tuple-element.51), channel_id=1, source_target_pairs={{0,96},{16,112},{32,0},{48,16},{64,32},{80,48},{96,64},{112,80},{1... | collective-permute-start | bytes 1179656 | tf_op jit(solution)/shard_map/ppermute | solution.py:353
  188.5 10.6 %collective-permute-start.12 = (bf16[2,384,256]{2,1,0:T(8,128)(2,1)S(1)}, bf16[2,384,256]{2,1,0:T(8,128)(2,1)S(1)}, u32[]{:S(2)}, u32[]{:S(2)}) collective-permute-start(bf16[2,384,256]{2,1,0:T(8,128)(2,1)S(1)} %get-tuple-element.53), channel_id=1, source_target_pairs={{0,32},{16,48},{32,64},{48,80},{64,96},{80,112},{96,0},{112,16},{1... | collective-permute-start | bytes 1179656 | tf_op jit(solution)/shard_map/ppermute | solution.py:352
  190.1 15.8 %collective-permute-start.19 = (bf16[384,256]{1,0:T(8,128)(2,1)S(1)}, bf16[384,256]{1,0:T(8,128)(2,1)S(1)}, u32[]{:S(2)}, u32[]{:S(2)}) collective-permute-start(bf16[384,256]{1,0:T(8,128)(2,1)S(1)} %fusion.16), channel_id=1, source_target_pairs={{0,96},{16,112},{32,0},{48,16},{64,32},{80,48},{96,64},{112,80},{1... | collective-permute-start | bytes 589832 | tf_op jit(solution)/shard_map/ppermute | solution.py:357
  195.9 12.1 %collective-permute-start.18 = (bf16[384,256]{1,0:T(8,128)(2,1)S(1)}, bf16[384,256]{1,0:T(8,128)(2,1)S(1)}, u32[]{:S(2)}, u32[]{:S(2)}) collective-permute-start(bf16[384,256]{1,0:T(8,128)(2,1)S(1)} %fusion.18), channel_id=1, source_target_pairs={{0,32},{16,48},{32,64},{48,80},{64,96},{80,112},{96,0},{112,16},{1... | collective-permute-start | bytes 589832 | tf_op jit(solution)/shard_map/ppermute | solution.py:356
  199.1 16.9 %collective-permute-start.14 = (bf16[384,256]{1,0:T(8,128)(2,1)S(1)}, bf16[384,256]{1,0:T(8,128)(2,1)S(1)}, u32[]{:S(2)}, u32[]{:S(2)}) collective-permute-start(bf16[384,256]{1,0:T(8,128)(2,1)S(1)} %fusion.20), channel_id=1, source_target_pairs={{0,96},{16,112},{32,0},{48,16},{64,32},{80,48},{96,64},{112,80},{1... | collective-permute-start | bytes 589832 | tf_op jit(solution)/shard_map/ppermute | solution.py:357
  199.9 16.1 %collective-permute-start.13 = (bf16[384,256]{1,0:T(8,128)(2,1)S(1)}, bf16[384,256]{1,0:T(8,128)(2,1)S(1)}, u32[]{:S(2)}, u32[]{:S(2)}) collective-permute-start(bf16[384,256]{1,0:T(8,128)(2,1)S(1)} %fusion.22), channel_id=1, source_target_pairs={{0,32},{16,48},{32,64},{48,80},{64,96},{80,112},{96,0},{112,16},{1... | collective-permute-start | bytes 589832 | tf_op jit(solution)/shard_map/ppermute | solution.py:356
  205.9 16.3 %collective-permute-start.6 = (bf16[2,256,768]{2,1,0:T(8,128)(2,1)S(1)}, bf16[2,256,768]{2,1,0:T(8,128)(2,1)S(1)}, u32[]{:S(2)}, u32[]{:S(2)}) collective-permute-start(bf16[2,256,768]{2,1,0:T(8,128)(2,1)S(1)} %get-tuple-element.45), channel_id=1, source_target_pairs={{0,96},{16,112},{32,0},{48,16},{64,32},{80,48},{96,64},{112,80},{1... | collective-permute-start | bytes 2359304 | tf_op jit(solution)/shard_map/ppermute | solution.py:353
  208.1 16.8 %collective-permute-start.7 = (bf16[2,256,768]{2,1,0:T(8,128)(2,1)S(1)}, bf16[2,256,768]{2,1,0:T(8,128)(2,1)S(1)}, u32[]{:S(2)}, u32[]{:S(2)}) collective-permute-start(bf16[2,256,768]{2,1,0:T(8,128)(2,1)S(1)} %get-tuple-element.47), channel_id=1, source_target_pairs={{0,32},{16,48},{32,64},{48,80},{64,96},{80,112},{96,0},{112,16},{1... | collective-permute-start | bytes 2359304 | tf_op jit(solution)/shard_map/ppermute | solution.py:352
  213.3 25.7 %collective-permute-start.1 = (bf16[2,256,768]{2,1,0:T(8,128)(2,1)S(1)}, bf16[2,256,768]{2,1,0:T(8,128)(2,1)S(1)}, u32[]{:S(2)}, u32[]{:S(2)}) collective-permute-start(bf16[2,256,768]{2,1,0:T(8,128)(2,1)S(1)} %get-tuple-element.40), channel_id=1, source_target_pairs={{0,96},{16,112},{32,0},{48,16},{64,32},{80,48},{96,64},{112,80},{1... | collective-permute-start | bytes 2359304 | tf_op jit(solution)/shard_map/ppermute | solution.py:353
  216.4 25.2 %collective-permute-start.2 = (bf16[2,256,768]{2,1,0:T(8,128)(2,1)S(1)}, bf16[2,256,768]{2,1,0:T(8,128)(2,1)S(1)}, u32[]{:S(2)}, u32[]{:S(2)}) collective-permute-start(bf16[2,256,768]{2,1,0:T(8,128)(2,1)S(1)} %get-tuple-element.42), channel_id=1, source_target_pairs={{0,32},{16,48},{32,64},{48,80},{64,96},{80,112},{96,0},{112,16},{1... | collective-permute-start | bytes 2359304 | tf_op jit(solution)/shard_map/ppermute | solution.py:352
  222.2 16.9 %copy-start.14 = (bf16[2,256,768]{2,1,0:T(8,128)(2,1)}, bf16[2,256,768]{2,1,0:T(8,128)(2,1)S(1)}, u32[]{:S(2)}) copy-start(bf16[2,256,768]{2,1,0:T(8,128)(2,1)S(1)} %collective-permute-done.6) | copy-start | bytes 2359300
  222.3 25.2 %collective-permute-start.9 = (bf16[256,768]{1,0:T(8,128)(2,1)S(1)}, bf16[256,768]{1,0:T(8,128)(2,1)}, u32[]{:S(2)}, u32[]{:S(2)}) collective-permute-start(bf16[256,768]{1,0:T(8,128)(2,1)S(1)} %fusion.4), channel_id=1, source_target_pairs={{0,96},{16,112},{32,0},{48,16},{64,32},{80,48},{96,64},{112,80},{1... | collective-permute-start | bytes 1179656 | tf_op jit(solution)/shard_map/ppermute | solution.py:357
  224.8 17.7 %copy-start.16 = (bf16[2,256,768]{2,1,0:T(8,128)(2,1)}, bf16[2,256,768]{2,1,0:T(8,128)(2,1)S(1)}, u32[]{:S(2)}) copy-start(bf16[2,256,768]{2,1,0:T(8,128)(2,1)S(1)} %collective-permute-done.7) | copy-start | bytes 2359300
  225.8 23.9 %collective-permute-start.8 = (bf16[256,768]{1,0:T(8,128)(2,1)}, bf16[256,768]{1,0:T(8,128)(2,1)}, u32[]{:S(2)}, u32[]{:S(2)}) collective-permute-start(bf16[256,768]{1,0:T(8,128)(2,1)} %fusion.7), channel_id=1, source_target_pairs={{0,32},{16,48},{32,64},{48,80},{64,96},{80,112},{96,0},{112,16},{1... | collective-permute-start | bytes 1179656 | tf_op jit(solution)/shard_map/ppermute | solution.py:356
  239.1 16.8 %collective-permute-start.4 = (bf16[256,768]{1,0:T(8,128)(2,1)S(1)}, bf16[256,768]{1,0:T(8,128)(2,1)}, u32[]{:S(2)}, u32[]{:S(2)}) collective-permute-start(bf16[256,768]{1,0:T(8,128)(2,1)S(1)} %fusion.10), channel_id=1, source_target_pairs={{0,96},{16,112},{32,0},{48,16},{64,32},{80,48},{96,64},{112,80},{1... | collective-permute-start | bytes 1179656 | tf_op jit(solution)/shard_map/ppermute | solution.py:357
  241.6 1.0 copy-start.18
  242.6 15.7 %collective-permute-start.3 = (bf16[256,768]{1,0:T(8,128)(2,1)}, bf16[256,768]{1,0:T(8,128)(2,1)}, u32[]{:S(2)}, u32[]{:S(2)}) collective-permute-start(bf16[256,768]{1,0:T(8,128)(2,1)} %fusion.13), channel_id=1, source_target_pairs={{0,32},{16,48},{32,64},{48,80},{64,96},{80,112},{96,0},{112,16},{1... | collective-permute-start | bytes 1179656 | tf_op jit(solution)/shard_map/ppermute | solution.py:356
  242.6 7.1 %copy-start.15 = (bf16[2,256,768]{2,1,0:T(8,128)(2,1)S(1)}, bf16[2,256,768]{2,1,0:T(8,128)(2,1)}, u32[]{:S(2)}) copy-start(bf16[2,256,768]{2,1,0:T(8,128)(2,1)} %copy-done.14) | copy-start | bytes 2359300
  242.6 7.1 %copy-start.17 = (bf16[2,256,768]{2,1,0:T(8,128)(2,1)S(1)}, bf16[2,256,768]{2,1,0:T(8,128)(2,1)}, u32[]{:S(2)}) copy-start(bf16[2,256,768]{2,1,0:T(8,128)(2,1)} %copy-done.16) | copy-start | bytes 2359300
  251.1 7.2 %copy-start.19 = (bf16[2,256,768]{2,1,0:T(8,128)(2,1)S(1)}, bf16[2,256,768]{2,1,0:T(8,128)(2,1)}, u32[]{:S(2)}) copy-start(bf16[2,256,768]{2,1,0:T(8,128)(2,1)} %copy-done.18) | copy-start | bytes 2359300

commit v2 on v1

v2 whole, which is shorter than its diff:
```python
import jax
import jax.numpy as jnp
from jax import lax
from jax.experimental import pallas as pl
from jax.experimental.pallas import tpu as pltpu
from jax.sharding import PartitionSpec as P

saturation = 2.0
weight_factor = 1.0 / 64.0
MIB = 1024 * 1024


def params(limit):
    return pltpu.CompilerParams(vmem_limit_bytes=limit * MIB)


def cost(flops, nbytes):
    return pl.CostEstimate(flops=int(flops), bytes_accessed=int(nbytes), transcendentals=0)


def dot_nn(a, b):
    return lax.dot_general(a, b, (((1,), (0,)), ((), ())), preferred_element_type=jnp.float32)


def dot_nt(a, b):
    return lax.dot_general(a, b, (((1,), (1,)), ((), ())), preferred_element_type=jnp.float32)


def dot_tn(a, b):
    return lax.dot_general(a, b, (((0,), (0,)), ((), ())), preferred_element_type=jnp.float32)


ANY = pl.BlockSpec(memory_space=pl.ANY)


LONG = 1000
MICROS = {'oD': 5, 'hg': 5, 'wD': 5, 'i0': 100, 'oG': 100, 'nD': 100, 'oU': 100, 'wG': 100, 'wU': 100, 'nG': 100, 'fD': 100, 'nU': 100, 'fG': 100, 'fU': 100}


def takes(micros):
    return cost(micros * 1.15e9, 1e6)


def in_hbm(value):
    return pltpu.with_memory_space_constraint(value, pltpu.HBM)


def ordered(body, n_read, n_after):
    if n_after == 0:
        return body
    return lambda *refs: body(*refs[:n_read], *refs[n_read + n_after :])


def in_vmem(value):
    return pltpu.with_memory_space_constraint(value, pltpu.VMEM)


def pack(tokens, grad, ids, codes, history, place):
    tok, width = tokens.shape
    experts = history.shape[1]
    cap = tok * 2 * 2 // experts
    slots = experts * cap
    step = 1024
    nx = width // step

    def body(ids_ref, codes_ref, hist_ref, x_ref, g_ref, out_ref, sel_ref, fac_ref):
        j = pl.program_id(0)

        @pl.when(j == 0)
        def _():
            rows = lax.broadcasted_iota(jnp.int32, (tok, tok), 0)
            cols = lax.broadcasted_iota(jnp.int32, (tok, tok), 1)
            earlier = (rows < cols).astype(jnp.bfloat16)
            expert = lax.broadcasted_iota(jnp.int32, (experts, tok), 0)
            largest = jnp.max(hist_ref[...], axis=0, keepdims=True).astype(jnp.float32)
            diagonal = lax.broadcasted_iota(
                jnp.int32, (experts, experts), 0
            ) == lax.broadcasted_iota(jnp.int32, (experts, experts), 1)
            wide = jnp.broadcast_to(largest, (experts, experts))
            magnitude = jnp.sum(jnp.where(diagonal, wide, 0.0), axis=1, keepdims=True)
            scale = jnp.zeros((experts, 1), jnp.float32)
            inverse = jnp.zeros((experts, 1), jnp.float32)
            for value in range(-2, 3):
                scale = jnp.where(magnitude == value, 2.0**-value, scale)
                inverse = jnp.where(magnitude == value, 2.0**value, inverse)
            id_rows = [ids_ref[k : k + 1, :] for k in range(2)]
            marks = [expert == row for row in id_rows]
            count = (marks[0] | marks[1]).astype(jnp.float32)
            before = dot_nn(count.astype(jnp.bfloat16), earlier)
            slot = lax.broadcasted_iota(jnp.int32, (slots, tok), 0)
            select = jnp.zeros((slots, tok), jnp.float32)
            factor = jnp.zeros((slots, tok), jnp.float32)
            unscale = jnp.zeros((slots, tok), jnp.float32)
            for k in range(2):
                place = jnp.sum(jnp.where(marks[k], before, 0.0), axis=0, keepdims=True)
                dest = id_rows[k] * cap + place.astype(jnp.int32)
                chosen = jnp.sum(jnp.where(marks[k], scale, 0.0), axis=0, keepdims=True)
                back = jnp.sum(jnp.where(marks[k], inverse, 0.0), axis=0, keepdims=True)
                weight = codes_ref[k : k + 1, :].astype(jnp.float32) / 64.0 * chosen
                hit = slot == dest
                select = jnp.where(hit, 1.0, select)
                factor = jnp.where(hit, weight, factor)
                unscale = jnp.where(hit, back, unscale)
            sel_ref[...] = select.astype(jnp.bfloat16)
            fac_ref[0] = jnp.sum(factor, axis=1, keepdims=True)
            fac_ref[1] = jnp.sum(unscale, axis=1, keepdims=True)

        @pl.when(j < nx)
        def _():
            out_ref[...] = dot_nn(sel_ref[...], x_ref[...]).astype(jnp.bfloat16)

        @pl.when(j >= nx)
        def _():
            picked = dot_nn(sel_ref[...], g_ref[...])
            clipped = jnp.clip(picked * fac_ref[0], -saturation, saturation)
            rounded = clipped.astype(jnp.bfloat16).astype(jnp.float32)
            out_ref[...] = (rounded * fac_ref[1]).astype(jnp.bfloat16)

    whole = lambda shape: pl.BlockSpec(shape, lambda j: (0,) * len(shape))
    return pl.pallas_call(
        ordered(body, 5, 1),
        grid=(2 * nx,),
        in_specs=[
            whole(ids.shape),
            whole(codes.shape),
            whole(history.shape),
            pl.BlockSpec((tok, step), lambda j: (0, jnp.minimum(j, nx - 1))),
            pl.BlockSpec((tok, step), lambda j: (0, jnp.maximum(j - nx, 0))),
            ANY,
        ],
        out_specs=[pl.BlockSpec((slots, step), lambda j: (0, j)), whole((slots, tok))],
        out_shape=[
            pltpu.HBM((slots, 2 * width), jnp.bfloat16),
            jax.ShapeDtypeStruct((slots, tok), jnp.bfloat16),
        ],
        scratch_shapes=[pltpu.VMEM((2, slots, 1), jnp.float32)],
        compiler_params=params(14),
        cost_estimate=takes(10),
        name="pack",
    )(in_hbm(ids), in_hbm(codes), in_hbm(history), in_hbm(tokens), in_hbm(grad), place)


def forward(first, w_gate, w_up):
    rows = first.shape[0]
    width, units = w_gate.shape[1:]
    block = 256

    def body(x_ref, wg_ref, wu_ref, hidden_ref, for_gate_ref, for_up_ref):
        gate = dot_nn(x_ref[...], wg_ref[...])
        up = dot_nn(x_ref[...], wu_ref[...])
        sig = jax.nn.sigmoid(gate)
        act = gate * sig
        hidden_ref[...] = (act * up).astype(jnp.bfloat16)
        for_gate_ref[...] = up * sig * (1.0 + gate * (1.0 - sig))
        for_up_ref[...] = act

    out = pl.BlockSpec((rows, block), lambda j: (0, j))
    weight = pl.BlockSpec((None, width, block), lambda j: (0, 0, j))
    return pl.pallas_call(
        body,
        grid=(units // block,),
        in_specs=[pl.BlockSpec((rows, width), lambda j: (0, 0)), weight, weight],
        out_specs=[out, out, out],
        out_shape=[
            jax.ShapeDtypeStruct((rows, units), jnp.bfloat16),
            jax.ShapeDtypeStruct((rows, units), jnp.float32),
            jax.ShapeDtypeStruct((rows, units), jnp.float32),
        ],
        compiler_params=params(24),
        cost_estimate=takes(10),
        name="forward",
    )(in_hbm(first), in_vmem(w_gate), in_vmem(w_up))


def hidden_grad(buf, offset, w_down, for_gate, for_up, after=(), micros=LONG):
    rows = buf.shape[0]
    units, width = w_down.shape[1:]
    block = 256

    def body(q_ref, wd_ref, for_gate_ref, for_up_ref, d_gate_ref, d_up_ref):
        total = dot_nt(q_ref[...], wd_ref[...])
        d_gate_ref[...] = (total * for_gate_ref[...]).astype(jnp.bfloat16)
        d_up_ref[...] = (total * for_up_ref[...]).astype(jnp.bfloat16)

    tile = pl.BlockSpec((rows, block), lambda j: (0, j))
    return pl.pallas_call(
        ordered(body, 4, len(after)),
        grid=(units // block,),
        in_specs=[
            pl.BlockSpec((rows, width), lambda j: (0, offset)),
            pl.BlockSpec((None, block, width), lambda j: (0, j, 0)),
            tile,
            tile,
        ]
        + [ANY] * len(after),
        out_specs=[tile] * 2,
        out_shape=[jax.ShapeDtypeStruct((rows, units), jnp.bfloat16)] * 2,
        compiler_params=params(20),
        cost_estimate=takes(micros),
        name="hidden_grad",
    )(in_hbm(buf), in_vmem(w_down), for_gate, for_up, *after)


def weight_part(kind, buf, base, width, other, place, own, received=None, after=(), micros=LONG):
    rows = buf.shape[0]
    units = other.shape[1]
    shape = (width, units) if kind == "rows" else (units, width)
    half = shape[0] // 2

    def product(buf_ref, other_ref):
        if kind == "rows":
            return dot_tn(buf_ref[...], other_ref[...])
        return dot_tn(other_ref[...], buf_ref[...])

    def plain(place_ref, buf_ref, other_ref, out_ref):
        out_ref[...] = product(buf_ref, other_ref).astype(jnp.bfloat16)

    def summed(place_ref, buf_ref, other_ref, in_ref, fwd_ref, bwd_ref, keep1_ref, keep3_ref, own_ref):
        j = pl.program_id(0)
        total = product(buf_ref, other_ref) + in_ref[...].astype(jnp.float32)
        total = total.astype(jnp.bfloat16)
        low, high = total[:half], total[half:]

        @pl.when(j == 0)
        def _():
            fwd_ref[0] = low
            bwd_ref[0] = high

        @pl.when(j == 1)
        def _():
            keep1_ref[...] = low
            fwd_ref[1] = high

        @pl.when(j == 2)
        def _():
            own_ref[...] = total

        @pl.when(j == 3)
        def _():
            bwd_ref[1] = low
            keep3_ref[...] = high

    def column(j, at):
        z, core = at[0] // 2, at[0] % 2
        wanted = core if own else 1 - core
        return (0, base + (z + 6 - j) % 4 * 2 + wanted)

    ins = [
        pl.BlockSpec((rows, width), column),
        pl.BlockSpec((rows, units), lambda j, at: (0, 0)),
    ]
    flat = jnp.bfloat16
    if received is None:
        outs = pl.BlockSpec((None,) + shape, lambda j, at: (j, 0, 0))
        out_shape = jax.ShapeDtypeStruct((4,) + shape, flat)
        args = (in_hbm(buf), other)
    else:
        ins.append(pl.BlockSpec((None,) + shape, lambda j, at: (j, 0, 0)))
        shapes = [(2, half, shape[1])] * 2 + [(half, shape[1])] * 2 + [shape]
        outs = [pl.BlockSpec(s, lambda j, at, n=len(s): (0,) * n) for s in shapes]
        out_shape = [jax.ShapeDtypeStruct(s, flat) for s in shapes]
        args = (in_hbm(buf), other, received)
    ins += [ANY] * len(after)
    body = plain if received is None else summed
    return pl.pallas_call(
        ordered(body, 1 + len(args), len(after)),
        grid_spec=pltpu.PrefetchScalarGridSpec(
            num_scalar_prefetch=1, grid=(4,), in_specs=ins, out_specs=outs
        ),
        out_shape=out_shape,
        compiler_params=params(18),
        cost_estimate=takes(micros),
        name="weight_part",
    )(place, *args, *after)


def input_rows(d_gate, d_up, w_gate, w_up, after=(), micros=LONG):
    rows, units = d_gate.shape
    width = w_gate.shape[1]
    block = 512

    def body(dg_ref, du_ref, wg_ref, wu_ref, out_ref):
        total = dot_nt(dg_ref[...], wg_ref[...]) + dot_nt(du_ref[...], wu_ref[...])
        out_ref[...] = total.astype(jnp.bfloat16)

    whole = pl.BlockSpec((rows, units), lambda j: (0, 0))
    weight = pl.BlockSpec((None, block, units), lambda j: (0, j, 0))
    return pl.pallas_call(
        ordered(body, 4, len(after)),
        grid=(width // block,),
        in_specs=[whole, whole, weight, weight] + [ANY] * len(after),
        out_specs=pl.BlockSpec((rows, block), lambda j: (0, j)),
        out_shape=pltpu.HBM((rows, width), jnp.bfloat16),
        compiler_params=params(16),
        cost_estimate=takes(micros),
        name="input_rows",
    )(d_gate, d_up, in_vmem(w_gate), in_vmem(w_up), *after)


def passed_on(parts, hop, after=(), micros=LONG):
    half, width = parts[2].shape

    def body(up_ref, down_ref, low_ref, high_ref, fwd_ref, bwd_ref):
        fwd = up_ref[...].astype(jnp.float32) + low_ref[...].astype(jnp.float32)
        bwd = down_ref[...].astype(jnp.float32) + high_ref[...].astype(jnp.float32)
        fwd_ref[...] = fwd.astype(jnp.bfloat16)
        bwd_ref[...] = bwd.astype(jnp.bfloat16)

    block = half // 2
    flat = pl.BlockSpec((block, width), lambda j: (j, 0))
    first = pl.BlockSpec((None, block, width), lambda j: (0, j, 0))
    return pl.pallas_call(
        ordered(body, 4, len(after)),
        grid=(2,),
        in_specs=[flat, flat, first, first] + [ANY] * len(after),
        out_specs=[flat, flat],
        out_shape=[jax.ShapeDtypeStruct((half, width), jnp.bfloat16)] * 2,
        compiler_params=params(8),
        cost_estimate=takes(micros),
        name="passed_on",
    )(parts[2], parts[3], *hop, *after)


def finished(parts, hop, last, after=(), micros=LONG):
    half, width = parts[2].shape

    def body(own_ref, ahead_ref, behind_ref, low_ref, high_ref, out_ref):
        own = own_ref[...].astype(jnp.float32)

        def store(near_ref, far_ref):
            total = own + near_ref[...].astype(jnp.float32) + far_ref[...].astype(jnp.float32)
            out_ref[...] = (total * weight_factor).astype(jnp.bfloat16)

        @pl.when(pl.program_id(0) == 0)
        def _():
            store(ahead_ref, low_ref)

        @pl.when(pl.program_id(0) == 1)
        def _():
            store(behind_ref, high_ref)

    tile = pl.BlockSpec((half, width), lambda j: (j, 0))
    second = pl.BlockSpec((None, half, width), lambda j: (1, 0, 0))
    whole = pl.BlockSpec((half, width), lambda j: (0, 0))
    return pl.pallas_call(
        ordered(body, 5, len(after)),
        grid=(2,),
        in_specs=[tile, second, second, whole, whole] + [ANY] * len(after),
        out_specs=tile,
        out_shape=jax.ShapeDtypeStruct((2 * half, width), jnp.bfloat16),
        compiler_params=params(10),
        cost_estimate=takes(micros),
        name="finished",
    )(parts[4], hop[1], hop[0], *last, *after)


def combine(select, returned, after=()):
    slots, tok = select.shape
    width = returned.shape[1]
    block = 1024

    def body(sel_ref, in_ref, out_ref):
        out_ref[...] = dot_tn(sel_ref[...], in_ref[...]).astype(jnp.bfloat16)

    return pl.pallas_call(
        ordered(body, 2, len(after)),
        grid=(width // block,),
        in_specs=[
            pl.BlockSpec((slots, tok), lambda j: (0, 0)),
            pl.BlockSpec((slots, block), lambda j: (0, j)),
        ]
        + [ANY] * len(after),
        out_specs=pl.BlockSpec((tok, block), lambda j: (0, j)),
        out_shape=jax.ShapeDtypeStruct((tok, width), jnp.bfloat16),
        compiler_params=params(12),
        cost_estimate=takes(5),
        name="combine",
    )(select, in_hbm(returned), *after)


def shards(tokens_in, out_grad, expert_ids, router_codes, amax_history, w_gate, w_up, w_down):
    n_dp = lax.axis_size("dp")
    peers = lax.axis_size("expert")
    width = tokens_in.shape[1]
    experts = amax_history.shape[0]
    part = width // n_dp
    place = lax.axis_index("dp").astype(jnp.int32).reshape(1)

    swap = [(i, i ^ 1) for i in range(n_dp)]
    ahead = [(i, (i + 2) % n_dp) for i in range(n_dp)]
    behind = [(i, (i - 2) % n_dp) for i in range(n_dp)]

    def exchange(buf):
        blocks = buf.reshape(peers, -1, buf.shape[1])
        out = lax.all_to_all(blocks, "expert", split_axis=0, concat_axis=0, tiled=True)
        return out.reshape(buf.shape)

    def corner(value):
        return value[:16, :128] * 2

    def swapped(value):
        return lax.ppermute(value, "dp", swap)

    def one_hop(fwd, bwd):
        return lax.ppermute(fwd, "dp", ahead), lax.ppermute(bwd, "dp", behind)

    sent, select = pack(
        tokens_in, out_grad, expert_ids.T, router_codes.T, amax_history.T, place
    )
    rows = exchange(sent)
    hidden, for_gate, for_up = forward(rows, w_gate, w_up)
    down = ("columns", rows, width // part, part, hidden)
    other_down = weight_part(*down, place, False, micros=MICROS['oD'])
    d_gate, d_up = hidden_grad(rows, 1, w_down, for_gate, for_up, after=(other_down,), micros=MICROS['hg'])
    own_down = weight_part(*down, place, True, swapped(other_down), after=(d_gate,), micros=MICROS['wD'])
    hop_down = one_hop(*own_down[:2])
    rows_back = input_rows(
        d_gate, d_up, w_gate, w_up, after=(own_down[0], own_down[1]), micros=MICROS["i0"]
    )
    back = exchange(rows_back)
    gate = ("rows", rows, 0, part, d_gate)
    other_gate = weight_part(
        *gate, place, False, after=(corner(rows_back),), micros=MICROS["oG"]
    )
    next_down = passed_on(own_down, hop_down, after=(other_gate,), micros=MICROS["nD"])
    last_down = one_hop(*next_down)
    up = ("rows", rows, 0, part, d_up)
    other_up = weight_part(*up, place, False, after=next_down, micros=MICROS["oU"])
    own_gate = weight_part(
        *gate, place, True, swapped(other_gate), after=(other_up,), micros=MICROS["wG"]
    )
    hop_gate = one_hop(*own_gate[:2])
    own_up = weight_part(
        *up, place, True, swapped(other_up), after=own_gate[:2], micros=MICROS["wU"]
    )
    hop_up = one_hop(*own_up[:2])
    next_gate = passed_on(own_gate, hop_gate, after=own_up[:2], micros=MICROS["nG"])
    last_gate = one_hop(*next_gate)
    grad_down = finished(own_down, hop_down, last_down, after=next_gate, micros=MICROS["fD"])
    next_up = passed_on(own_up, hop_up, after=(grad_down,), micros=MICROS["nU"])
    last_up = one_hop(*next_up)
    grad_tokens = combine(select, back, after=next_up)
    grad_gate = finished(own_gate, hop_gate, last_gate, after=(grad_tokens,), micros=MICROS["fG"])
    grad_up = finished(own_up, hop_up, last_up, after=(grad_gate,), micros=MICROS["fU"])
    return (grad_tokens, grad_gate[None], grad_up[None], grad_down[None])


def solution(mesh):
    return jax.shard_map(
        shards,
        mesh=mesh,
        in_specs=(
            P(("dp", "expert"), None),
            P(("dp", "expert"), None),
            P(("dp", "expert"), None),
            P(("dp", "expert"), None),
            P(),
            P("expert", None, None),
            P("expert", None, None),
            P("expert", None, None),
        ),
        out_specs=(
            P(("dp", "expert"), None),
            P("expert", "dp", None),
            P("expert", "dp", None),
            P("expert", None, "dp"),
        ),
        check_vma=False,
    )
```

time: 265 us -> 240 us (0.906); the launches traced: 261 us -> 239 us
  blocking collectives: 79.5 us -> 103 us
  local copies, waits for them, and re-layouts: 26 us -> 3.64 us
  waiting for transfers between devices: 39.9 us -> 24.7 us
  Pallas kernels: 71.4 us -> 80.3 us
  starting transfers between devices: 34.3 us -> 25.8 us
  other arithmetic: 8.49 us -> 0.68 us
    all_to_all x1, blocking collectives: 79.5 us -> 103 us  [exchange(): lax.all_to_all(blocks, 'expert', split_axis=0, concat_axis=0, tiled=True)]
    unnamed x61 -> x30, local copies, waits for them, and re-layouts: 26 us -> 3.64 us
    ppermute x20 -> x15, waiting for transfers between devices: 35.7 us -> 24.7 us  [the longest x12 24.7 us: one_hop(): return (lax.ppermute(fwd, 'dp', ahead), lax.ppermute(bwd, 'dp', behind))]
    pallas_call x13 -> x16, Pallas kernels: 61.7 us -> 69.9 us  [the longest x6 29.5 us: weight_part(): pl.pallas_call(ordered(body, 1 + len(args), len(after)), grid_spec=pltpu....]
    all_to_all x2 -> x1, starting transfers between devices: 9.3 us -> 4.56 us  [exchange(): lax.all_to_all(blocks, 'expert', split_axis=0, concat_axis=0, tiled=True)]
    convert_element_type x11 -> x0, other arithmetic: 4.51 us -> none  [the longest x3 2.16 us: reduced(): return (total * weight_factor).astype(jnp.bfloat16)]
    all_to_all x2 -> x1, waiting for transfers between devices: 4.17 us -> 0.01 us  [exchange(): lax.all_to_all(blocks, 'expert', split_axis=0, concat_axis=0, tiled=True)]
    ppermute x20 -> x15, starting transfers between devices: 25 us -> 21.3 us  [the longest x12 17.5 us: one_hop(): return (lax.ppermute(fwd, 'dp', ahead), lax.ppermute(bwd, 'dp', behind))]
  transfers between devices with their start and end apart: 22 -> 16, of which waited for: 10 -> 4; matrix products, arithmetic and copies ran while one was open for 2% -> 0% of each run, Pallas kernels for 22% -> 21%
where the time goes in v2:
time: 240 us; the launch traced here: 239 us
  blocking collectives  103 us (43%)
  Pallas kernels  80.3 us (33%)
  starting transfers between devices  25.8 us (11%)
  waiting for transfers between devices  24.7 us (10%)
  local copies, waits for them, and re-layouts  3.64 us (2%)
    all_to_all x1, blocking collectives, exchange(): lax.all_to_all(blocks, 'expert', split_axis=0, concat_axis=0, tiled=True)  103 us
    pallas_call x6, Pallas kernels, weight_part(): pl.pallas_call(ordered(body, 1 + len(args), len(after)), grid_spec=pltpu....  29.5 us
    ppermute x12, waiting for transfers between devices, one_hop(): return (lax.ppermute(fwd, 'dp', ahead), lax.ppermute(bwd, 'dp', behind))  24.7 us
    ppermute x12, starting transfers between devices, one_hop(): return (lax.ppermute(fwd, 'dp', ahead), lax.ppermute(bwd, 'dp', behind))  17.5 us
    pallas_call x1, Pallas kernels, forward(): pl.pallas_call(body, grid=(units // block,), in_specs=[pl.BlockSpec((rows...  10.4 us
    pallas_call x1, Pallas kernels, input_rows(): pl.pallas_call(ordered(body, 4, len(after)), grid=(width // block,), in_s...  8.98 us
    pallas_call x1, Pallas kernels, pack(): pl.pallas_call(ordered(body, 5, 1), grid=(2 * nx,), in_specs=[whole(ids.s...  8.83 us
    pallas_call x3, Pallas kernels, finished(): pl.pallas_call(ordered(body, 5, len(after)), grid=(2,), in_specs=[tile, s...  7.04 us
  transfers between devices with their start and end apart: 16, of which 4 were waited for; matrix products, arithmetic and copies ran while one was open for 0% of the time, Pallas kernels for 21%

profile of v2, /device:TPU:1, one launch (start us, length us, event | category | flops | bytes accessed | tf_op | source)
XLA Modules:
  0.0 238.6 jit_solution(12242762367101516741)
XLA Ops:
  0.6 8.8 %pack.1 = (bf16[512,8192]{1,0:T(8,128)(2,1)}, bf16[512,128]{1,0:T(8,128)(2,1)S(1)}) custom-call(s32[2,128]{1,0:T(2,128)} %bitcast.26, s32[2,128]{1,0:T(2,128)} %bitcast.27, s32[4,16]{1,0:T(4,128)} %bitcast.25, bf16[128,4096]{1,0:T(8,128)(2,1)} %refs_3_.2, bf16[128,4096]{1,0:T(8,128)(2,1)} %refs_4_.1, s32[1]{0:T(128)} %bitcast.3.refs_5_.place_ref.refs_0_), custom_call_target="tpu_custom_call" | custom-call | flops 11500000256 | bytes 1000000 | tf_op jit(solution)/shard_map/pack/pallas_call | solution.py:120
  9.5 102.7 %all_to_all.10 = bf16[16,32,8192]{2,1,0:T(8,128)(2,1)} all-to-all(bf16[16,32,8192]{2,1,0:T(8,128)(2,1)} %bitcast.23), channel_id=1, replica_groups=mesh['dp'=8,'expert'=16] {'expert'}, dimensions={0} | all-to-all | bytes 16777216 | tf_op jit(solution)/shard_map/all_to_all | solution.py:395
  112.2 0.0 copy-done
  112.2 0.0 copy-done.1
  112.2 10.4 %forward.1 = (bf16[512,768]{1,0:T(8,128)(2,1)S(1)}, f32[512,768]{1,0:T(8,128)S(1)}, f32[512,768]{1,0:T(8,128)S(1)}) custom-call(bf16[512,8192]{1,0:T(8,128)(2,1)} %bitcast.15, bf16[1,4096,768]{2,1,0:T(8,128)(2,1)S(1)} %copy-done, bf16[1,4096,768]{2,1,0:T(8,128)(2,1)S(1)} %copy-done.1), custom_call_target="tpu_custom_call" | custom-call | flops 11500000256 | bytes 1000000 | tf_op jit(solution)/shard_map/forward/pallas_call | solution.py:159
  122.5 4.0 %weight_part.6.refs_4_ = bf16[4,768,512]{2,1,0:T(8,128)(2,1)S(1)} custom-call(s32[1]{0:T(128)} %bitcast.3.refs_5_.place_ref.refs_0_, bf16[512,8192]{1,0:T(8,128)(2,1)} %bitcast.16, bf16[512,768]{1,0:T(8,128)(2,1)S(1)} %get-tuple-element.36.other_ref.refs_2_), custom_call_target="tpu_custom_call" | custom-call | flops 5750000128 | bytes 1000000 | tf_op jit(solution)/shard_map/weight_part/pallas_call | solution.py:265
  126.6 2.7 %collective-permute-start = (bf16[4,768,512]{2,1,0:T(8,128)(2,1)S(1)}, bf16[4,768,512]{2,1,0:T(8,128)(2,1)S(1)}, u32[]{:S(2)}, u32[]{:S(2)}) collective-permute-start(bf16[4,768,512]{2,1,0:T(8,128)(2,1)S(1)} %weight_part.6.refs_4_), channel_id=1, source_target_pairs={{0,16},{16,0},{32,48},{48,32},{64,80},{80,64},{96,112},{112,96},{1... | collective-permute-start | bytes 9437192 | tf_op jit(solution)/shard_map/ppermute | solution.py:402
  129.2 6.3 %hidden_grad.1 = (bf16[512,768]{1,0:T(8,128)(2,1)S(1)}, bf16[512,768]{1,0:T(8,128)(2,1)S(1)}) custom-call(bf16[512,8192]{1,0:T(8,128)(2,1)} %bitcast.17, bf16[1,768,4096]{2,1,0:T(8,128)(2,1)S(1)} %bitcast.12, f32[512,768]{1,0:T(8,128)S(1)} %get-tuple-element.34.refs_2_, f32[512,768]{1,0:T(8,128)S(1)} %get-tuple-element.35.refs_3_, ...), custom_call_target="tpu_custom_call" | custom-call | flops 5750000128 | bytes 1000000 | tf_op jit(solution)/shard_map/hidden_grad/pallas_call | solution.py:186
  135.6 0.0 copy-start.9
  135.6 0.0 copy-start.11
  135.6 0.0 collective-permute-done.refs_3_
  135.6 5.8 %weight_part.7 = (bf16[2,384,512]{2,1,0:T(8,128)(2,1)}, bf16[2,384,512]{2,1,0:T(8,128)(2,1)}, bf16[384,512]{1,0:T(8,128)(2,1)S(1)}, bf16[384,512]{1,0:T(8,128)(2,1)S(1)}, bf16[768,512]{1,0:T(8,128)(2,1)S(1)}) custom-call(s32[1]{0:T(128)} %bitcast.3.refs_5_.place_ref.refs_0_, bf16[512,8192]{1,0:T(8,128)(2,1)} %bitcast.18, ...), custom_call_target="tpu_custom_call" | custom-call | flops 5750000128 | bytes 1000000 | tf_op jit(solution)/shard_map/weight_part/pallas_call | solution.py:265
  141.4 1.6 collective-permute-start.1
  143.1 2.1 collective-permute-start.2
  145.2 0.0 copy-done.9
  145.2 9.0 %input_rows.1 = bf16[512,4096]{1,0:T(8,128)(2,1)} custom-call(bf16[512,768]{1,0:T(8,128)(2,1)S(1)} %get-tuple-element.37.refs_4_.refs_0_.refs_2_, bf16[512,768]{1,0:T(8,128)(2,1)S(1)} %get-tuple-element.38.refs_1_.refs_2_, bf16[1,4096,768]{2,1,0:T(8,128)(2,1)S(1)} %copy-done, bf16[1,4096,768]{2,1,0:T(8,128)(2,1)S(1)} %copy-done.1, ...), custom_call_target="tpu_custom_call" | custom-call | flops 115000000512 | bytes 1000000 | tf_op jit(solution)/shard_map/input_rows/pallas_call | solution.py:288
  154.2 0.7 slice_multiply_fusion.refs_3_
  154.8 0.0 copy-done.11
  154.8 5.2 %weight_part.8.refs_4_ = bf16[4,512,768]{2,1,0:T(8,128)(2,1)} custom-call(s32[1]{0:T(128)} %bitcast.3.refs_5_.place_ref.refs_0_, bf16[512,8192]{1,0:T(8,128)(2,1)} %bitcast.19, bf16[512,768]{1,0:T(8,128)(2,1)S(1)} %get-tuple-element.37.refs_4_.refs_0_.refs_2_, bf16[16,128]{1,0:T(8,128)(2,1)S(1)} %slice_multiply_fusion.refs_3_), custom_call_target="tpu_custom_call" | custom-call | flops 115000000512 | bytes 1000000 | tf_op jit(solution)/shard_map/weight_part/pallas_call | solution.py:265
  160.0 0.3 collective-permute-start.4
  160.4 4.6 %all-to-all-start.1 = ((bf16[16,32,4096]{2,1,0:T(8,128)(2,1)}), bf16[16,32,4096]{2,1,0:T(8,128)(2,1)}, u32[]{:S(2)}, u32[]{:S(2)}) async-start(bf16[16,32,4096]{2,1,0:T(8,128)(2,1)} %bitcast.24), calls=%async_computation.1 | async-start | bytes 8388608 | tf_op jit(solution)/shard_map/all_to_all | solution.py:395
  164.9 0.0 collective-permute-done.1.refs_2_
  164.9 0.0 collective-permute-done.2.refs_3_.refs_1_
  165.0 0.0 copy-start.10
  165.0 2.1 passed_on.3
  167.0 0.0 collective-permute-start.7
  167.0 0.0 copy-start.12
  167.1 4.1 %weight_part.9.refs_4_ = bf16[4,512,768]{2,1,0:T(8,128)(2,1)S(1)} custom-call(s32[1]{0:T(128)} %bitcast.3.refs_5_.place_ref.refs_0_, bf16[512,8192]{1,0:T(8,128)(2,1)} %bitcast.20, bf16[512,768]{1,0:T(8,128)(2,1)S(1)} %copy-done.10, bf16[384,512]{1,0:T(8,128)(2,1)} %get-tuple-element.43.refs_3_, bf16[384,512]{1,0:T(8,128)(2,1)} %get-tuple-element.44.refs_4_), custom_call_target="tpu_custom_call" | custom-call | flops 115000000512 | bytes 1000000 | tf_op jit(solution)/shard_map/weight_part/pallas_call | solution.py:265
  171.2 2.7 %collective-permute-start.8 = (bf16[384,512]{1,0:T(8,128)(2,1)}, bf16[384,512]{1,0:T(8,128)(2,1)}, u32[]{:S(2)}, u32[]{:S(2)}) collective-permute-start(bf16[384,512]{1,0:T(8,128)(2,1)} %get-tuple-element.44.refs_4_), channel_id=1, source_target_pairs={{0,96},{16,112},{32,0},{48,16},{64,32},{80,48},{96,64},{112,80},{1... | collective-permute-start | bytes 1179656 | tf_op jit(solution)/shard_map/ppermute | solution.py:405
  173.9 0.8 collective-permute-start.3
  174.7 0.0 collective-permute-done.4.refs_3_
  174.7 4.9 %weight_part.10 = (bf16[2,256,768]{2,1,0:T(8,128)(2,1)S(1)}, bf16[2,256,768]{2,1,0:T(8,128)(2,1)S(1)}, bf16[256,768]{1,0:T(8,128)(2,1)S(1)}, bf16[256,768]{1,0:T(8,128)(2,1)S(1)}, bf16[512,768]{1,0:T(8,128)(2,1)S(1)}) custom-call(s32[1]{0:T(128)} %bitcast.3.refs_5_.place_ref.refs_0_, bf16[512,8192]{1,0:T(8,128)(2,1)} %bitcast.21, ...), custom_call_target="tpu_custom_call" | custom-call | flops 115000000512 | bytes 1000000 | tf_op jit(solution)/shard_map/weight_part/pallas_call | solution.py:265
  179.6 0.4 collective-permute-start.10
  180.0 1.1 collective-permute-start.9
  181.1 0.0 collective-permute-done.3.refs_3_
  181.2 5.4 %weight_part.11 = (bf16[2,256,768]{2,1,0:T(8,128)(2,1)}, bf16[2,256,768]{2,1,0:T(8,128)(2,1)}, bf16[256,768]{1,0:T(8,128)(2,1)S(1)}, bf16[256,768]{1,0:T(8,128)(2,1)S(1)}, bf16[512,768]{1,0:T(8,128)(2,1)S(1)}) custom-call(s32[1]{0:T(128)} %bitcast.3.refs_5_.place_ref.refs_0_, bf16[512,8192]{1,0:T(8,128)(2,1)} %bitcast.22, bf16[512,768]{1,0:T(8,128)(2,1)S(1)} %copy-done.10, ...), custom_call_target="tpu_custom_call" | custom-call | flops 115000000512 | bytes 1000000 | tf_op jit(solution)/shard_map/weight_part/pallas_call | solution.py:265
  186.6 0.0 collective-permute-start.5
  186.6 12.7 %collective-permute-done.10.refs_3_.refs_1_ = bf16[2,256,768]{2,1,0:T(8,128)(2,1)S(1)} collective-permute-done((bf16[2,256,768]{2,1,0:T(8,128)(2,1)S(1)}, bf16[2,256,768]{2,1,0:T(8,128)(2,1)S(1)}, u32[]{:S(2)}, u32[]{:S(2)}) %collective-permute-start.10) | collective-permute-done | bytes 786464 | tf_op jit(solution)/shard_map/ppermute | solution.py:405
  199.3 3.3 %collective-permute-start.6 = (bf16[2,256,768]{2,1,0:T(8,128)(2,1)}, bf16[2,256,768]{2,1,0:T(8,128)(2,1)}, u32[]{:S(2)}, u32[]{:S(2)}) collective-permute-start(bf16[2,256,768]{2,1,0:T(8,128)(2,1)} %get-tuple-element.50.refs_5_), channel_id=1, source_target_pairs={{0,96},{16,112},{32,0},{48,16},{64,32},{80,48},{96,64},{112,80},{1... | collective-permute-start | bytes 2359304 | tf_op jit(solution)/shard_map/ppermute | solution.py:405
  202.5 0.0 collective-permute-done.9.refs_2_
  202.5 1.1 passed_on.4
  203.6 0.1 copy-done.4
  203.7 0.0 collective-permute-start.11
  203.7 0.0 collective-permute-done.7.refs_3_
  203.7 2.7 %collective-permute-start.12 = (bf16[256,768]{1,0:T(8,128)(2,1)}, bf16[256,768]{1,0:T(8,128)(2,1)}, u32[]{:S(2)}, u32[]{:S(2)}) collective-permute-start(bf16[256,768]{1,0:T(8,128)(2,1)} %get-tuple-element.55.refs_6_), channel_id=1, source_target_pairs={{0,96},{16,112},{32,0},{48,16},{64,32},{80,48},{96,64},{112,80},{1... | collective-permute-start | bytes 1179656 | tf_op jit(solution)/shard_map/ppermute | solution.py:405
  206.4 0.0 collective-permute-done.8.refs_4_
  206.4 2.5 %finished.3.refs_4_ = bf16[768,512]{1,0:T(8,128)(2,1)} custom-call(bf16[768,512]{1,0:T(8,128)(2,1)S(1)} %get-tuple-element.51.refs_0_, bf16[2,384,512]{2,1,0:T(8,128)(2,1)} %collective-permute-done.2.refs_3_.refs_1_, bf16[2,384,512]{2,1,0:T(8,128)(2,1)} %collective-permute-done.1.refs_2_, bf16[384,512]{1,0:T(8,128)(2,1)} %collective-permute-done.7.refs_3_, ...), custom_call_target="tpu_custom_call" | custom-call | flops 115000000512 | bytes 1000000 | tf_op jit(solution)/shard_map/finished/pallas_call | solution.py:345
  208.9 8.1 %collective-permute-done.5.refs_2_ = bf16[2,256,768]{2,1,0:T(8,128)(2,1)} collective-permute-done((bf16[2,256,768]{2,1,0:T(8,128)(2,1)}, bf16[2,256,768]{2,1,0:T(8,128)(2,1)}, u32[]{:S(2)}, u32[]{:S(2)}) %collective-permute-start.5) | collective-permute-done | bytes 786464 | tf_op jit(solution)/shard_map/ppermute | solution.py:405
  217.0 1.4 collective-permute-done.6.refs_3_.refs_1_
  218.5 1.1 copy-done.7
  219.6 1.3 passed_on.5
  220.9 0.1 collective-permute-start.13
  221.0 3.5 %collective-permute-start.14 = (bf16[256,768]{1,0:T(8,128)(2,1)S(1)}, bf16[256,768]{1,0:T(8,128)(2,1)S(1)}, u32[]{:S(2)}, u32[]{:S(2)}) collective-permute-start(bf16[256,768]{1,0:T(8,128)(2,1)S(1)} %get-tuple-element.57.refs_3_), channel_id=1, source_target_pairs={{0,96},{16,112},{32,0},{48,16},{64,32},{80,48},{96,64},{112,80},{1... | collective-permute-start | bytes 1179656 | tf_op jit(solution)/shard_map/ppermute | solution.py:405
  224.5 0.0 all-to-all-done.1
  224.5 4.7 %combine.1.refs_5_ = bf16[128,4096]{1,0:T(8,128)(2,1)} custom-call(bf16[512,128]{1,0:T(8,128)(2,1)S(1)} %get-tuple-element.32.refs_0_, bf16[512,4096]{1,0:T(8,128)(2,1)} %bitcast.7.refs_1_, bf16[256,768]{1,0:T(8,128)(2,1)S(1)} %get-tuple-element.56.refs_2_, bf16[256,768]{1,0:T(8,128)(2,1)S(1)} %get-tuple-element.57.refs_3_), custom_call_target="tpu_custom_call" | custom-call | flops 5750000128 | bytes 1000000 | tf_op jit(solution)/shard_map/combine/pallas_call | solution.py:365
  229.2 0.0 collective-permute-done.11.refs_3_
  229.2 0.0 collective-permute-done.12.refs_4_
  229.2 0.0 copy-start.6
  229.3 1.2 copy-done.6
  230.5 2.3 finished.4.refs_5_
  232.7 0.0 collective-permute-done.13.refs_3_
  232.7 2.5 %collective-permute-done.14.refs_4_ = bf16[256,768]{1,0:T(8,128)(2,1)S(1)} collective-permute-done((bf16[256,768]{1,0:T(8,128)(2,1)S(1)}, bf16[256,768]{1,0:T(8,128)(2,1)S(1)}, u32[]{:S(2)}, u32[]{:S(2)}) %collective-permute-start.14) | collective-permute-done | bytes 393248 | tf_op jit(solution)/shard_map/ppermute | solution.py:405
  235.2 1.1 copy-done.8
  236.3 2.3 finished.5
  (18 shorter events, 0.0 us)
Async XLA Ops:
  9.5 102.7 %copy-start = (bf16[1,4096,768]{2,1,0:T(8,128)(2,1)S(1)}, bf16[1,4096,768]{2,1,0:T(8,128)(2,1)}, u32[]{:S(2)}) copy-start(bf16[1,4096,768]{2,1,0:T(8,128)(2,1)} %refs_2_.1) | copy-start | bytes 18874372
  9.5 102.7 %copy-start.1 = (bf16[1,4096,768]{2,1,0:T(8,128)(2,1)S(1)}, bf16[1,4096,768]{2,1,0:T(8,128)(2,1)}, u32[]{:S(2)}) copy-start(bf16[1,4096,768]{2,1,0:T(8,128)(2,1)} %refs_3_.3) | copy-start | bytes 18874372
  9.5 119.8 %slice-start = ((s8[6291456]{0:T(1024)(128)(4,1)}), s8[4194304]{0:T(1024)(128)(4,1)S(1)}, s32[]{:S(2)}) async-start(s8[6291456]{0:T(1024)(128)(4,1)} %bitcast.11), calls=%async_computation.2 | async-start | bytes 8388608
  112.2 17.1 %slice-start.1 = ((s8[6291456]{0:T(1024)(128)(4,1)}), s8[2097152]{0:T(1024)(128)(4,1)S(1)}, s32[]{:S(2)}) async-start(s8[6291456]{0:T(1024)(128)(4,1)} %bitcast.11), calls=%async_computation.3 | async-start | bytes 4194304
  126.6 9.0 %collective-permute-start = (bf16[4,768,512]{2,1,0:T(8,128)(2,1)S(1)}, bf16[4,768,512]{2,1,0:T(8,128)(2,1)S(1)}, u32[]{:S(2)}, u32[]{:S(2)}) collective-permute-start(bf16[4,768,512]{2,1,0:T(8,128)(2,1)S(1)} %weight_part.6.refs_4_), channel_id=1, source_target_pairs={{0,16},{16,0},{32,48},{48,32},{64,80},{80,64},{96,112},{112,96},{1... | collective-permute-start | bytes 9437192 | tf_op jit(solution)/shard_map/ppermute | solution.py:402
  135.6 9.6 %copy-start.9 = (bf16[512,768]{1,0:T(8,128)(2,1)}, bf16[512,768]{1,0:T(8,128)(2,1)S(1)}, u32[]{:S(2)}) copy-start(bf16[512,768]{1,0:T(8,128)(2,1)S(1)} %get-tuple-element.38.refs_1_.refs_2_) | copy-start | bytes 2359300
  135.6 19.3 %copy-start.11 = (bf16[512,768]{1,0:T(8,128)(2,1)}, bf16[512,768]{1,0:T(8,128)(2,1)S(1)}, u32[]{:S(2)}) copy-start(bf16[512,768]{1,0:T(8,128)(2,1)S(1)} %get-tuple-element.37.refs_4_.refs_0_.refs_2_) | copy-start | bytes 2359300
  141.4 23.5 %collective-permute-start.1 = (bf16[2,384,512]{2,1,0:T(8,128)(2,1)}, bf16[2,384,512]{2,1,0:T(8,128)(2,1)}, u32[]{:S(2)}, u32[]{:S(2)}) collective-permute-start(bf16[2,384,512]{2,1,0:T(8,128)(2,1)} %get-tuple-element.39.refs_4_), channel_id=1, source_target_pairs={{0,32},{16,48},{32,64},{48,80},{64,96},{80,112},{96,0},{112,16},{1... | collective-permute-start | bytes 2359304 | tf_op jit(solution)/shard_map/ppermute | solution.py:405
  143.1 21.9 %collective-permute-start.2 = (bf16[2,384,512]{2,1,0:T(8,128)(2,1)}, bf16[2,384,512]{2,1,0:T(8,128)(2,1)}, u32[]{:S(2)}, u32[]{:S(2)}) collective-permute-start(bf16[2,384,512]{2,1,0:T(8,128)(2,1)} %get-tuple-element.40.refs_5_), channel_id=1, source_target_pairs={{0,96},{16,112},{32,0},{48,16},{64,32},{80,48},{96,64},{112,80},{1... | collective-permute-start | bytes 2359304 | tf_op jit(solution)/shard_map/ppermute | solution.py:405
  160.0 14.6 %collective-permute-start.4 = (bf16[4,512,768]{2,1,0:T(8,128)(2,1)}, bf16[4,512,768]{2,1,0:T(8,128)(2,1)}, u32[]{:S(2)}, u32[]{:S(2)}) collective-permute-start(bf16[4,512,768]{2,1,0:T(8,128)(2,1)} %weight_part.8.refs_4_), channel_id=1, source_target_pairs={{0,16},{16,0},{32,48},{48,32},{64,80},{80,64},{96,112},{112,96},{1... | collective-permute-start | bytes 9437192 | tf_op jit(solution)/shard_map/ppermute | solution.py:402
  160.4 64.1 %all-to-all-start.1 = ((bf16[16,32,4096]{2,1,0:T(8,128)(2,1)}), bf16[16,32,4096]{2,1,0:T(8,128)(2,1)}, u32[]{:S(2)}, u32[]{:S(2)}) async-start(bf16[16,32,4096]{2,1,0:T(8,128)(2,1)} %bitcast.24), calls=%async_computation.1 | async-start | bytes 8388608 | tf_op jit(solution)/shard_map/all_to_all | solution.py:395
  165.0 2.1 copy-start.10
  167.0 36.7 %collective-permute-start.7 = (bf16[384,512]{1,0:T(8,128)(2,1)}, bf16[384,512]{1,0:T(8,128)(2,1)}, u32[]{:S(2)}, u32[]{:S(2)}) collective-permute-start(bf16[384,512]{1,0:T(8,128)(2,1)} %get-tuple-element.43.refs_3_), channel_id=1, source_target_pairs={{0,32},{16,48},{32,64},{48,80},{64,96},{80,112},{96,0},{112,16},{1... | collective-permute-start | bytes 1179656 | tf_op jit(solution)/shard_map/ppermute | solution.py:405
  167.0 7.6 %copy-start.12 = (bf16[512,768]{1,0:T(8,128)(2,1)S(1)}, bf16[512,768]{1,0:T(8,128)(2,1)}, u32[]{:S(2)}) copy-start(bf16[512,768]{1,0:T(8,128)(2,1)} %copy-done.11) | copy-start | bytes 2359300
  171.2 35.2 %collective-permute-start.8 = (bf16[384,512]{1,0:T(8,128)(2,1)}, bf16[384,512]{1,0:T(8,128)(2,1)}, u32[]{:S(2)}, u32[]{:S(2)}) collective-permute-start(bf16[384,512]{1,0:T(8,128)(2,1)} %get-tuple-element.44.refs_4_), channel_id=1, source_target_pairs={{0,96},{16,112},{32,0},{48,16},{64,32},{80,48},{96,64},{112,80},{1... | collective-permute-start | bytes 1179656 | tf_op jit(solution)/shard_map/ppermute | solution.py:405
  173.9 7.2 %collective-permute-start.3 = (bf16[4,512,768]{2,1,0:T(8,128)(2,1)S(1)}, bf16[4,512,768]{2,1,0:T(8,128)(2,1)S(1)}, u32[]{:S(2)}, u32[]{:S(2)}) collective-permute-start(bf16[4,512,768]{2,1,0:T(8,128)(2,1)S(1)} %weight_part.9.refs_4_), channel_id=1, source_target_pairs={{0,16},{16,0},{32,48},{48,32},{64,80},{80,64},{96,112},{112,96},{1... | collective-permute-start | bytes 9437192 | tf_op jit(solution)/shard_map/ppermute | solution.py:402
  179.6 19.6 %collective-permute-start.10 = (bf16[2,256,768]{2,1,0:T(8,128)(2,1)S(1)}, bf16[2,256,768]{2,1,0:T(8,128)(2,1)S(1)}, u32[]{:S(2)}, u32[]{:S(2)}) collective-permute-start(bf16[2,256,768]{2,1,0:T(8,128)(2,1)S(1)} %get-tuple-element.46.refs_5_), channel_id=1, source_target_pairs={{0,96},{16,112},{32,0},{48,16},{64,32},{80,48},{96,64},{112,80},{1... | collective-permute-start | bytes 2359304 | tf_op jit(solution)/shard_map/ppermute | solution.py:405
  180.0 22.5 %collective-permute-start.9 = (bf16[2,256,768]{2,1,0:T(8,128)(2,1)S(1)}, bf16[2,256,768]{2,1,0:T(8,128)(2,1)S(1)}, u32[]{:S(2)}, u32[]{:S(2)}) collective-permute-start(bf16[2,256,768]{2,1,0:T(8,128)(2,1)S(1)} %get-tuple-element.45.refs_4_), channel_id=1, source_target_pairs={{0,32},{16,48},{32,64},{48,80},{64,96},{80,112},{96,0},{112,16},{1... | collective-permute-start | bytes 2359304 | tf_op jit(solution)/shard_map/ppermute | solution.py:405
  186.6 30.5 %collective-permute-start.5 = (bf16[2,256,768]{2,1,0:T(8,128)(2,1)}, bf16[2,256,768]{2,1,0:T(8,128)(2,1)}, u32[]{:S(2)}, u32[]{:S(2)}) collective-permute-start(bf16[2,256,768]{2,1,0:T(8,128)(2,1)} %get-tuple-element.49.refs_4_), channel_id=1, source_target_pairs={{0,32},{16,48},{32,64},{48,80},{64,96},{80,112},{96,0},{112,16},{1... | collective-permute-start | bytes 2359304 | tf_op jit(solution)/shard_map/ppermute | solution.py:405
  199.2 4.4 %copy-start.2 = (bf16[2,256,768]{2,1,0:T(8,128)(2,1)}, bf16[2,256,768]{2,1,0:T(8,128)(2,1)S(1)}, u32[]{:S(2)}) copy-start(bf16[2,256,768]{2,1,0:T(8,128)(2,1)S(1)} %collective-permute-done.10.refs_3_.refs_1_) | copy-start | bytes 2359300
  199.3 19.2 %collective-permute-start.6 = (bf16[2,256,768]{2,1,0:T(8,128)(2,1)}, bf16[2,256,768]{2,1,0:T(8,128)(2,1)}, u32[]{:S(2)}, u32[]{:S(2)}) collective-permute-start(bf16[2,256,768]{2,1,0:T(8,128)(2,1)} %get-tuple-element.50.refs_5_), channel_id=1, source_target_pairs={{0,96},{16,112},{32,0},{48,16},{64,32},{80,48},{96,64},{112,80},{1... | collective-permute-start | bytes 2359304 | tf_op jit(solution)/shard_map/ppermute | solution.py:405
  202.5 1.2 copy-start.4
  203.7 25.5 %collective-permute-start.11 = (bf16[256,768]{1,0:T(8,128)(2,1)}, bf16[256,768]{1,0:T(8,128)(2,1)}, u32[]{:S(2)}, u32[]{:S(2)}) collective-permute-start(bf16[256,768]{1,0:T(8,128)(2,1)} %get-tuple-element.54.refs_5_), channel_id=1, source_target_pairs={{0,32},{16,48},{32,64},{48,80},{64,96},{80,112},{96,0},{112,16},{1... | collective-permute-start | bytes 1179656 | tf_op jit(solution)/shard_map/ppermute | solution.py:405
  203.7 25.5 %collective-permute-start.12 = (bf16[256,768]{1,0:T(8,128)(2,1)}, bf16[256,768]{1,0:T(8,128)(2,1)}, u32[]{:S(2)}, u32[]{:S(2)}) collective-permute-start(bf16[256,768]{1,0:T(8,128)(2,1)} %get-tuple-element.55.refs_6_), channel_id=1, source_target_pairs={{0,96},{16,112},{32,0},{48,16},{64,32},{80,48},{96,64},{112,80},{1... | collective-permute-start | bytes 1179656 | tf_op jit(solution)/shard_map/ppermute | solution.py:405
  218.5 1.1 copy-start.7
  220.9 11.8 %collective-permute-start.13 = (bf16[256,768]{1,0:T(8,128)(2,1)S(1)}, bf16[256,768]{1,0:T(8,128)(2,1)S(1)}, u32[]{:S(2)}, u32[]{:S(2)}) collective-permute-start(bf16[256,768]{1,0:T(8,128)(2,1)S(1)} %get-tuple-element.56.refs_2_), channel_id=1, source_target_pairs={{0,32},{16,48},{32,64},{48,80},{64,96},{80,112},{96,0},{112,16},{1... | collective-permute-start | bytes 1179656 | tf_op jit(solution)/shard_map/ppermute | solution.py:405
  221.0 14.2 %collective-permute-start.14 = (bf16[256,768]{1,0:T(8,128)(2,1)S(1)}, bf16[256,768]{1,0:T(8,128)(2,1)S(1)}, u32[]{:S(2)}, u32[]{:S(2)}) collective-permute-start(bf16[256,768]{1,0:T(8,128)(2,1)S(1)} %get-tuple-element.57.refs_3_), channel_id=1, source_target_pairs={{0,96},{16,112},{32,0},{48,16},{64,32},{80,48},{96,64},{112,80},{1... | collective-permute-start | bytes 1179656 | tf_op jit(solution)/shard_map/ppermute | solution.py:405
  224.5 4.7 %copy-start.3 = (bf16[2,256,768]{2,1,0:T(8,128)(2,1)S(1)}, bf16[2,256,768]{2,1,0:T(8,128)(2,1)}, u32[]{:S(2)}) copy-start(bf16[2,256,768]{2,1,0:T(8,128)(2,1)} %copy-done.2) | copy-start | bytes 2359300
  224.5 4.7 %copy-start.5 = (bf16[2,256,768]{2,1,0:T(8,128)(2,1)S(1)}, bf16[2,256,768]{2,1,0:T(8,128)(2,1)}, u32[]{:S(2)}) copy-start(bf16[2,256,768]{2,1,0:T(8,128)(2,1)} %copy-done.4) | copy-start | bytes 2359300
  229.2 1.2 copy-start.6
  235.2 1.1 copy-start.8

commit v3 on v2

--- a/solution.py
+++ b/solution.py
@@ -130,7 +130,7 @@
         ],
         out_specs=[pl.BlockSpec((slots, step), lambda j: (0, j)), whole((slots, tok))],
         out_shape=[
-            pltpu.HBM((slots, 2 * width), jnp.bfloat16),
+            pltpu.VMEM((slots, 2 * width), jnp.bfloat16),
             jax.ShapeDtypeStruct((slots, tok), jnp.bfloat16),
         ],
         scratch_shapes=[pltpu.VMEM((2, slots, 1), jnp.float32)],
@@ -143,30 +143,47 @@
 def forward(first, w_gate, w_up):
     rows = first.shape[0]
     width, units = w_gate.shape[1:]
-    block = 256
+    block = 1024
+    steps = width // block
 
     def body(x_ref, wg_ref, wu_ref, hidden_ref, for_gate_ref, for_up_ref):
-        gate = dot_nn(x_ref[...], wg_ref[...])
-        up = dot_nn(x_ref[...], wu_ref[...])
-        sig = jax.nn.sigmoid(gate)
-        act = gate * sig
-        hidden_ref[...] = (act * up).astype(jnp.bfloat16)
-        for_gate_ref[...] = up * sig * (1.0 + gate * (1.0 - sig))
-        for_up_ref[...] = act
-
-    out = pl.BlockSpec((rows, block), lambda j: (0, j))
-    weight = pl.BlockSpec((None, width, block), lambda j: (0, 0, j))
+        k = pl.program_id(0)
+        gate_part = dot_nn(x_ref[...], wg_ref[...])
+        up_part = dot_nn(x_ref[...], wu_ref[...])
+
+        @pl.when(k == 0)
+        def _():
+            for_up_ref[...] = gate_part
+            for_gate_ref[...] = up_part
+
+        @pl.when((k > 0) & (k < steps - 1))
+        def _():
+            for_up_ref[...] += gate_part
+            for_gate_ref[...] += up_part
+
+        @pl.when(k == steps - 1)
+        def _():
+            gate = for_up_ref[...] + gate_part
+            up = for_gate_ref[...] + up_part
+            sig = jax.nn.sigmoid(gate)
+            act = gate * sig
+            hidden_ref[...] = (act * up).astype(jnp.bfloat16)
+            for_gate_ref[...] = up * sig * (1.0 + gate * (1.0 - sig))
+            for_up_ref[...] = act
+
+    out = pl.BlockSpec((rows, units), lambda k: (0, 0))
+    weight = pl.BlockSpec((None, block, units), lambda k: (0, k, 0))
     return pl.pallas_call(
         body,
-        grid=(units // block,),
-        in_specs=[pl.BlockSpec((rows, width), lambda j: (0, 0)), weight, weight],
+        grid=(steps,),
+        in_specs=[pl.BlockSpec((rows, block), lambda k: (0, k)), weight, weight],
         out_specs=[out, out, out],
         out_shape=[
             jax.ShapeDtypeStruct((rows, units), jnp.bfloat16),
             jax.ShapeDtypeStruct((rows, units), jnp.float32),
             jax.ShapeDtypeStruct((rows, units), jnp.float32),
         ],
-        compiler_params=params(24),
+        compiler_params=params(28),
         cost_estimate=takes(10),
         name="forward",
     )(in_hbm(first), in_vmem(w_gate), in_vmem(w_up))
@@ -175,27 +192,42 @@
 def hidden_grad(buf, offset, w_down, for_gate, for_up, after=(), micros=LONG):
     rows = buf.shape[0]
     units, width = w_down.shape[1:]
-    block = 256
-
-    def body(q_ref, wd_ref, for_gate_ref, for_up_ref, d_gate_ref, d_up_ref):
-        total = dot_nt(q_ref[...], wd_ref[...])
-        d_gate_ref[...] = (total * for_gate_ref[...]).astype(jnp.bfloat16)
-        d_up_ref[...] = (total * for_up_ref[...]).astype(jnp.bfloat16)
-
-    tile = pl.BlockSpec((rows, block), lambda j: (0, j))
+    block = 1024
+    steps = width // block
+
+    def body(q_ref, wd_ref, for_gate_ref, for_up_ref, d_gate_ref, d_up_ref, sum_ref):
+        k = pl.program_id(0)
+        part = dot_nt(q_ref[...], wd_ref[...])
+
+        @pl.when(k == 0)
+        def _():
+            sum_ref[...] = part
+
+        @pl.when((k > 0) & (k < steps - 1))
+        def _():
+            sum_ref[...] += part
+
+        @pl.when(k == steps - 1)
+        def _():
+            total = sum_ref[...] + part
+            d_gate_ref[...] = (total * for_gate_ref[...]).astype(jnp.bfloat16)
+            d_up_ref[...] = (total * for_up_ref[...]).astype(jnp.bfloat16)
+
+    tile = pl.BlockSpec((rows, units), lambda k: (0, 0))
     return pl.pallas_call(
         ordered(body, 4, len(after)),
-        grid=(units // block,),
+        grid=(steps,),
         in_specs=[
-            pl.BlockSpec((rows, width), lambda j: (0, offset)),
-            pl.BlockSpec((None, block, width), lambda j: (0, j, 0)),
+            pl.BlockSpec((rows, block), lambda k: (0, offset * steps + k)),
+            pl.BlockSpec((None, units, block), lambda k: (0, 0, k)),
             tile,
             tile,
         ]
         + [ANY] * len(after),
         out_specs=[tile] * 2,
         out_shape=[jax.ShapeDtypeStruct((rows, units), jnp.bfloat16)] * 2,
-        compiler_params=params(20),
+        scratch_shapes=[pltpu.VMEM((rows, units), jnp.float32)],
+        compiler_params=params(24),
         cost_estimate=takes(micros),
         name="hidden_grad",
     )(in_hbm(buf), in_vmem(w_down), for_gate, for_up, *after)
@@ -414,30 +446,32 @@
     d_gate, d_up = hidden_grad(rows, 1, w_down, for_gate, for_up, after=(other_down,), micros=MICROS['hg'])
     own_down = weight_part(*down, place, True, swapped(other_down), after=(d_gate,), micros=MICROS['wD'])
     hop_down = one_hop(*own_down[:2])
-    rows_back = input_rows(
-        d_gate, d_up, w_gate, w_up, after=(own_down[0], own_down[1]), micros=MICROS["i0"]
-    )
-    back = exchange(rows_back)
     gate = ("rows", rows, 0, part, d_gate)
     other_gate = weight_part(
-        *gate, place, False, after=(corner(rows_back),), micros=MICROS["oG"]
-    )
-    next_down = passed_on(own_down, hop_down, after=(other_gate,), micros=MICROS["nD"])
+        *gate, place, False, after=tuple(own_down), micros=MICROS["oG"]
+    )
+    rows_back = input_rows(
+        d_gate, d_up, w_gate, w_up, after=(other_gate,), micros=MICROS["i0"]
+    )
+    back = exchange(rows_back)
+    next_down = passed_on(
+        own_down, hop_down, after=(corner(rows_back),), micros=MICROS["nD"]
+    )
     last_down = one_hop(*next_down)
+    own_gate = weight_part(
+        *gate, place, True, swapped(other_gate), after=next_down, micros=MICROS["wG"]
+    )
     up = ("rows", rows, 0, part, d_up)
-    other_up = weight_part(*up, place, False, after=next_down, micros=MICROS["oU"])
-    own_gate = weight_part(
-        *gate, place, True, swapped(other_gate), after=(other_up,), micros=MICROS["wG"]
-    )
+    other_up = weight_part(*up, place, False, after=tuple(own_gate), micros=MICROS["oU"])
     hop_gate = one_hop(*own_gate[:2])
+    grad_down = finished(own_down, hop_down, last_down, after=(other_up,), micros=MICROS["fD"])
     own_up = weight_part(
-        *up, place, True, swapped(other_up), after=own_gate[:2], micros=MICROS["wU"]
+        *up, place, True, swapped(other_up), after=(grad_down,), micros=MICROS["wU"]
     )
     hop_up = one_hop(*own_up[:2])
     next_gate = passed_on(own_gate, hop_gate, after=own_up[:2], micros=MICROS["nG"])
     last_gate = one_hop(*next_gate)
-    grad_down = finished(own_down, hop_down, last_down, after=next_gate, micros=MICROS["fD"])
-    next_up = passed_on(own_up, hop_up, after=(grad_down,), micros=MICROS["nU"])
+    next_up = passed_on(own_up, hop_up, after=next_gate, micros=MICROS["nU"])
     last_up = one_hop(*next_up)
     grad_tokens = combine(select, back, after=next_up)
     grad_gate = finished(own_gate, hop_gate, last_gate, after=(grad_tokens,), micros=MICROS["fG"])

time: 240 us -> 236 us (0.983)
  waiting for transfers between devices: 24.7 us -> 20 us
    ppermute x12, waiting for transfers between devices: 24.7 us -> 17.2 us  [one_hop(): return (lax.ppermute(fwd, 'dp', ahead), lax.ppermute(bwd, 'dp', behind))]
    ppermute x3, waiting for transfers between devices: 0.01 us -> 2.74 us  [swapped(): return lax.ppermute(value, 'dp', swap)]
    unnamed x30 -> x42, local copies, waits for them, and re-layouts: 3.64 us -> 5.94 us
where the time goes in v3:
time: 236 us; the launch traced here: 233 us
  blocking collectives  102 us (43%)
  Pallas kernels  78.1 us (33%)
  starting transfers between devices  24.9 us (11%)
  waiting for transfers between devices  20 us (8%)
  local copies, waits for them, and re-layouts  5.94 us (3%)
    all_to_all x1, blocking collectives, exchange(): lax.all_to_all(blocks, 'expert', split_axis=0, concat_axis=0, tiled=True)  102 us
    pallas_call x6, Pallas kernels, weight_part(): pl.pallas_call(ordered(body, 1 + len(args), len(after)), grid_spec=pltpu....  29.4 us
    ppermute x12, waiting for transfers between devices, one_hop(): return (lax.ppermute(fwd, 'dp', ahead), lax.ppermute(bwd, 'dp', behind))  17.2 us
    ppermute x12, starting transfers between devices, one_hop(): return (lax.ppermute(fwd, 'dp', ahead), lax.ppermute(bwd, 'dp', behind))  16.1 us
    pallas_call x1, Pallas kernels, forward(): pl.pallas_call(body, grid=(steps,), in_specs=[pl.BlockSpec((rows, block),...  10.3 us
    pallas_call x1, Pallas kernels, input_rows(): pl.pallas_call(ordered(body, 4, len(after)), grid=(width // block,), in_s...  9.01 us
    pallas_call x1, Pallas kernels, pack(): pl.pallas_call(ordered(body, 5, 1), grid=(2 * nx,), in_specs=[whole(ids.s...  7.1 us
    pallas_call x3, Pallas kernels, finished(): pl.pallas_call(ordered(body, 5, len(after)), grid=(2,), in_specs=[tile, s...  6.95 us
  transfers between devices with their start and end apart: 16, of which 4 were waited for; matrix products, arithmetic and copies ran while one was open for 0% of the time, Pallas kernels for 21%

profile of v3, /device:TPU:1, one launch (start us, length us, event | category | flops | bytes accessed | tf_op | source)
XLA Modules:
  0.0 233.0 jit_solution(8438608953490223287)
XLA Ops:
  0.6 7.1 %pack.1 = (bf16[512,8192]{1,0:T(8,128)(2,1)S(1)}, bf16[512,128]{1,0:T(8,128)(2,1)S(1)}) custom-call(s32[2,128]{1,0:T(2,128)} %bitcast.26, s32[2,128]{1,0:T(2,128)} %bitcast.27, s32[4,16]{1,0:T(4,128)} %bitcast.25, bf16[128,4096]{1,0:T(8,128)(2,1)} %refs_3_.2, bf16[128,4096]{1,0:T(8,128)(2,1)} %refs_4_.1, s32[1]{0:T(128)} %bitcast.3.refs_5_.place_ref.refs_0_), custom_call_target="tpu_custom_call" | custom-call | flops 11500000256 | bytes 1000000 | tf_op jit(solution)/shard_map/pack/pallas_call | solution.py:120
  7.7 0.0 copy-start.9
  7.8 0.0 copy-start
  7.8 0.0 copy-start.1
  7.8 0.0 slice-start
  7.8 102.5 %all_to_all.10 = bf16[16,32,8192]{2,1,0:T(8,128)(2,1)} all-to-all(bf16[16,32,8192]{2,1,0:T(8,128)(2,1)S(1)} %bitcast.11), channel_id=1, replica_groups=mesh['dp'=8,'expert'=16] {'expert'}, dimensions={0} | all-to-all | bytes 16777216 | tf_op jit(solution)/shard_map/all_to_all | solution.py:427
  110.3 0.0 slice-start.1
  110.3 10.3 %forward.1 = (bf16[512,768]{1,0:T(8,128)(2,1)S(1)}, f32[512,768]{1,0:T(8,128)S(1)}, f32[512,768]{1,0:T(8,128)S(1)}) custom-call(bf16[512,8192]{1,0:T(8,128)(2,1)} %bitcast.16, bf16[1,4096,768]{2,1,0:T(8,128)(2,1)S(1)} %copy-done, bf16[1,4096,768]{2,1,0:T(8,128)(2,1)S(1)} %copy-done.1), custom_call_target="tpu_custom_call" | custom-call | flops 11500000256 | bytes 1000000 | tf_op jit(solution)/shard_map/forward/pallas_call | solution.py:176
  120.6 4.0 %weight_part.6.refs_4_ = bf16[4,768,512]{2,1,0:T(8,128)(2,1)S(1)} custom-call(s32[1]{0:T(128)} %bitcast.3.refs_5_.place_ref.refs_0_, bf16[512,8192]{1,0:T(8,128)(2,1)} %bitcast.17, bf16[512,768]{1,0:T(8,128)(2,1)S(1)} %get-tuple-element.36.other_ref.refs_2_), custom_call_target="tpu_custom_call" | custom-call | flops 5750000128 | bytes 1000000 | tf_op jit(solution)/shard_map/weight_part/pallas_call | solution.py:297
  124.6 2.6 %collective-permute-start = (bf16[4,768,512]{2,1,0:T(8,128)(2,1)S(1)}, bf16[4,768,512]{2,1,0:T(8,128)(2,1)S(1)}, u32[]{:S(2)}, u32[]{:S(2)}) collective-permute-start(bf16[4,768,512]{2,1,0:T(8,128)(2,1)S(1)} %weight_part.6.refs_4_), channel_id=1, source_target_pairs={{0,16},{16,0},{32,48},{48,32},{64,80},{80,64},{96,112},{112,96},{1... | collective-permute-start | bytes 9437192 | tf_op jit(solution)/shard_map/ppermute | solution.py:434
  127.3 6.3 %hidden_grad.1 = (bf16[512,768]{1,0:T(8,128)(2,1)S(1)}, bf16[512,768]{1,0:T(8,128)(2,1)S(1)}) custom-call(bf16[512,8192]{1,0:T(8,128)(2,1)} %bitcast.18, bf16[1,768,4096]{2,1,0:T(8,128)(2,1)S(1)} %bitcast.13, f32[512,768]{1,0:T(8,128)S(1)} %get-tuple-element.34.refs_2_, f32[512,768]{1,0:T(8,128)S(1)} %get-tuple-element.35.refs_3_, ...), custom_call_target="tpu_custom_call" | custom-call | flops 5750000128 | bytes 1000000 | tf_op jit(solution)/shard_map/hidden_grad/pallas_call | solution.py:217
  133.6 0.0 copy-start.5
  133.6 0.0 collective-permute-done.refs_3_
  133.6 5.7 %weight_part.7 = (bf16[2,384,512]{2,1,0:T(8,128)(2,1)}, bf16[2,384,512]{2,1,0:T(8,128)(2,1)}, bf16[384,512]{1,0:T(8,128)(2,1)S(1)}, bf16[384,512]{1,0:T(8,128)(2,1)S(1)}, bf16[768,512]{1,0:T(8,128)(2,1)S(1)}) custom-call(s32[1]{0:T(128)} %bitcast.3.refs_5_.place_ref.refs_0_, bf16[512,8192]{1,0:T(8,128)(2,1)} %bitcast.19, ...), custom_call_target="tpu_custom_call" | custom-call | flops 5750000128 | bytes 1000000 | tf_op jit(solution)/shard_map/weight_part/pallas_call | solution.py:297
  139.3 1.7 collective-permute-start.2
  140.9 2.1 collective-permute-start.3
  143.1 5.2 %weight_part.8.refs_4_ = bf16[4,512,768]{2,1,0:T(8,128)(2,1)} custom-call(s32[1]{0:T(128)} %bitcast.3.refs_5_.place_ref.refs_0_, bf16[512,8192]{1,0:T(8,128)(2,1)} %bitcast.20, bf16[512,768]{1,0:T(8,128)(2,1)S(1)} %get-tuple-element.37.refs_4_.refs_2_.refs_0_, bf16[2,384,512]{2,1,0:T(8,128)(2,1)} %get-tuple-element.39.refs_3_, ...), custom_call_target="tpu_custom_call" | custom-call | flops 115000000512 | bytes 1000000 | tf_op jit(solution)/shard_map/weight_part/pallas_call | solution.py:297
  148.3 0.3 collective-permute-start.1
  148.6 9.0 %input_rows.1 = bf16[512,4096]{1,0:T(8,128)(2,1)} custom-call(bf16[512,768]{1,0:T(8,128)(2,1)S(1)} %get-tuple-element.37.refs_4_.refs_2_.refs_0_, bf16[512,768]{1,0:T(8,128)(2,1)S(1)} %get-tuple-element.38.refs_1_.refs_2_, bf16[1,4096,768]{2,1,0:T(8,128)(2,1)S(1)} %copy-done, bf16[1,4096,768]{2,1,0:T(8,128)(2,1)S(1)} %copy-done.1, ...), custom_call_target="tpu_custom_call" | custom-call | flops 115000000512 | bytes 1000000 | tf_op jit(solution)/shard_map/input_rows/pallas_call | solution.py:320
  157.6 4.6 %all-to-all-start.1 = ((bf16[16,32,4096]{2,1,0:T(8,128)(2,1)}), bf16[16,32,4096]{2,1,0:T(8,128)(2,1)}, u32[]{:S(2)}, u32[]{:S(2)}) async-start(bf16[16,32,4096]{2,1,0:T(8,128)(2,1)} %bitcast.24), calls=%async_computation.1 | async-start | bytes 8388608 | tf_op jit(solution)/shard_map/all_to_all | solution.py:427
  162.2 0.7 slice_multiply_fusion.refs_4_
  162.9 0.0 collective-permute-done.2.refs_2_
  162.9 0.0 collective-permute-done.3.refs_3_.refs_1_
  162.9 2.0 passed_on.3
  164.9 0.0 collective-permute-start.5
  164.9 2.7 %collective-permute-start.6 = (bf16[384,512]{1,0:T(8,128)(2,1)}, bf16[384,512]{1,0:T(8,128)(2,1)}, u32[]{:S(2)}, u32[]{:S(2)}) collective-permute-start(bf16[384,512]{1,0:T(8,128)(2,1)} %get-tuple-element.45.refs_5_), channel_id=1, source_target_pairs={{0,96},{16,112},{32,0},{48,16},{64,32},{80,48},{96,64},{112,80},{1... | collective-permute-start | bytes 1179656 | tf_op jit(solution)/shard_map/ppermute | solution.py:437
  167.6 0.0 collective-permute-done.1.refs_3_
  167.6 6.0 %weight_part.9 = (bf16[2,256,768]{2,1,0:T(8,128)(2,1)}, bf16[2,256,768]{2,1,0:T(8,128)(2,1)}, bf16[256,768]{1,0:T(8,128)(2,1)S(1)}, bf16[256,768]{1,0:T(8,128)(2,1)S(1)}, bf16[512,768]{1,0:T(8,128)(2,1)S(1)}) custom-call(s32[1]{0:T(128)} %bitcast.3.refs_5_.place_ref.refs_0_, bf16[512,8192]{1,0:T(8,128)(2,1)} %bitcast.21, ...), custom_call_target="tpu_custom_call" | custom-call | flops 115000000512 | bytes 1000000 | tf_op jit(solution)/shard_map/weight_part/pallas_call | solution.py:297
  173.6 0.5 collective-permute-start.10
  174.1 0.9 collective-permute-start.9
  175.1 4.1 %weight_part.10.refs_5_ = bf16[4,512,768]{2,1,0:T(8,128)(2,1)S(1)} custom-call(s32[1]{0:T(128)} %bitcast.3.refs_5_.place_ref.refs_0_, bf16[512,8192]{1,0:T(8,128)(2,1)} %bitcast.22, bf16[512,768]{1,0:T(8,128)(2,1)S(1)} %copy-done.6, bf16[2,256,768]{2,1,0:T(8,128)(2,1)} %get-tuple-element.46.refs_3_, bf16[2,256,768]{2,1,0:T(8,128)(2,1)} %get-tuple-element.47.refs_4_, ...), custom_call_target="tpu_custom_call" | custom-call | flops 115000000512 | bytes 1000000 | tf_op jit(solution)/shard_map/weight_part/pallas_call | solution.py:297
  179.2 0.7 copy-done.15
  180.0 0.7 copy-done.17
  180.7 1.3 collective-permute-start.4
  182.0 0.0 collective-permute-done.5.refs_3_
  182.0 0.0 collective-permute-done.6.refs_4_
  182.0 2.5 %finished.3.refs_4_ = bf16[768,512]{1,0:T(8,128)(2,1)} custom-call(bf16[768,512]{1,0:T(8,128)(2,1)S(1)} %copy-done.8, bf16[2,384,512]{2,1,0:T(8,128)(2,1)} %collective-permute-done.3.refs_3_.refs_1_, bf16[2,384,512]{2,1,0:T(8,128)(2,1)} %collective-permute-done.2.refs_2_, bf16[384,512]{1,0:T(8,128)(2,1)} %collective-permute-done.5.refs_3_, ...), custom_call_target="tpu_custom_call" | custom-call | flops 115000000512 | bytes 1000000 | tf_op jit(solution)/shard_map/finished/pallas_call | solution.py:377
  184.5 2.7 %collective-permute-done.4.refs_3_ = bf16[4,512,768]{2,1,0:T(8,128)(2,1)S(1)} collective-permute-done((bf16[4,512,768]{2,1,0:T(8,128)(2,1)S(1)}, bf16[4,512,768]{2,1,0:T(8,128)(2,1)S(1)}, u32[]{:S(2)}, u32[]{:S(2)}) %collective-permute-start.4) | collective-permute-done | bytes 3145760 | tf_op jit(solution)/shard_map/ppermute | solution.py:434
  187.3 1.1 copy-done.3
  188.4 4.4 %weight_part.11 = (bf16[2,256,768]{2,1,0:T(8,128)(2,1)S(1)}, bf16[2,256,768]{2,1,0:T(8,128)(2,1)S(1)}, bf16[256,768]{1,0:T(8,128)(2,1)S(1)}, bf16[256,768]{1,0:T(8,128)(2,1)S(1)}, bf16[512,768]{1,0:T(8,128)(2,1)S(1)}) custom-call(s32[1]{0:T(128)} %bitcast.3.refs_5_.place_ref.refs_0_, bf16[512,8192]{1,0:T(8,128)(2,1)} %bitcast.23, ...), custom_call_target="tpu_custom_call" | custom-call | flops 115000000512 | bytes 1000000 | tf_op jit(solution)/shard_map/weight_part/pallas_call | solution.py:297
  192.8 0.1 collective-permute-start.7
  192.9 2.7 %collective-permute-start.8 = (bf16[2,256,768]{2,1,0:T(8,128)(2,1)S(1)}, bf16[2,256,768]{2,1,0:T(8,128)(2,1)S(1)}, u32[]{:S(2)}, u32[]{:S(2)}) collective-permute-start(bf16[2,256,768]{2,1,0:T(8,128)(2,1)S(1)} %get-tuple-element.54.refs_5_), channel_id=1, source_target_pairs={{0,96},{16,112},{32,0},{48,16},{64,32},{80,48},{96,64},{112,80},{1... | collective-permute-start | bytes 2359304 | tf_op jit(solution)/shard_map/ppermute | solution.py:437
  195.6 0.0 collective-permute-done.10.refs_3_.refs_1_
  195.6 0.0 collective-permute-done.9.refs_2_
  195.6 1.3 passed_on.4
  196.9 0.1 collective-permute-start.11
  197.0 2.7 %collective-permute-start.12 = (bf16[256,768]{1,0:T(8,128)(2,1)S(1)}, bf16[256,768]{1,0:T(8,128)(2,1)S(1)}, u32[]{:S(2)}, u32[]{:S(2)}) collective-permute-start(bf16[256,768]{1,0:T(8,128)(2,1)S(1)} %get-tuple-element.56.refs_5_), channel_id=1, source_target_pairs={{0,96},{16,112},{32,0},{48,16},{64,32},{80,48},{96,64},{112,80},{1... | collective-permute-start | bytes 1179656 | tf_op jit(solution)/shard_map/ppermute | solution.py:437
  199.7 13.3 %collective-permute-done.7.refs_2_ = bf16[2,256,768]{2,1,0:T(8,128)(2,1)S(1)} collective-permute-done((bf16[2,256,768]{2,1,0:T(8,128)(2,1)S(1)}, bf16[2,256,768]{2,1,0:T(8,128)(2,1)S(1)}, u32[]{:S(2)}, u32[]{:S(2)}) %collective-permute-start.7) | collective-permute-done | bytes 786464 | tf_op jit(solution)/shard_map/ppermute | solution.py:437
  213.0 0.0 collective-permute-done.8.refs_3_.refs_1_
  213.0 0.9 passed_on.5
  213.9 0.0 collective-permute-start.13
  213.9 2.7 %collective-permute-start.14 = (bf16[256,768]{1,0:T(8,128)(2,1)}, bf16[256,768]{1,0:T(8,128)(2,1)}, u32[]{:S(2)}, u32[]{:S(2)}) collective-permute-start(bf16[256,768]{1,0:T(8,128)(2,1)} %get-tuple-element.58.refs_3_), channel_id=1, source_target_pairs={{0,96},{16,112},{32,0},{48,16},{64,32},{80,48},{96,64},{112,80},{1... | collective-permute-start | bytes 1179656 | tf_op jit(solution)/shard_map/ppermute | solution.py:437
  216.6 0.1 all-to-all-done.1
  216.6 0.9 copy-done.10
  217.6 4.7 %combine.1.refs_5_ = bf16[128,4096]{1,0:T(8,128)(2,1)} custom-call(bf16[512,128]{1,0:T(8,128)(2,1)S(1)} %copy-done.10, bf16[512,4096]{1,0:T(8,128)(2,1)} %bitcast.7.refs_1_, bf16[256,768]{1,0:T(8,128)(2,1)} %get-tuple-element.57.refs_2_, bf16[256,768]{1,0:T(8,128)(2,1)} %get-tuple-element.58.refs_3_), custom_call_target="tpu_custom_call" | custom-call | flops 5750000128 | bytes 1000000 | tf_op jit(solution)/shard_map/combine/pallas_call | solution.py:397
  222.3 0.0 collective-permute-done.11.refs_3_
  222.3 0.0 collective-permute-done.12.refs_4_
  222.3 0.0 copy-start.2
  222.3 1.2 copy-done.2
  223.5 2.3 finished.4.refs_5_
  225.8 3.9 %collective-permute-done.13.refs_3_ = bf16[256,768]{1,0:T(8,128)(2,1)S(1)} collective-permute-done((bf16[256,768]{1,0:T(8,128)(2,1)}, bf16[256,768]{1,0:T(8,128)(2,1)S(1)}, u32[]{:S(2)}, u32[]{:S(2)}) %collective-permute-start.13) | collective-permute-done | bytes 393248 | tf_op jit(solution)/shard_map/ppermute | solution.py:437
  229.7 0.0 collective-permute-done.14.refs_4_
  229.7 1.1 copy-done.4
  230.9 2.1 finished.5
  (30 shorter events, 0.1 us)
Async XLA Ops:
  7.7 102.5 %copy-start.9 = (bf16[512,128]{1,0:T(8,128)(2,1)}, bf16[512,128]{1,0:T(8,128)(2,1)S(1)}, u32[]{:S(2)}) copy-start(bf16[512,128]{1,0:T(8,128)(2,1)S(1)} %get-tuple-element.32.refs_0_) | copy-start | bytes 393220
  7.8 102.5 %copy-start = (bf16[1,4096,768]{2,1,0:T(8,128)(2,1)S(1)}, bf16[1,4096,768]{2,1,0:T(8,128)(2,1)}, u32[]{:S(2)}) copy-start(bf16[1,4096,768]{2,1,0:T(8,128)(2,1)} %refs_2_.1) | copy-start | bytes 18874372
  7.8 102.5 %copy-start.1 = (bf16[1,4096,768]{2,1,0:T(8,128)(2,1)S(1)}, bf16[1,4096,768]{2,1,0:T(8,128)(2,1)}, u32[]{:S(2)}) copy-start(bf16[1,4096,768]{2,1,0:T(8,128)(2,1)} %refs_3_.3) | copy-start | bytes 18874372
  7.8 119.5 %slice-start = ((s8[6291456]{0:T(1024)(128)(4,1)}), s8[4194304]{0:T(1024)(128)(4,1)S(1)}, s32[]{:S(2)}) async-start(s8[6291456]{0:T(1024)(128)(4,1)} %bitcast.12), calls=%async_computation.2 | async-start | bytes 8388608
  110.3 17.0 %slice-start.1 = ((s8[6291456]{0:T(1024)(128)(4,1)}), s8[2097152]{0:T(1024)(128)(4,1)S(1)}, s32[]{:S(2)}) async-start(s8[6291456]{0:T(1024)(128)(4,1)} %bitcast.12), calls=%async_computation.3 | async-start | bytes 4194304
  124.6 9.0 %collective-permute-start = (bf16[4,768,512]{2,1,0:T(8,128)(2,1)S(1)}, bf16[4,768,512]{2,1,0:T(8,128)(2,1)S(1)}, u32[]{:S(2)}, u32[]{:S(2)}) collective-permute-start(bf16[4,768,512]{2,1,0:T(8,128)(2,1)S(1)} %weight_part.6.refs_4_), channel_id=1, source_target_pairs={{0,16},{16,0},{32,48},{48,32},{64,80},{80,64},{96,112},{112,96},{1... | collective-permute-start | bytes 9437192 | tf_op jit(solution)/shard_map/ppermute | solution.py:434
  133.6 15.0 %copy-start.5 = (bf16[512,768]{1,0:T(8,128)(2,1)}, bf16[512,768]{1,0:T(8,128)(2,1)S(1)}, u32[]{:S(2)}) copy-start(bf16[512,768]{1,0:T(8,128)(2,1)S(1)} %get-tuple-element.38.refs_1_.refs_2_) | copy-start | bytes 2359300
  139.3 9.0 %copy-start.7 = (bf16[768,512]{1,0:T(8,128)(2,1)}, bf16[768,512]{1,0:T(8,128)(2,1)S(1)}, u32[]{:S(2)}) copy-start(bf16[768,512]{1,0:T(8,128)(2,1)S(1)} %get-tuple-element.43.refs_7_.refs_0_) | copy-start | bytes 2359300
  139.3 23.6 %collective-permute-start.2 = (bf16[2,384,512]{2,1,0:T(8,128)(2,1)}, bf16[2,384,512]{2,1,0:T(8,128)(2,1)}, u32[]{:S(2)}, u32[]{:S(2)}) collective-permute-start(bf16[2,384,512]{2,1,0:T(8,128)(2,1)} %get-tuple-element.39.refs_3_), channel_id=1, source_target_pairs={{0,32},{16,48},{32,64},{48,80},{64,96},{80,112},{96,0},{112,16},{1... | collective-permute-start | bytes 2359304 | tf_op jit(solution)/shard_map/ppermute | solution.py:437
  140.9 21.9 %collective-permute-start.3 = (bf16[2,384,512]{2,1,0:T(8,128)(2,1)}, bf16[2,384,512]{2,1,0:T(8,128)(2,1)}, u32[]{:S(2)}, u32[]{:S(2)}) collective-permute-start(bf16[2,384,512]{2,1,0:T(8,128)(2,1)} %get-tuple-element.40.refs_4_), channel_id=1, source_target_pairs={{0,96},{16,112},{32,0},{48,16},{64,32},{80,48},{96,64},{112,80},{1... | collective-permute-start | bytes 2359304 | tf_op jit(solution)/shard_map/ppermute | solution.py:437
  148.3 19.3 %collective-permute-start.1 = (bf16[4,512,768]{2,1,0:T(8,128)(2,1)}, bf16[4,512,768]{2,1,0:T(8,128)(2,1)}, u32[]{:S(2)}, u32[]{:S(2)}) collective-permute-start(bf16[4,512,768]{2,1,0:T(8,128)(2,1)} %weight_part.8.refs_4_), channel_id=1, source_target_pairs={{0,16},{16,0},{32,48},{48,32},{64,80},{80,64},{96,112},{112,96},{1... | collective-permute-start | bytes 9437192 | tf_op jit(solution)/shard_map/ppermute | solution.py:434
  157.6 59.0 %all-to-all-start.1 = ((bf16[16,32,4096]{2,1,0:T(8,128)(2,1)}), bf16[16,32,4096]{2,1,0:T(8,128)(2,1)}, u32[]{:S(2)}, u32[]{:S(2)}) async-start(bf16[16,32,4096]{2,1,0:T(8,128)(2,1)} %bitcast.24), calls=%async_computation.1 | async-start | bytes 8388608 | tf_op jit(solution)/shard_map/all_to_all | solution.py:427
  164.9 17.1 %collective-permute-start.5 = (bf16[384,512]{1,0:T(8,128)(2,1)}, bf16[384,512]{1,0:T(8,128)(2,1)}, u32[]{:S(2)}, u32[]{:S(2)}) collective-permute-start(bf16[384,512]{1,0:T(8,128)(2,1)} %get-tuple-element.44.refs_4_), channel_id=1, source_target_pairs={{0,32},{16,48},{32,64},{48,80},{64,96},{80,112},{96,0},{112,16},{1... | collective-permute-start | bytes 1179656 | tf_op jit(solution)/shard_map/ppermute | solution.py:437
  164.9 10.2 %copy-start.6 = (bf16[512,768]{1,0:T(8,128)(2,1)S(1)}, bf16[512,768]{1,0:T(8,128)(2,1)}, u32[]{:S(2)}) copy-start(bf16[512,768]{1,0:T(8,128)(2,1)} %copy-done.5) | copy-start | bytes 2359300
  164.9 17.1 %collective-permute-start.6 = (bf16[384,512]{1,0:T(8,128)(2,1)}, bf16[384,512]{1,0:T(8,128)(2,1)}, u32[]{:S(2)}, u32[]{:S(2)}) collective-permute-start(bf16[384,512]{1,0:T(8,128)(2,1)} %get-tuple-element.45.refs_5_), channel_id=1, source_target_pairs={{0,96},{16,112},{32,0},{48,16},{64,32},{80,48},{96,64},{112,80},{1... | collective-permute-start | bytes 1179656 | tf_op jit(solution)/shard_map/ppermute | solution.py:437
  173.6 5.6 %copy-start.11 = (bf16[512,768]{1,0:T(8,128)(2,1)}, bf16[512,768]{1,0:T(8,128)(2,1)S(1)}, u32[]{:S(2)}) copy-start(bf16[512,768]{1,0:T(8,128)(2,1)S(1)} %get-tuple-element.50.refs_7_.refs_0_) | copy-start | bytes 2359300
  173.6 22.0 %collective-permute-start.10 = (bf16[2,256,768]{2,1,0:T(8,128)(2,1)}, bf16[2,256,768]{2,1,0:T(8,128)(2,1)}, u32[]{:S(2)}, u32[]{:S(2)}) collective-permute-start(bf16[2,256,768]{2,1,0:T(8,128)(2,1)} %get-tuple-element.47.refs_4_), channel_id=1, source_target_pairs={{0,96},{16,112},{32,0},{48,16},{64,32},{80,48},{96,64},{112,80},{1... | collective-permute-start | bytes 2359304 | tf_op jit(solution)/shard_map/ppermute | solution.py:437
  174.1 21.4 %collective-permute-start.9 = (bf16[2,256,768]{2,1,0:T(8,128)(2,1)}, bf16[2,256,768]{2,1,0:T(8,128)(2,1)}, u32[]{:S(2)}, u32[]{:S(2)}) collective-permute-start(bf16[2,256,768]{2,1,0:T(8,128)(2,1)} %get-tuple-element.46.refs_3_), channel_id=1, source_target_pairs={{0,32},{16,48},{32,64},{48,80},{64,96},{80,112},{96,0},{112,16},{1... | collective-permute-start | bytes 2359304 | tf_op jit(solution)/shard_map/ppermute | solution.py:437
  175.1 6.9 %copy-start.8 = (bf16[768,512]{1,0:T(8,128)(2,1)S(1)}, bf16[768,512]{1,0:T(8,128)(2,1)}, u32[]{:S(2)}) copy-start(bf16[768,512]{1,0:T(8,128)(2,1)} %copy-done.7) | copy-start | bytes 2359300
  179.2 0.7 copy-start.15
  180.0 0.7 copy-start.17
  180.7 6.6 %collective-permute-start.4 = (bf16[4,512,768]{2,1,0:T(8,128)(2,1)S(1)}, bf16[4,512,768]{2,1,0:T(8,128)(2,1)S(1)}, u32[]{:S(2)}, u32[]{:S(2)}) collective-permute-start(bf16[4,512,768]{2,1,0:T(8,128)(2,1)S(1)} %weight_part.10.refs_5_), channel_id=1, source_target_pairs={{0,16},{16,0},{32,48},{48,32},{64,80},{80,64},{96,112},{112,96},{1... | collective-permute-start | bytes 9437192 | tf_op jit(solution)/shard_map/ppermute | solution.py:434
  187.3 1.1 copy-start.3
  188.4 7.2 %copy-start.16 = (bf16[256,768]{1,0:T(8,128)(2,1)S(1)}, bf16[256,768]{1,0:T(8,128)(2,1)}, u32[]{:S(2)}) copy-start(bf16[256,768]{1,0:T(8,128)(2,1)} %copy-done.15) | copy-start | bytes 1179652
  188.4 7.2 %copy-start.18 = (bf16[256,768]{1,0:T(8,128)(2,1)S(1)}, bf16[256,768]{1,0:T(8,128)(2,1)}, u32[]{:S(2)}) copy-start(bf16[256,768]{1,0:T(8,128)(2,1)} %copy-done.17) | copy-start | bytes 1179652
  192.8 4.1 %copy-start.13 = (bf16[512,768]{1,0:T(8,128)(2,1)}, bf16[512,768]{1,0:T(8,128)(2,1)S(1)}, u32[]{:S(2)}) copy-start(bf16[512,768]{1,0:T(8,128)(2,1)S(1)} %get-tuple-element.59.refs_0_) | copy-start | bytes 2359300
  192.8 20.1 %collective-permute-start.7 = (bf16[2,256,768]{2,1,0:T(8,128)(2,1)S(1)}, bf16[2,256,768]{2,1,0:T(8,128)(2,1)S(1)}, u32[]{:S(2)}, u32[]{:S(2)}) collective-permute-start(bf16[2,256,768]{2,1,0:T(8,128)(2,1)S(1)} %get-tuple-element.53.refs_4_), channel_id=1, source_target_pairs={{0,32},{16,48},{32,64},{48,80},{64,96},{80,112},{96,0},{112,16},{1... | collective-permute-start | bytes 2359304 | tf_op jit(solution)/shard_map/ppermute | solution.py:437
  192.9 20.1 %collective-permute-start.8 = (bf16[2,256,768]{2,1,0:T(8,128)(2,1)S(1)}, bf16[2,256,768]{2,1,0:T(8,128)(2,1)S(1)}, u32[]{:S(2)}, u32[]{:S(2)}) collective-permute-start(bf16[2,256,768]{2,1,0:T(8,128)(2,1)S(1)} %get-tuple-element.54.refs_5_), channel_id=1, source_target_pairs={{0,96},{16,112},{32,0},{48,16},{64,32},{80,48},{96,64},{112,80},{1... | collective-permute-start | bytes 2359304 | tf_op jit(solution)/shard_map/ppermute | solution.py:437
  196.9 25.3 %collective-permute-start.11 = (bf16[256,768]{1,0:T(8,128)(2,1)S(1)}, bf16[256,768]{1,0:T(8,128)(2,1)S(1)}, u32[]{:S(2)}, u32[]{:S(2)}) collective-permute-start(bf16[256,768]{1,0:T(8,128)(2,1)S(1)} %get-tuple-element.55.refs_4_), channel_id=1, source_target_pairs={{0,32},{16,48},{32,64},{48,80},{64,96},{80,112},{96,0},{112,16},{1... | collective-permute-start | bytes 1179656 | tf_op jit(solution)/shard_map/ppermute | solution.py:437
  197.0 25.2 %collective-permute-start.12 = (bf16[256,768]{1,0:T(8,128)(2,1)S(1)}, bf16[256,768]{1,0:T(8,128)(2,1)S(1)}, u32[]{:S(2)}, u32[]{:S(2)}) collective-permute-start(bf16[256,768]{1,0:T(8,128)(2,1)S(1)} %get-tuple-element.56.refs_5_), channel_id=1, source_target_pairs={{0,96},{16,112},{32,0},{48,16},{64,32},{80,48},{96,64},{112,80},{1... | collective-permute-start | bytes 1179656 | tf_op jit(solution)/shard_map/ppermute | solution.py:437
  213.9 15.8 %collective-permute-start.13 = (bf16[256,768]{1,0:T(8,128)(2,1)}, bf16[256,768]{1,0:T(8,128)(2,1)S(1)}, u32[]{:S(2)}, u32[]{:S(2)}) collective-permute-start(bf16[256,768]{1,0:T(8,128)(2,1)} %get-tuple-element.57.refs_2_), channel_id=1, source_target_pairs={{0,32},{16,48},{32,64},{48,80},{64,96},{80,112},{96,0},{112,16},{1... | collective-permute-start | bytes 1179656 | tf_op jit(solution)/shard_map/ppermute | solution.py:437
  213.9 15.8 %collective-permute-start.14 = (bf16[256,768]{1,0:T(8,128)(2,1)}, bf16[256,768]{1,0:T(8,128)(2,1)}, u32[]{:S(2)}, u32[]{:S(2)}) collective-permute-start(bf16[256,768]{1,0:T(8,128)(2,1)} %get-tuple-element.58.refs_3_), channel_id=1, source_target_pairs={{0,96},{16,112},{32,0},{48,16},{64,32},{80,48},{96,64},{112,80},{1... | collective-permute-start | bytes 1179656 | tf_op jit(solution)/shard_map/ppermute | solution.py:437
  216.6 0.9 copy-start.10
  217.5 4.7 %copy-start.12 = (bf16[512,768]{1,0:T(8,128)(2,1)S(1)}, bf16[512,768]{1,0:T(8,128)(2,1)}, u32[]{:S(2)}) copy-start(bf16[512,768]{1,0:T(8,128)(2,1)} %copy-done.11) | copy-start | bytes 2359300
  217.5 12.2 %copy-start.14 = (bf16[512,768]{1,0:T(8,128)(2,1)S(1)}, bf16[512,768]{1,0:T(8,128)(2,1)}, u32[]{:S(2)}) copy-start(bf16[512,768]{1,0:T(8,128)(2,1)} %copy-done.13) | copy-start | bytes 2359300
  222.3 1.2 copy-start.2
  229.7 1.1 copy-start.4

commit v4 on v3

--- a/solution.py
+++ b/solution.py
@@ -60,7 +60,7 @@
     experts = history.shape[1]
     cap = tok * 2 * 2 // experts
     slots = experts * cap
-    step = 1024
+    step = 2048
     nx = width // step
 
     def body(ids_ref, codes_ref, hist_ref, x_ref, g_ref, out_ref, sel_ref, fac_ref):
@@ -134,59 +134,82 @@
             jax.ShapeDtypeStruct((slots, tok), jnp.bfloat16),
         ],
         scratch_shapes=[pltpu.VMEM((2, slots, 1), jnp.float32)],
-        compiler_params=params(14),
+        compiler_params=params(22),
         cost_estimate=takes(10),
         name="pack",
     )(in_hbm(ids), in_hbm(codes), in_hbm(history), in_hbm(tokens), in_hbm(grad), place)
 
 
-def forward(first, w_gate, w_up):
+def forward(first, w_gate, w_up, place):
     rows = first.shape[0]
     width, units = w_gate.shape[1:]
     block = 1024
     steps = width // block
-
-    def body(x_ref, wg_ref, wu_ref, hidden_ref, for_gate_ref, for_up_ref):
+    part = width // 8
+
+    def body(place_ref, x_ref, q_ref, wg_ref, wu_ref, hidden_ref, for_gate_ref, for_up_ref, down_ref):
         k = pl.program_id(0)
-        gate_part = dot_nn(x_ref[...], wg_ref[...])
-        up_part = dot_nn(x_ref[...], wu_ref[...])
 
         @pl.when(k == 0)
         def _():
-            for_up_ref[...] = gate_part
-            for_gate_ref[...] = up_part
+            for_up_ref[...] = dot_nn(x_ref[...], wg_ref[...])
+            for_gate_ref[...] = dot_nn(x_ref[...], wu_ref[...])
 
         @pl.when((k > 0) & (k < steps - 1))
         def _():
-            for_up_ref[...] += gate_part
-            for_gate_ref[...] += up_part
+            for_up_ref[...] += dot_nn(x_ref[...], wg_ref[...])
+            for_gate_ref[...] += dot_nn(x_ref[...], wu_ref[...])
 
         @pl.when(k == steps - 1)
         def _():
-            gate = for_up_ref[...] + gate_part
-            up = for_gate_ref[...] + up_part
+            gate = for_up_ref[...] + dot_nn(x_ref[...], wg_ref[...])
+            up = for_gate_ref[...] + dot_nn(x_ref[...], wu_ref[...])
             sig = jax.nn.sigmoid(gate)
             act = gate * sig
             hidden_ref[...] = (act * up).astype(jnp.bfloat16)
             for_gate_ref[...] = up * sig * (1.0 + gate * (1.0 - sig))
             for_up_ref[...] = act
 
-    out = pl.BlockSpec((rows, units), lambda k: (0, 0))
-    weight = pl.BlockSpec((None, block, units), lambda k: (0, k, 0))
+        @pl.when(k >= steps)
+        def _():
+            down_ref[...] = dot_tn(hidden_ref[...], q_ref[...]).astype(jnp.bfloat16)
+
+    def column(k, at):
+        z, core = at[0] // 2, at[0] % 2
+        j = jnp.maximum(k - steps, 0)
+        return (0, width // part + (z + 6 - j) % 4 * 2 + 1 - core)
+
+    held = lambda k: jnp.minimum(k, steps - 1)
+    out = pl.BlockSpec((rows, units), lambda k, at: (0, 0))
+    weight = pl.BlockSpec((None, block, units), lambda k, at: (0, held(k), 0))
     return pl.pallas_call(
         body,
-        grid=(steps,),
-        in_specs=[pl.BlockSpec((rows, block), lambda k: (0, k)), weight, weight],
-        out_specs=[out, out, out],
+        grid_spec=pltpu.PrefetchScalarGridSpec(
+            num_scalar_prefetch=1,
+            grid=(steps + 4,),
+            in_specs=[
+                pl.BlockSpec((rows, block), lambda k, at: (0, held(k))),
+                pl.BlockSpec((rows, part), column),
+                weight,
+                weight,
+            ],
+            out_specs=[
+                out,
+                out,
+                out,
+                pl.BlockSpec((None, units, part), lambda k, at: (jnp.maximum(k - steps, 0), 0, 0)),
+            ],
+        ),
         out_shape=[
             jax.ShapeDtypeStruct((rows, units), jnp.bfloat16),
             jax.ShapeDtypeStruct((rows, units), jnp.float32),
             jax.ShapeDtypeStruct((rows, units), jnp.float32),
+            jax.ShapeDtypeStruct((4, units, part), jnp.bfloat16),
         ],
-        compiler_params=params(28),
+        compiler_params=params(26),
         cost_estimate=takes(10),
         name="forward",
-    )(in_hbm(first), in_vmem(w_gate), in_vmem(w_up))
+    )(place, in_hbm(first), in_hbm(first), in_vmem(w_gate), in_vmem(w_up))
 
 
 def hidden_grad(buf, offset, w_down, for_gate, for_up, after=(), micros=LONG):
@@ -290,7 +313,8 @@
         ins.append(pl.BlockSpec((None,) + shape, lambda j, at: (j, 0, 0)))
         shapes = [(2, half, shape[1])] * 2 + [(half, shape[1])] * 2 + [shape]
         outs = [pl.BlockSpec(s, lambda j, at, n=len(s): (0,) * n) for s in shapes]
-        out_shape = [jax.ShapeDtypeStruct(s, flat) for s in shapes]
+        out_shape = [jax.ShapeDtypeStruct(s, flat) for s in shapes[:2]]
+        out_shape += [pltpu.HBM(s, flat) for s in shapes[2:]]
         args = (in_hbm(buf), other, received)
     ins += [ANY] * len(after)
     body = plain if received is None else summed
@@ -350,7 +374,7 @@
         compiler_params=params(8),
         cost_estimate=takes(micros),
         name="passed_on",
-    )(parts[2], parts[3], *hop, *after)
+    )(in_hbm(parts[2]), in_hbm(parts[3]), *hop, *after)
 
 
 def finished(parts, hop, last, after=(), micros=LONG):
@@ -383,7 +407,7 @@
         compiler_params=params(10),
         cost_estimate=takes(micros),
         name="finished",
-    )(parts[4], hop[1], hop[0], *last, *after)
+    )(in_hbm(parts[4]), hop[1], hop[0], *last, *after)
 
 
 def combine(select, returned, after=()):
@@ -407,7 +431,7 @@
         compiler_params=params(12),
         cost_estimate=takes(5),
         name="combine",
-    )(select, in_hbm(returned), *after)
+    )(in_hbm(select), in_hbm(returned), *after)
 
 
 def shards(tokens_in, out_grad, expert_ids, router_codes, amax_history, w_gate, w_up, w_down):
@@ -430,6 +454,9 @@
     def corner(value):
         return value[:16, :128] * 2
 
+    def named(parts):
+        return (*parts[:2], *[in_hbm(value) for value in parts[2:]])
+
     def swapped(value):
         return lax.ppermute(value, "dp", swap)
 
@@ -440,15 +467,14 @@
         tokens_in, out_grad, expert_ids.T, router_codes.T, amax_history.T, place
     )
     rows = exchange(sent)
-    hidden, for_gate, for_up = forward(rows, w_gate, w_up)
+    hidden, for_gate, for_up, other_down = forward(rows, w_gate, w_up, place)
     down = ("columns", rows, width // part, part, hidden)
-    other_down = weight_part(*down, place, False, micros=MICROS['oD'])
     d_gate, d_up = hidden_grad(rows, 1, w_down, for_gate, for_up, after=(other_down,), micros=MICROS['hg'])
     own_down = weight_part(*down, place, True, swapped(other_down), after=(d_gate,), micros=MICROS['wD'])
     hop_down = one_hop(*own_down[:2])
     gate = ("rows", rows, 0, part, d_gate)
     other_gate = weight_part(
-        *gate, place, False, after=tuple(own_down), micros=MICROS["oG"]
+        *gate, place, False, after=named(own_down), micros=MICROS["oG"]
     )
     rows_back = input_rows(
         d_gate, d_up, w_gate, w_up, after=(other_gate,), micros=MICROS["i0"]
@@ -462,11 +488,11 @@
         *gate, place, True, swapped(other_gate), after=next_down, micros=MICROS["wG"]
     )
     up = ("rows", rows, 0, part, d_up)
-    other_up = weight_part(*up, place, False, after=tuple(own_gate), micros=MICROS["oU"])
+    other_up = weight_part(*up, place, False, after=named(own_gate), micros=MICROS["oU"])
     hop_gate = one_hop(*own_gate[:2])
     grad_down = finished(own_down, hop_down, last_down, after=(other_up,), micros=MICROS["fD"])
     own_up = weight_part(
-        *up, place, True, swapped(other_up), after=(grad_down,), micros=MICROS["wU"]
+        *up, place, True, swapped(other_up), after=(in_hbm(grad_down),), micros=MICROS["wU"]
     )
     hop_up = one_hop(*own_up[:2])
     next_gate = passed_on(own_gate, hop_gate, after=own_up[:2], micros=MICROS["nG"])
@@ -474,8 +500,8 @@
     next_up = passed_on(own_up, hop_up, after=next_gate, micros=MICROS["nU"])
     last_up = one_hop(*next_up)
     grad_tokens = combine(select, back, after=next_up)
-    grad_gate = finished(own_gate, hop_gate, last_gate, after=(grad_tokens,), micros=MICROS["fG"])
-    grad_up = finished(own_up, hop_up, last_up, after=(grad_gate,), micros=MICROS["fU"])
+    grad_gate = finished(own_gate, hop_gate, last_gate, after=(in_hbm(grad_tokens),), micros=MICROS["fG"])
+    grad_up = finished(own_up, hop_up, last_up, after=(in_hbm(grad_gate),), micros=MICROS["fU"])
     return (grad_tokens, grad_gate[None], grad_up[None], grad_down[None])
 
 

time: 236 us -> 230 us (0.975)
  local copies, waits for them, and re-layouts: 5.94 us -> 0.04 us
    unnamed x42 -> x14, local copies, waits for them, and re-layouts: 5.94 us -> 0.04 us
    pallas_call x6 -> x5, Pallas kernels: 29.4 us -> 27.5 us  [weight_part(): pl.pallas_call(ordered(body, 1 + len(args), len(after)), grid_spec=pltpu....]
  transfers between devices with their start and end apart: 16 -> 16, of which waited for: 4 -> 3; matrix products, arithmetic and copies ran while one was open for 0% -> 0% of each run, Pallas kernels for 21% -> 23%
where the time goes in v4:
time: 230 us; the launch traced here: 228 us
  blocking collectives  102 us (44%)
  Pallas kernels  78.7 us (34%)
  starting transfers between devices  24.9 us (11%)
  waiting for transfers between devices  20.7 us (9%)
    all_to_all x1, blocking collectives, exchange(): lax.all_to_all(blocks, 'expert', split_axis=0, concat_axis=0, tiled=True)  102 us
    pallas_call x5, Pallas kernels, weight_part(): pl.pallas_call(ordered(body, 1 + len(args), len(after)), grid_spec=pltpu....  27.5 us
    ppermute x12, waiting for transfers between devices, one_hop(): return (lax.ppermute(fwd, 'dp', ahead), lax.ppermute(bwd, 'dp', behind))  18.1 us
    ppermute x12, starting transfers between devices, one_hop(): return (lax.ppermute(fwd, 'dp', ahead), lax.ppermute(bwd, 'dp', behind))  16 us
    pallas_call x1, Pallas kernels, forward(): pl.pallas_call(body, grid_spec=pltpu.PrefetchScalarGridSpec(num_scalar_pr...  12.5 us
    pallas_call x1, Pallas kernels, input_rows(): pl.pallas_call(ordered(body, 4, len(after)), grid=(width // block,), in_s...  9.01 us
    pallas_call x3, Pallas kernels, finished(): pl.pallas_call(ordered(body, 5, len(after)), grid=(2,), in_specs=[tile, s...  7.32 us
    pallas_call x1, Pallas kernels, hidden_grad(): pl.pallas_call(ordered(body, 4, len(after)), grid=(steps,), in_specs=[pl....  6.33 us
  transfers between devices with their start and end apart: 16, of which 3 were waited for; matrix products, arithmetic and copies ran while one was open for 0% of the time, Pallas kernels for 23%

profile of v4, /device:TPU:1, one launch (start us, length us, event | category | flops | bytes accessed | tf_op | source)
XLA Modules:
  0.0 228.3 jit_solution(4422894521004076472)
XLA Ops:
  0.6 5.6 %pack.1 = (bf16[512,8192]{1,0:T(8,128)(2,1)S(1)}, bf16[512,128]{1,0:T(8,128)(2,1)S(1)}) custom-call(s32[2,128]{1,0:T(2,128)} %bitcast.24, s32[2,128]{1,0:T(2,128)} %bitcast.25, s32[4,16]{1,0:T(4,128)} %bitcast.23, bf16[128,4096]{1,0:T(8,128)(2,1)} %refs_3_.2, bf16[128,4096]{1,0:T(8,128)(2,1)} %refs_4_.1, s32[1]{0:T(128)} %bitcast.3.refs_5_.place_ref.refs_0_), custom_call_target="tpu_custom_call" | custom-call | flops 11500000256 | bytes 1000000 | tf_op jit(solution)/shard_map/pack/pallas_call | solution.py:120
  6.2 0.0 copy-start.4
  6.2 0.0 copy-start
  6.3 0.0 copy-start.1
  6.3 0.0 slice-start
  6.3 102.4 %all_to_all.10 = bf16[16,32,8192]{2,1,0:T(8,128)(2,1)} all-to-all(bf16[16,32,8192]{2,1,0:T(8,128)(2,1)S(1)} %bitcast.11), channel_id=1, replica_groups=mesh['dp'=8,'expert'=16] {'expert'}, dimensions={0} | all-to-all | bytes 16777216 | tf_op jit(solution)/shard_map/all_to_all | solution.py:451
  108.7 0.0 copy-done.4
  108.7 0.0 copy-done
  108.7 0.0 copy-done.1
  108.7 0.0 slice-start.1
  108.7 12.5 %forward.1 = (bf16[512,768]{1,0:T(8,128)(2,1)S(1)}, f32[512,768]{1,0:T(8,128)S(1)}, f32[512,768]{1,0:T(8,128)S(1)}, bf16[4,768,512]{2,1,0:T(8,128)(2,1)S(1)}) custom-call(s32[1]{0:T(128)} %bitcast.3.refs_5_.place_ref.refs_0_, bf16[512,8192]{1,0:T(8,128)(2,1)} %bitcast.14, bf16[512,8192]{1,0:T(8,128)(2,1)} %bitcast.15, bf16[1,4096,768]{2,1,0:T(8,128)(2,1)S(1)} %copy-done, ...), custom_call_target="tpu_custom_call" | custom-call | flops 11500000256 | bytes 1000000 | tf_op jit(solution)/shard_map/forward/pallas_call | solution.py:185
  121.2 2.7 %collective-permute-start = (bf16[4,768,512]{2,1,0:T(8,128)(2,1)S(1)}, bf16[4,768,512]{2,1,0:T(8,128)(2,1)S(1)}, u32[]{:S(2)}, u32[]{:S(2)}) collective-permute-start(bf16[4,768,512]{2,1,0:T(8,128)(2,1)S(1)} %get-tuple-element.37.refs_4_), channel_id=1, source_target_pairs={{0,16},{16,0},{32,48},{48,32},{64,80},{80,64},{96,112},{112,96},{1... | collective-permute-start | bytes 9437192 | tf_op jit(solution)/shard_map/ppermute | solution.py:461
  123.9 0.0 slice-done
  123.9 0.0 slice-done.1
  123.9 6.3 %hidden_grad.1 = (bf16[512,768]{1,0:T(8,128)(2,1)S(1)}, bf16[512,768]{1,0:T(8,128)(2,1)S(1)}) custom-call(bf16[512,8192]{1,0:T(8,128)(2,1)} %bitcast.16, bf16[1,768,4096]{2,1,0:T(8,128)(2,1)S(1)} %bitcast.13, f32[512,768]{1,0:T(8,128)S(1)} %get-tuple-element.35.refs_2_, f32[512,768]{1,0:T(8,128)S(1)} %get-tuple-element.36.refs_3_, ...), custom_call_target="tpu_custom_call" | custom-call | flops 5750000128 | bytes 1000000 | tf_op jit(solution)/shard_map/hidden_grad/pallas_call | solution.py:240
  130.2 0.0 copy-start.2
  130.3 0.0 collective-permute-done.refs_3_
  130.3 6.2 %weight_part.5 = (bf16[2,384,512]{2,1,0:T(8,128)(2,1)}, bf16[2,384,512]{2,1,0:T(8,128)(2,1)}, bf16[384,512]{1,0:T(8,128)(2,1)}, bf16[384,512]{1,0:T(8,128)(2,1)}, bf16[768,512]{1,0:T(8,128)(2,1)}) custom-call(s32[1]{0:T(128)} %bitcast.3.refs_5_.place_ref.refs_0_, bf16[512,8192]{1,0:T(8,128)(2,1)} %bitcast.17, ...), custom_call_target="tpu_custom_call" | custom-call | flops 5750000128 | bytes 1000000 | tf_op jit(solution)/shard_map/weight_part/pallas_call | solution.py:321
  136.5 1.7 collective-permute-start.2
  138.1 2.1 collective-permute-start.3
  140.2 5.2 %weight_part.6.refs_4_ = bf16[4,512,768]{2,1,0:T(8,128)(2,1)} custom-call(s32[1]{0:T(128)} %bitcast.3.refs_5_.place_ref.refs_0_, bf16[512,8192]{1,0:T(8,128)(2,1)} %bitcast.18, bf16[512,768]{1,0:T(8,128)(2,1)S(1)} %get-tuple-element.38.refs_4_.refs_2_.refs_0_, bf16[2,384,512]{2,1,0:T(8,128)(2,1)} %get-tuple-element.41.refs_3_, ...), custom_call_target="tpu_custom_call" | custom-call | flops 115000000512 | bytes 1000000 | tf_op jit(solution)/shard_map/weight_part/pallas_call | solution.py:321
  145.5 0.3 collective-permute-start.1
  145.8 0.0 copy-done.2
  145.8 9.0 %input_rows.1 = bf16[512,4096]{1,0:T(8,128)(2,1)} custom-call(bf16[512,768]{1,0:T(8,128)(2,1)S(1)} %get-tuple-element.38.refs_4_.refs_2_.refs_0_, bf16[512,768]{1,0:T(8,128)(2,1)S(1)} %get-tuple-element.39.refs_1_.refs_2_, bf16[1,4096,768]{2,1,0:T(8,128)(2,1)S(1)} %copy-done, bf16[1,4096,768]{2,1,0:T(8,128)(2,1)S(1)} %copy-done.1, ...), custom_call_target="tpu_custom_call" | custom-call | flops 115000000512 | bytes 1000000 | tf_op jit(solution)/shard_map/input_rows/pallas_call | solution.py:344
  154.8 4.6 %all-to-all-start.1 = ((bf16[16,32,4096]{2,1,0:T(8,128)(2,1)}), bf16[16,32,4096]{2,1,0:T(8,128)(2,1)}, u32[]{:S(2)}, u32[]{:S(2)}) async-start(bf16[16,32,4096]{2,1,0:T(8,128)(2,1)} %bitcast.22), calls=%async_computation.1 | async-start | bytes 8388608 | tf_op jit(solution)/shard_map/all_to_all | solution.py:451
  159.4 0.7 slice_multiply_fusion.refs_4_
  160.1 0.0 collective-permute-done.2.refs_2_
  160.1 0.0 collective-permute-done.3.refs_3_.refs_1_
  160.1 2.3 %passed_on.3 = (bf16[384,512]{1,0:T(8,128)(2,1)}, bf16[384,512]{1,0:T(8,128)(2,1)}) custom-call(bf16[384,512]{1,0:T(8,128)(2,1)} %get-tuple-element.43.refs_5_.refs_0_, bf16[384,512]{1,0:T(8,128)(2,1)} %get-tuple-element.44.refs_6_.refs_1_, bf16[2,384,512]{2,1,0:T(8,128)(2,1)} %collective-permute-done.2.refs_2_, ...), custom_call_target="tpu_custom_call" | custom-call | flops 115000000512 | bytes 1000000 | tf_op jit(solution)/shard_map/passed_on/pallas_call | solution.py:368
  162.4 0.0 collective-permute-start.5
  162.4 0.0 copy-start.3
  162.4 2.7 %collective-permute-start.6 = (bf16[384,512]{1,0:T(8,128)(2,1)}, bf16[384,512]{1,0:T(8,128)(2,1)}, u32[]{:S(2)}, u32[]{:S(2)}) collective-permute-start(bf16[384,512]{1,0:T(8,128)(2,1)} %get-tuple-element.47.refs_5_), channel_id=1, source_target_pairs={{0,96},{16,112},{32,0},{48,16},{64,32},{80,48},{96,64},{112,80},{1... | collective-permute-start | bytes 1179656 | tf_op jit(solution)/shard_map/ppermute | solution.py:464
  165.0 0.0 collective-permute-done.1.refs_3_
  165.0 6.5 %weight_part.7 = (bf16[2,256,768]{2,1,0:T(8,128)(2,1)}, bf16[2,256,768]{2,1,0:T(8,128)(2,1)}, bf16[256,768]{1,0:T(8,128)(2,1)}, bf16[256,768]{1,0:T(8,128)(2,1)}, bf16[512,768]{1,0:T(8,128)(2,1)}) custom-call(s32[1]{0:T(128)} %bitcast.3.refs_5_.place_ref.refs_0_, bf16[512,8192]{1,0:T(8,128)(2,1)} %bitcast.19, ...), custom_call_target="tpu_custom_call" | custom-call | flops 115000000512 | bytes 1000000 | tf_op jit(solution)/shard_map/weight_part/pallas_call | solution.py:321
  171.6 0.5 collective-permute-start.10
  172.1 0.9 collective-permute-start.9
  173.0 0.0 copy-done.3
  173.0 4.1 %weight_part.8.refs_5_ = bf16[4,512,768]{2,1,0:T(8,128)(2,1)S(1)} custom-call(s32[1]{0:T(128)} %bitcast.3.refs_5_.place_ref.refs_0_, bf16[512,8192]{1,0:T(8,128)(2,1)} %bitcast.20, bf16[512,768]{1,0:T(8,128)(2,1)S(1)} %copy-done.3, bf16[2,256,768]{2,1,0:T(8,128)(2,1)} %get-tuple-element.48.refs_3_, bf16[2,256,768]{2,1,0:T(8,128)(2,1)} %get-tuple-element.49.refs_4_, ...), custom_call_target="tpu_custom_call" | custom-call | flops 115000000512 | bytes 1000000 | tf_op jit(solution)/shard_map/weight_part/pallas_call | solution.py:321
  177.1 1.4 collective-permute-start.4
  178.5 0.0 collective-permute-done.5.refs_3_
  178.5 0.0 collective-permute-done.6.refs_4_
  178.5 2.6 %finished.3.refs_4_ = bf16[768,512]{1,0:T(8,128)(2,1)} custom-call(bf16[768,512]{1,0:T(8,128)(2,1)} %get-tuple-element.45.refs_7_.refs_0_, bf16[2,384,512]{2,1,0:T(8,128)(2,1)} %collective-permute-done.3.refs_3_.refs_1_, bf16[2,384,512]{2,1,0:T(8,128)(2,1)} %collective-permute-done.2.refs_2_, bf16[384,512]{1,0:T(8,128)(2,1)} %collective-permute-done.5.refs_3_, ...), custom_call_target="tpu_custom_call" | custom-call | flops 115000000512 | bytes 1000000 | tf_op jit(solution)/shard_map/finished/pallas_call | solution.py:401
  181.1 2.6 %collective-permute-done.4.refs_3_ = bf16[4,512,768]{2,1,0:T(8,128)(2,1)S(1)} collective-permute-done((bf16[4,512,768]{2,1,0:T(8,128)(2,1)S(1)}, bf16[4,512,768]{2,1,0:T(8,128)(2,1)S(1)}, u32[]{:S(2)}, u32[]{:S(2)}) %collective-permute-start.4) | collective-permute-done | bytes 3145760 | tf_op jit(solution)/shard_map/ppermute | solution.py:461
  183.8 5.5 %weight_part.9 = (bf16[2,256,768]{2,1,0:T(8,128)(2,1)S(1)}, bf16[2,256,768]{2,1,0:T(8,128)(2,1)S(1)}, bf16[256,768]{1,0:T(8,128)(2,1)}, bf16[256,768]{1,0:T(8,128)(2,1)}, bf16[512,768]{1,0:T(8,128)(2,1)}) custom-call(s32[1]{0:T(128)} %bitcast.3.refs_5_.place_ref.refs_0_, bf16[512,8192]{1,0:T(8,128)(2,1)} %bitcast.21, bf16[512,768]{1,0:T(8,128)(2,1)S(1)} %copy-done.3, ...), custom_call_target="tpu_custom_call" | custom-call | flops 115000000512 | bytes 1000000 | tf_op jit(solution)/shard_map/weight_part/pallas_call | solution.py:321
  189.2 0.0 collective-permute-start.7
  189.2 2.7 %collective-permute-start.8 = (bf16[2,256,768]{2,1,0:T(8,128)(2,1)S(1)}, bf16[2,256,768]{2,1,0:T(8,128)(2,1)S(1)}, u32[]{:S(2)}, u32[]{:S(2)}) collective-permute-start(bf16[2,256,768]{2,1,0:T(8,128)(2,1)S(1)} %get-tuple-element.56.refs_5_), channel_id=1, source_target_pairs={{0,96},{16,112},{32,0},{48,16},{64,32},{80,48},{96,64},{112,80},{1... | collective-permute-start | bytes 2359304 | tf_op jit(solution)/shard_map/ppermute | solution.py:464
  191.9 0.0 collective-permute-done.10.refs_3_.refs_1_
  191.9 0.0 collective-permute-done.9.refs_2_
  191.9 1.6 passed_on.4
  193.5 0.1 collective-permute-start.11
  193.6 2.7 %collective-permute-start.12 = (bf16[256,768]{1,0:T(8,128)(2,1)S(1)}, bf16[256,768]{1,0:T(8,128)(2,1)S(1)}, u32[]{:S(2)}, u32[]{:S(2)}) collective-permute-start(bf16[256,768]{1,0:T(8,128)(2,1)S(1)} %get-tuple-element.58.refs_5_), channel_id=1, source_target_pairs={{0,96},{16,112},{32,0},{48,16},{64,32},{80,48},{96,64},{112,80},{1... | collective-permute-start | bytes 1179656 | tf_op jit(solution)/shard_map/ppermute | solution.py:464
  196.3 13.1 %collective-permute-done.7.refs_2_ = bf16[2,256,768]{2,1,0:T(8,128)(2,1)S(1)} collective-permute-done((bf16[2,256,768]{2,1,0:T(8,128)(2,1)S(1)}, bf16[2,256,768]{2,1,0:T(8,128)(2,1)S(1)}, u32[]{:S(2)}, u32[]{:S(2)}) %collective-permute-start.7) | collective-permute-done | bytes 786464 | tf_op jit(solution)/shard_map/ppermute | solution.py:464
  209.3 0.0 collective-permute-done.8.refs_3_.refs_1_
  209.3 2.0 passed_on.5
  211.3 0.0 collective-permute-start.13
  211.3 2.7 %collective-permute-start.14 = (bf16[256,768]{1,0:T(8,128)(2,1)}, bf16[256,768]{1,0:T(8,128)(2,1)}, u32[]{:S(2)}, u32[]{:S(2)}) collective-permute-start(bf16[256,768]{1,0:T(8,128)(2,1)} %get-tuple-element.60.refs_3_), channel_id=1, source_target_pairs={{0,96},{16,112},{32,0},{48,16},{64,32},{80,48},{96,64},{112,80},{1... | collective-permute-start | bytes 1179656 | tf_op jit(solution)/shard_map/ppermute | solution.py:464
  214.0 0.0 all-to-all-done.1
  214.0 4.6 %combine.1.refs_5_ = bf16[128,4096]{1,0:T(8,128)(2,1)} custom-call(bf16[512,128]{1,0:T(8,128)(2,1)} %copy-done.4, bf16[512,4096]{1,0:T(8,128)(2,1)} %bitcast.7.refs_1_, bf16[256,768]{1,0:T(8,128)(2,1)} %get-tuple-element.59.refs_2_, bf16[256,768]{1,0:T(8,128)(2,1)} %get-tuple-element.60.refs_3_), custom_call_target="tpu_custom_call" | custom-call | flops 5750000128 | bytes 1000000 | tf_op jit(solution)/shard_map/combine/pallas_call | solution.py:421
  218.6 0.0 collective-permute-done.11.refs_3_
  218.6 0.0 collective-permute-done.12.refs_4_
  218.6 2.4 %finished.4.refs_5_ = bf16[512,768]{1,0:T(8,128)(2,1)} custom-call(bf16[512,768]{1,0:T(8,128)(2,1)} %get-tuple-element.52.refs_7_.refs_0_, bf16[2,256,768]{2,1,0:T(8,128)(2,1)} %collective-permute-done.10.refs_3_.refs_1_, bf16[2,256,768]{2,1,0:T(8,128)(2,1)} %collective-permute-done.9.refs_2_, bf16[256,768]{1,0:T(8,128)(2,1)S(1)} %collective-permute-done.11.refs_3_, ...), custom_call_target="tpu_custom_call" | custom-call | flops 115000000512 | bytes 1000000 | tf_op jit(solution)/shard_map/finished/pallas_call | solution.py:401
  221.0 5.0 %collective-permute-done.13.refs_3_ = bf16[256,768]{1,0:T(8,128)(2,1)S(1)} collective-permute-done((bf16[256,768]{1,0:T(8,128)(2,1)}, bf16[256,768]{1,0:T(8,128)(2,1)S(1)}, u32[]{:S(2)}, u32[]{:S(2)}) %collective-permute-start.13) | collective-permute-done | bytes 393248 | tf_op jit(solution)/shard_map/ppermute | solution.py:464
  226.1 0.0 collective-permute-done.14.refs_4_
  226.1 2.3 finished.5
  (1 shorter events, 0.0 us)
Async XLA Ops:
  6.2 102.5 %copy-start.4 = (bf16[512,128]{1,0:T(8,128)(2,1)}, bf16[512,128]{1,0:T(8,128)(2,1)S(1)}, u32[]{:S(2)}) copy-start(bf16[512,128]{1,0:T(8,128)(2,1)S(1)} %get-tuple-element.33.refs_0_) | copy-start | bytes 393220
  6.2 102.5 %copy-start = (bf16[1,4096,768]{2,1,0:T(8,128)(2,1)S(1)}, bf16[1,4096,768]{2,1,0:T(8,128)(2,1)}, u32[]{:S(2)}) copy-start(bf16[1,4096,768]{2,1,0:T(8,128)(2,1)} %refs_2_.1) | copy-start | bytes 18874372
  6.3 102.5 %copy-start.1 = (bf16[1,4096,768]{2,1,0:T(8,128)(2,1)S(1)}, bf16[1,4096,768]{2,1,0:T(8,128)(2,1)}, u32[]{:S(2)}) copy-start(bf16[1,4096,768]{2,1,0:T(8,128)(2,1)} %refs_3_.3) | copy-start | bytes 18874372
  6.3 117.6 %slice-start = ((s8[6291456]{0:T(1024)(128)(4,1)}), s8[4194304]{0:T(1024)(128)(4,1)S(1)}, s32[]{:S(2)}) async-start(s8[6291456]{0:T(1024)(128)(4,1)} %bitcast.12), calls=%async_computation.2 | async-start | bytes 8388608
  108.7 15.2 %slice-start.1 = ((s8[6291456]{0:T(1024)(128)(4,1)}), s8[2097152]{0:T(1024)(128)(4,1)S(1)}, s32[]{:S(2)}) async-start(s8[6291456]{0:T(1024)(128)(4,1)} %bitcast.12), calls=%async_computation.3 | async-start | bytes 4194304
  121.2 9.0 %collective-permute-start = (bf16[4,768,512]{2,1,0:T(8,128)(2,1)S(1)}, bf16[4,768,512]{2,1,0:T(8,128)(2,1)S(1)}, u32[]{:S(2)}, u32[]{:S(2)}) collective-permute-start(bf16[4,768,512]{2,1,0:T(8,128)(2,1)S(1)} %get-tuple-element.37.refs_4_), channel_id=1, source_target_pairs={{0,16},{16,0},{32,48},{48,32},{64,80},{80,64},{96,112},{112,96},{1... | collective-permute-start | bytes 9437192 | tf_op jit(solution)/shard_map/ppermute | solution.py:461
  130.2 15.5 %copy-start.2 = (bf16[512,768]{1,0:T(8,128)(2,1)}, bf16[512,768]{1,0:T(8,128)(2,1)S(1)}, u32[]{:S(2)}) copy-start(bf16[512,768]{1,0:T(8,128)(2,1)S(1)} %get-tuple-element.39.refs_1_.refs_2_) | copy-start | bytes 2359300
  136.5 23.6 %collective-permute-start.2 = (bf16[2,384,512]{2,1,0:T(8,128)(2,1)}, bf16[2,384,512]{2,1,0:T(8,128)(2,1)}, u32[]{:S(2)}, u32[]{:S(2)}) collective-permute-start(bf16[2,384,512]{2,1,0:T(8,128)(2,1)} %get-tuple-element.41.refs_3_), channel_id=1, source_target_pairs={{0,32},{16,48},{32,64},{48,80},{64,96},{80,112},{96,0},{112,16},{1... | collective-permute-start | bytes 2359304 | tf_op jit(solution)/shard_map/ppermute | solution.py:464
  138.1 21.9 %collective-permute-start.3 = (bf16[2,384,512]{2,1,0:T(8,128)(2,1)}, bf16[2,384,512]{2,1,0:T(8,128)(2,1)}, u32[]{:S(2)}, u32[]{:S(2)}) collective-permute-start(bf16[2,384,512]{2,1,0:T(8,128)(2,1)} %get-tuple-element.42.refs_4_), channel_id=1, source_target_pairs={{0,96},{16,112},{32,0},{48,16},{64,32},{80,48},{96,64},{112,80},{1... | collective-permute-start | bytes 2359304 | tf_op jit(solution)/shard_map/ppermute | solution.py:464
  145.5 19.6 %collective-permute-start.1 = (bf16[4,512,768]{2,1,0:T(8,128)(2,1)}, bf16[4,512,768]{2,1,0:T(8,128)(2,1)}, u32[]{:S(2)}, u32[]{:S(2)}) collective-permute-start(bf16[4,512,768]{2,1,0:T(8,128)(2,1)} %weight_part.6.refs_4_), channel_id=1, source_target_pairs={{0,16},{16,0},{32,48},{48,32},{64,80},{80,64},{96,112},{112,96},{1... | collective-permute-start | bytes 9437192 | tf_op jit(solution)/shard_map/ppermute | solution.py:461
  154.8 59.2 %all-to-all-start.1 = ((bf16[16,32,4096]{2,1,0:T(8,128)(2,1)}), bf16[16,32,4096]{2,1,0:T(8,128)(2,1)}, u32[]{:S(2)}, u32[]{:S(2)}) async-start(bf16[16,32,4096]{2,1,0:T(8,128)(2,1)} %bitcast.22), calls=%async_computation.1 | async-start | bytes 8388608 | tf_op jit(solution)/shard_map/all_to_all | solution.py:451
  162.4 16.1 %collective-permute-start.5 = (bf16[384,512]{1,0:T(8,128)(2,1)}, bf16[384,512]{1,0:T(8,128)(2,1)}, u32[]{:S(2)}, u32[]{:S(2)}) collective-permute-start(bf16[384,512]{1,0:T(8,128)(2,1)} %get-tuple-element.46.refs_4_), channel_id=1, source_target_pairs={{0,32},{16,48},{32,64},{48,80},{64,96},{80,112},{96,0},{112,16},{1... | collective-permute-start | bytes 1179656 | tf_op jit(solution)/shard_map/ppermute | solution.py:464
  162.4 10.7 %copy-start.3 = (bf16[512,768]{1,0:T(8,128)(2,1)S(1)}, bf16[512,768]{1,0:T(8,128)(2,1)}, u32[]{:S(2)}) copy-start(bf16[512,768]{1,0:T(8,128)(2,1)} %copy-done.2) | copy-start | bytes 2359300
  162.4 16.1 %collective-permute-start.6 = (bf16[384,512]{1,0:T(8,128)(2,1)}, bf16[384,512]{1,0:T(8,128)(2,1)}, u32[]{:S(2)}, u32[]{:S(2)}) collective-permute-start(bf16[384,512]{1,0:T(8,128)(2,1)} %get-tuple-element.47.refs_5_), channel_id=1, source_target_pairs={{0,96},{16,112},{32,0},{48,16},{64,32},{80,48},{96,64},{112,80},{1... | collective-permute-start | bytes 1179656 | tf_op jit(solution)/shard_map/ppermute | solution.py:464
  171.6 20.3 %collective-permute-start.10 = (bf16[2,256,768]{2,1,0:T(8,128)(2,1)}, bf16[2,256,768]{2,1,0:T(8,128)(2,1)}, u32[]{:S(2)}, u32[]{:S(2)}) collective-permute-start(bf16[2,256,768]{2,1,0:T(8,128)(2,1)} %get-tuple-element.49.refs_4_), channel_id=1, source_target_pairs={{0,96},{16,112},{32,0},{48,16},{64,32},{80,48},{96,64},{112,80},{1... | collective-permute-start | bytes 2359304 | tf_op jit(solution)/shard_map/ppermute | solution.py:464
  172.1 19.8 %collective-permute-start.9 = (bf16[2,256,768]{2,1,0:T(8,128)(2,1)}, bf16[2,256,768]{2,1,0:T(8,128)(2,1)}, u32[]{:S(2)}, u32[]{:S(2)}) collective-permute-start(bf16[2,256,768]{2,1,0:T(8,128)(2,1)} %get-tuple-element.48.refs_3_), channel_id=1, source_target_pairs={{0,32},{16,48},{32,64},{48,80},{64,96},{80,112},{96,0},{112,16},{1... | collective-permute-start | bytes 2359304 | tf_op jit(solution)/shard_map/ppermute | solution.py:464
  177.1 6.7 %collective-permute-start.4 = (bf16[4,512,768]{2,1,0:T(8,128)(2,1)S(1)}, bf16[4,512,768]{2,1,0:T(8,128)(2,1)S(1)}, u32[]{:S(2)}, u32[]{:S(2)}) collective-permute-start(bf16[4,512,768]{2,1,0:T(8,128)(2,1)S(1)} %weight_part.8.refs_5_), channel_id=1, source_target_pairs={{0,16},{16,0},{32,48},{48,32},{64,80},{80,64},{96,112},{112,96},{1... | collective-permute-start | bytes 9437192 | tf_op jit(solution)/shard_map/ppermute | solution.py:461
  189.2 20.1 %collective-permute-start.7 = (bf16[2,256,768]{2,1,0:T(8,128)(2,1)S(1)}, bf16[2,256,768]{2,1,0:T(8,128)(2,1)S(1)}, u32[]{:S(2)}, u32[]{:S(2)}) collective-permute-start(bf16[2,256,768]{2,1,0:T(8,128)(2,1)S(1)} %get-tuple-element.55.refs_4_), channel_id=1, source_target_pairs={{0,32},{16,48},{32,64},{48,80},{64,96},{80,112},{96,0},{112,16},{1... | collective-permute-start | bytes 2359304 | tf_op jit(solution)/shard_map/ppermute | solution.py:464
  189.2 20.1 %collective-permute-start.8 = (bf16[2,256,768]{2,1,0:T(8,128)(2,1)S(1)}, bf16[2,256,768]{2,1,0:T(8,128)(2,1)S(1)}, u32[]{:S(2)}, u32[]{:S(2)}) collective-permute-start(bf16[2,256,768]{2,1,0:T(8,128)(2,1)S(1)} %get-tuple-element.56.refs_5_), channel_id=1, source_target_pairs={{0,96},{16,112},{32,0},{48,16},{64,32},{80,48},{96,64},{112,80},{1... | collective-permute-start | bytes 2359304 | tf_op jit(solution)/shard_map/ppermute | solution.py:464
  193.5 25.1 %collective-permute-start.11 = (bf16[256,768]{1,0:T(8,128)(2,1)S(1)}, bf16[256,768]{1,0:T(8,128)(2,1)S(1)}, u32[]{:S(2)}, u32[]{:S(2)}) collective-permute-start(bf16[256,768]{1,0:T(8,128)(2,1)S(1)} %get-tuple-element.57.refs_4_), channel_id=1, source_target_pairs={{0,32},{16,48},{32,64},{48,80},{64,96},{80,112},{96,0},{112,16},{1... | collective-permute-start | bytes 1179656 | tf_op jit(solution)/shard_map/ppermute | solution.py:464
  193.6 25.0 %collective-permute-start.12 = (bf16[256,768]{1,0:T(8,128)(2,1)S(1)}, bf16[256,768]{1,0:T(8,128)(2,1)S(1)}, u32[]{:S(2)}, u32[]{:S(2)}) collective-permute-start(bf16[256,768]{1,0:T(8,128)(2,1)S(1)} %get-tuple-element.58.refs_5_), channel_id=1, source_target_pairs={{0,96},{16,112},{32,0},{48,16},{64,32},{80,48},{96,64},{112,80},{1... | collective-permute-start | bytes 1179656 | tf_op jit(solution)/shard_map/ppermute | solution.py:464
  211.3 14.7 %collective-permute-start.13 = (bf16[256,768]{1,0:T(8,128)(2,1)}, bf16[256,768]{1,0:T(8,128)(2,1)S(1)}, u32[]{:S(2)}, u32[]{:S(2)}) collective-permute-start(bf16[256,768]{1,0:T(8,128)(2,1)} %get-tuple-element.59.refs_2_), channel_id=1, source_target_pairs={{0,32},{16,48},{32,64},{48,80},{64,96},{80,112},{96,0},{112,16},{1... | collective-permute-start | bytes 1179656 | tf_op jit(solution)/shard_map/ppermute | solution.py:464
  211.3 14.7 %collective-permute-start.14 = (bf16[256,768]{1,0:T(8,128)(2,1)}, bf16[256,768]{1,0:T(8,128)(2,1)}, u32[]{:S(2)}, u32[]{:S(2)}) collective-permute-start(bf16[256,768]{1,0:T(8,128)(2,1)} %get-tuple-element.60.refs_3_), channel_id=1, source_target_pairs={{0,96},{16,112},{32,0},{48,16},{64,32},{80,48},{96,64},{112,80},{1... | collective-permute-start | bytes 1179656 | tf_op jit(solution)/shard_map/ppermute | solution.py:464

commit v5 on v4

--- a/solution.py
+++ b/solution.py
@@ -256,7 +256,7 @@
     )(in_hbm(buf), in_vmem(w_down), for_gate, for_up, *after)
 
 
-def weight_part(kind, buf, base, width, other, place, own, received=None, after=(), micros=LONG):
+def weight_part(kind, buf, base, width, other, place, own, received=None, after=(), micros=LONG, stay=2):
     rows = buf.shape[0]
     units = other.shape[1]
     shape = (width, units) if kind == "rows" else (units, width)
@@ -278,13 +278,13 @@
 
         @pl.when(j == 0)
         def _():
-            fwd_ref[0] = low
-            bwd_ref[0] = high
+            fwd_ref[...] = low
+            bwd_ref[...] = high
 
         @pl.when(j == 1)
         def _():
             keep1_ref[...] = low
-            fwd_ref[1] = high
+            fwd_ref[...] = high
 
         @pl.when(j == 2)
         def _():
@@ -292,7 +292,7 @@
 
         @pl.when(j == 3)
         def _():
-            bwd_ref[1] = low
+            bwd_ref[...] = low
             keep3_ref[...] = high
 
     def column(j, at):
@@ -313,8 +313,11 @@
         ins.append(pl.BlockSpec((None,) + shape, lambda j, at: (j, 0, 0)))
         shapes = [(2, half, shape[1])] * 2 + [(half, shape[1])] * 2 + [shape]
         outs = [pl.BlockSpec(s, lambda j, at, n=len(s): (0,) * n) for s in shapes]
-        out_shape = [jax.ShapeDtypeStruct(s, flat) for s in shapes[:2]]
-        out_shape += [pltpu.HBM(s, flat) for s in shapes[2:]]
+        pair = (None,) + shapes[0][1:]
+        outs[0] = pl.BlockSpec(pair, lambda j, at: (jnp.minimum(j, 1), 0, 0))
+        outs[1] = pl.BlockSpec(pair, lambda j, at: (j // 3, 0, 0))
+        out_shape = [jax.ShapeDtypeStruct(s, flat) for s in shapes[:stay]]
+        out_shape += [pltpu.HBM(s, flat) for s in shapes[stay:]]
         args = (in_hbm(buf), other, received)
     ins += [ANY] * len(after)
     body = plain if received is None else summed
@@ -333,7 +336,7 @@
 def input_rows(d_gate, d_up, w_gate, w_up, after=(), micros=LONG):
     rows, units = d_gate.shape
     width = w_gate.shape[1]
-    block = 512
+    block = 1024
 
     def body(dg_ref, du_ref, wg_ref, wu_ref, out_ref):
         total = dot_nt(dg_ref[...], wg_ref[...]) + dot_nt(du_ref[...], wu_ref[...])
@@ -347,13 +350,13 @@
         in_specs=[whole, whole, weight, weight] + [ANY] * len(after),
         out_specs=pl.BlockSpec((rows, block), lambda j: (0, j)),
         out_shape=pltpu.HBM((rows, width), jnp.bfloat16),
-        compiler_params=params(16),
+        compiler_params=params(24),
         cost_estimate=takes(micros),
         name="input_rows",
     )(d_gate, d_up, in_vmem(w_gate), in_vmem(w_up), *after)
 
 
-def passed_on(parts, hop, after=(), micros=LONG):
+def passed_on(parts, hop, after=(), micros=LONG, where=in_hbm):
     half, width = parts[2].shape
 
     def body(up_ref, down_ref, low_ref, high_ref, fwd_ref, bwd_ref):
@@ -374,7 +377,7 @@
         compiler_params=params(8),
         cost_estimate=takes(micros),
         name="passed_on",
-    )(in_hbm(parts[2]), in_hbm(parts[3]), *hop, *after)
+    )(where(parts[2]), where(parts[3]), *hop, *after)
 
 
 def finished(parts, hop, last, after=(), micros=LONG):
@@ -451,9 +454,6 @@
         out = lax.all_to_all(blocks, "expert", split_axis=0, concat_axis=0, tiled=True)
         return out.reshape(buf.shape)
 
-    def corner(value):
-        return value[:16, :128] * 2
-
     def named(parts):
         return (*parts[:2], *[in_hbm(value) for value in parts[2:]])
 
@@ -481,7 +481,7 @@
     )
     back = exchange(rows_back)
     next_down = passed_on(
-        own_down, hop_down, after=(corner(rows_back),), micros=MICROS["nD"]
+        own_down, hop_down, after=(in_hbm(rows_back),), micros=MICROS["nD"]
     )
     last_down = one_hop(*next_down)
     own_gate = weight_part(
@@ -492,12 +492,14 @@
     hop_gate = one_hop(*own_gate[:2])
     grad_down = finished(own_down, hop_down, last_down, after=(other_up,), micros=MICROS["fD"])
     own_up = weight_part(
-        *up, place, True, swapped(other_up), after=(in_hbm(grad_down),), micros=MICROS["wU"]
+        *up, place, True, swapped(other_up), after=(in_hbm(grad_down),), micros=MICROS["wU"], stay=4
     )
     hop_up = one_hop(*own_up[:2])
     next_gate = passed_on(own_gate, hop_gate, after=own_up[:2], micros=MICROS["nG"])
     last_gate = one_hop(*next_gate)
-    next_up = passed_on(own_up, hop_up, after=next_gate, micros=MICROS["nU"])
+    next_up = passed_on(
+        own_up, hop_up, after=next_gate, micros=MICROS["nU"], where=lambda value: value
+    )
     last_up = one_hop(*next_up)
     grad_tokens = combine(select, back, after=next_up)
     grad_gate = finished(own_gate, hop_gate, last_gate, after=(in_hbm(grad_tokens),), micros=MICROS["fG"])

time: 230 us -> 229 us (level)
  transfers between devices with their start and end apart: 16 -> 16, of which waited for: 3 -> 4; matrix products, arithmetic and copies ran while one was open for 0% -> 0% of each run, Pallas kernels for 23% -> 22%
where the time goes in v5:
time: 229 us; the launch traced here: 227 us
  blocking collectives  102 us (45%)
  Pallas kernels  76.4 us (33%)
  starting transfers between devices  25.1 us (11%)
  waiting for transfers between devices  22.7 us (10%)
    all_to_all x1, blocking collectives, exchange(): lax.all_to_all(blocks, 'expert', split_axis=0, concat_axis=0, tiled=True)  102 us
    pallas_call x5, Pallas kernels, weight_part(): pl.pallas_call(ordered(body, 1 + len(args), len(after)), grid_spec=pltpu....  26.9 us
    ppermute x12, waiting for transfers between devices, one_hop(): return (lax.ppermute(fwd, 'dp', ahead), lax.ppermute(bwd, 'dp', behind))  19.1 us
    ppermute x12, starting transfers between devices, one_hop(): return (lax.ppermute(fwd, 'dp', ahead), lax.ppermute(bwd, 'dp', behind))  16 us
    pallas_call x1, Pallas kernels, forward(): pl.pallas_call(body, grid_spec=pltpu.PrefetchScalarGridSpec(num_scalar_pr...  12.5 us
    pallas_call x1, Pallas kernels, input_rows(): pl.pallas_call(ordered(body, 4, len(after)), grid=(width // block,), in_s...  8.34 us
    pallas_call x3, Pallas kernels, finished(): pl.pallas_call(ordered(body, 5, len(after)), grid=(2,), in_specs=[tile, s...  7.32 us
    pallas_call x1, Pallas kernels, hidden_grad(): pl.pallas_call(ordered(body, 4, len(after)), grid=(steps,), in_specs=[pl....  6.33 us
  transfers between devices with their start and end apart: 16, of which 4 were waited for; matrix products, arithmetic and copies ran while one was open for 0% of the time, Pallas kernels for 22%

profile of v5, /device:TPU:1, one launch (start us, length us, event | category | flops | bytes accessed | tf_op | source)
XLA Modules:
  0.0 227.4 jit_solution(5621612023130801651)
XLA Ops:
  0.6 5.6 %pack.1 = (bf16[512,8192]{1,0:T(8,128)(2,1)S(1)}, bf16[512,128]{1,0:T(8,128)(2,1)S(1)}) custom-call(s32[2,128]{1,0:T(2,128)} %bitcast.24, s32[2,128]{1,0:T(2,128)} %bitcast.25, s32[4,16]{1,0:T(4,128)} %bitcast.23, bf16[128,4096]{1,0:T(8,128)(2,1)} %refs_3_.2, bf16[128,4096]{1,0:T(8,128)(2,1)} %refs_4_.1, s32[1]{0:T(128)} %bitcast.3.refs_5_.place_ref.refs_0_), custom_call_target="tpu_custom_call" | custom-call | flops 11500000256 | bytes 1000000 | tf_op jit(solution)/shard_map/pack/pallas_call | solution.py:120
  6.2 0.0 copy-start.4
  6.2 0.0 copy-start
  6.3 0.0 copy-start.1
  6.3 0.0 slice-start
  6.3 102.4 %all_to_all.10 = bf16[16,32,8192]{2,1,0:T(8,128)(2,1)} all-to-all(bf16[16,32,8192]{2,1,0:T(8,128)(2,1)S(1)} %bitcast.11), channel_id=1, replica_groups=mesh['dp'=8,'expert'=16] {'expert'}, dimensions={0} | all-to-all | bytes 16777216 | tf_op jit(solution)/shard_map/all_to_all | solution.py:454
  108.7 0.0 copy-done.4
  108.7 0.0 copy-done
  108.7 0.0 copy-done.1
  108.7 0.0 slice-start.1
  108.7 12.5 %forward.1 = (bf16[512,768]{1,0:T(8,128)(2,1)S(1)}, f32[512,768]{1,0:T(8,128)S(1)}, f32[512,768]{1,0:T(8,128)S(1)}, bf16[4,768,512]{2,1,0:T(8,128)(2,1)S(1)}) custom-call(s32[1]{0:T(128)} %bitcast.3.refs_5_.place_ref.refs_0_, bf16[512,8192]{1,0:T(8,128)(2,1)} %bitcast.14, bf16[512,8192]{1,0:T(8,128)(2,1)} %bitcast.15, bf16[1,4096,768]{2,1,0:T(8,128)(2,1)S(1)} %copy-done, ...), custom_call_target="tpu_custom_call" | custom-call | flops 11500000256 | bytes 1000000 | tf_op jit(solution)/shard_map/forward/pallas_call | solution.py:185
  121.2 2.7 %collective-permute-start = (bf16[4,768,512]{2,1,0:T(8,128)(2,1)S(1)}, bf16[4,768,512]{2,1,0:T(8,128)(2,1)S(1)}, u32[]{:S(2)}, u32[]{:S(2)}) collective-permute-start(bf16[4,768,512]{2,1,0:T(8,128)(2,1)S(1)} %get-tuple-element.37.refs_4_), channel_id=1, source_target_pairs={{0,16},{16,0},{32,48},{48,32},{64,80},{80,64},{96,112},{112,96},{1... | collective-permute-start | bytes 9437192 | tf_op jit(solution)/shard_map/ppermute | solution.py:461
  123.9 0.0 slice-done
  123.9 0.0 slice-done.1
  123.9 6.3 %hidden_grad.1 = (bf16[512,768]{1,0:T(8,128)(2,1)S(1)}, bf16[512,768]{1,0:T(8,128)(2,1)S(1)}) custom-call(bf16[512,8192]{1,0:T(8,128)(2,1)} %bitcast.16, bf16[1,768,4096]{2,1,0:T(8,128)(2,1)S(1)} %bitcast.13, f32[512,768]{1,0:T(8,128)S(1)} %get-tuple-element.35.refs_2_, f32[512,768]{1,0:T(8,128)S(1)} %get-tuple-element.36.refs_3_, ...), custom_call_target="tpu_custom_call" | custom-call | flops 5750000128 | bytes 1000000 | tf_op jit(solution)/shard_map/hidden_grad/pallas_call | solution.py:240
  130.2 0.0 copy-start.2
  130.3 0.0 collective-permute-done.refs_3_
  130.3 6.1 %weight_part.5 = (bf16[2,384,512]{2,1,0:T(8,128)(2,1)}, bf16[2,384,512]{2,1,0:T(8,128)(2,1)}, bf16[384,512]{1,0:T(8,128)(2,1)}, bf16[384,512]{1,0:T(8,128)(2,1)}, bf16[768,512]{1,0:T(8,128)(2,1)}) custom-call(s32[1]{0:T(128)} %bitcast.3.refs_5_.place_ref.refs_0_, bf16[512,8192]{1,0:T(8,128)(2,1)} %bitcast.17, ...), custom_call_target="tpu_custom_call" | custom-call | flops 5750000128 | bytes 1000000 | tf_op jit(solution)/shard_map/weight_part/pallas_call | solution.py:324
  136.3 1.7 collective-permute-start.2
  138.0 2.1 collective-permute-start.3
  140.1 5.2 %weight_part.6.refs_4_ = bf16[4,512,768]{2,1,0:T(8,128)(2,1)} custom-call(s32[1]{0:T(128)} %bitcast.3.refs_5_.place_ref.refs_0_, bf16[512,8192]{1,0:T(8,128)(2,1)} %bitcast.18, bf16[512,768]{1,0:T(8,128)(2,1)S(1)} %get-tuple-element.38.refs_4_.refs_2_.refs_0_, bf16[2,384,512]{2,1,0:T(8,128)(2,1)} %get-tuple-element.41.refs_3_, ...), custom_call_target="tpu_custom_call" | custom-call | flops 115000000512 | bytes 1000000 | tf_op jit(solution)/shard_map/weight_part/pallas_call | solution.py:324
  145.3 0.3 collective-permute-start.1
  145.7 0.0 copy-done.2
  145.7 8.3 %input_rows.1.refs_4_ = bf16[512,4096]{1,0:T(8,128)(2,1)} custom-call(bf16[512,768]{1,0:T(8,128)(2,1)S(1)} %get-tuple-element.38.refs_4_.refs_2_.refs_0_, bf16[512,768]{1,0:T(8,128)(2,1)S(1)} %get-tuple-element.39.refs_1_.refs_2_, bf16[1,4096,768]{2,1,0:T(8,128)(2,1)S(1)} %copy-done, bf16[1,4096,768]{2,1,0:T(8,128)(2,1)S(1)} %copy-done.1, ...), custom_call_target="tpu_custom_call" | custom-call | flops 115000000512 | bytes 1000000 | tf_op jit(solution)/shard_map/input_rows/pallas_call | solution.py:347
  154.0 4.6 %all-to-all-start.1 = ((bf16[16,32,4096]{2,1,0:T(8,128)(2,1)}), bf16[16,32,4096]{2,1,0:T(8,128)(2,1)}, u32[]{:S(2)}, u32[]{:S(2)}) async-start(bf16[16,32,4096]{2,1,0:T(8,128)(2,1)} %bitcast.22), calls=%async_computation.1 | async-start | bytes 8388608 | tf_op jit(solution)/shard_map/all_to_all | solution.py:454
  158.6 0.0 collective-permute-done.2.refs_2_
  158.6 0.0 collective-permute-done.3.refs_3_.refs_1_
  158.6 2.3 %passed_on.3 = (bf16[384,512]{1,0:T(8,128)(2,1)}, bf16[384,512]{1,0:T(8,128)(2,1)}) custom-call(bf16[384,512]{1,0:T(8,128)(2,1)} %get-tuple-element.43.refs_5_.refs_0_, bf16[384,512]{1,0:T(8,128)(2,1)} %get-tuple-element.44.refs_6_.refs_1_, bf16[2,384,512]{2,1,0:T(8,128)(2,1)} %collective-permute-done.2.refs_2_, ...), custom_call_target="tpu_custom_call" | custom-call | flops 115000000512 | bytes 1000000 | tf_op jit(solution)/shard_map/passed_on/pallas_call | solution.py:371
  160.9 0.1 collective-permute-start.5
  161.0 0.0 copy-start.3
  161.0 2.5 %collective-permute-start.6 = (bf16[384,512]{1,0:T(8,128)(2,1)}, bf16[384,512]{1,0:T(8,128)(2,1)}, u32[]{:S(2)}, u32[]{:S(2)}) collective-permute-start(bf16[384,512]{1,0:T(8,128)(2,1)} %get-tuple-element.47.refs_5_), channel_id=1, source_target_pairs={{0,96},{16,112},{32,0},{48,16},{64,32},{80,48},{96,64},{112,80},{1... | collective-permute-start | bytes 1179656 | tf_op jit(solution)/shard_map/ppermute | solution.py:464
  163.6 0.0 collective-permute-done.1.refs_3_
  163.6 6.4 %weight_part.7 = (bf16[2,256,768]{2,1,0:T(8,128)(2,1)}, bf16[2,256,768]{2,1,0:T(8,128)(2,1)}, bf16[256,768]{1,0:T(8,128)(2,1)}, bf16[256,768]{1,0:T(8,128)(2,1)}, bf16[512,768]{1,0:T(8,128)(2,1)}) custom-call(s32[1]{0:T(128)} %bitcast.3.refs_5_.place_ref.refs_0_, bf16[512,8192]{1,0:T(8,128)(2,1)} %bitcast.19, ...), custom_call_target="tpu_custom_call" | custom-call | flops 115000000512 | bytes 1000000 | tf_op jit(solution)/shard_map/weight_part/pallas_call | solution.py:324
  169.9 0.9 collective-permute-start.10
  170.9 0.5 collective-permute-start.9
  171.4 0.0 copy-done.3
  171.4 4.1 %weight_part.8.refs_5_ = bf16[4,512,768]{2,1,0:T(8,128)(2,1)S(1)} custom-call(s32[1]{0:T(128)} %bitcast.3.refs_5_.place_ref.refs_0_, bf16[512,8192]{1,0:T(8,128)(2,1)} %bitcast.20, bf16[512,768]{1,0:T(8,128)(2,1)S(1)} %copy-done.3, bf16[2,256,768]{2,1,0:T(8,128)(2,1)} %get-tuple-element.48.refs_3_, bf16[2,256,768]{2,1,0:T(8,128)(2,1)} %get-tuple-element.49.refs_4_, ...), custom_call_target="tpu_custom_call" | custom-call | flops 115000000512 | bytes 1000000 | tf_op jit(solution)/shard_map/weight_part/pallas_call | solution.py:324
  175.5 1.5 collective-permute-start.4
  177.0 0.0 collective-permute-done.5.refs_3_
  177.0 0.0 collective-permute-done.6.refs_4_
  177.0 2.6 %finished.3.refs_4_ = bf16[768,512]{1,0:T(8,128)(2,1)} custom-call(bf16[768,512]{1,0:T(8,128)(2,1)} %get-tuple-element.45.refs_7_.refs_0_, bf16[2,384,512]{2,1,0:T(8,128)(2,1)} %collective-permute-done.3.refs_3_.refs_1_, bf16[2,384,512]{2,1,0:T(8,128)(2,1)} %collective-permute-done.2.refs_2_, bf16[384,512]{1,0:T(8,128)(2,1)} %collective-permute-done.5.refs_3_, ...), custom_call_target="tpu_custom_call" | custom-call | flops 115000000512 | bytes 1000000 | tf_op jit(solution)/shard_map/finished/pallas_call | solution.py:404
  179.7 2.6 %collective-permute-done.4.refs_3_ = bf16[4,512,768]{2,1,0:T(8,128)(2,1)S(1)} collective-permute-done((bf16[4,512,768]{2,1,0:T(8,128)(2,1)S(1)}, bf16[4,512,768]{2,1,0:T(8,128)(2,1)S(1)}, u32[]{:S(2)}, u32[]{:S(2)}) %collective-permute-start.4) | collective-permute-done | bytes 3145760 | tf_op jit(solution)/shard_map/ppermute | solution.py:461
  182.3 5.2 %weight_part.9 = (bf16[2,256,768]{2,1,0:T(8,128)(2,1)S(1)}, bf16[2,256,768]{2,1,0:T(8,128)(2,1)S(1)}, bf16[256,768]{1,0:T(8,128)(2,1)S(1)}, bf16[256,768]{1,0:T(8,128)(2,1)S(1)}, bf16[512,768]{1,0:T(8,128)(2,1)}) custom-call(s32[1]{0:T(128)} %bitcast.3.refs_5_.place_ref.refs_0_, bf16[512,8192]{1,0:T(8,128)(2,1)} %bitcast.21, bf16[512,768]{1,0:T(8,128)(2,1)S(1)} %copy-done.3, ...), custom_call_target="tpu_custom_call" | custom-call | flops 115000000512 | bytes 1000000 | tf_op jit(solution)/shard_map/weight_part/pallas_call | solution.py:324
  187.5 0.0 collective-permute-start.7
  187.5 2.7 %collective-permute-start.8 = (bf16[2,256,768]{2,1,0:T(8,128)(2,1)S(1)}, bf16[2,256,768]{2,1,0:T(8,128)(2,1)S(1)}, u32[]{:S(2)}, u32[]{:S(2)}) collective-permute-start(bf16[2,256,768]{2,1,0:T(8,128)(2,1)S(1)} %get-tuple-element.56.refs_5_), channel_id=1, source_target_pairs={{0,96},{16,112},{32,0},{48,16},{64,32},{80,48},{96,64},{112,80},{1... | collective-permute-start | bytes 2359304 | tf_op jit(solution)/shard_map/ppermute | solution.py:464
  190.2 0.0 collective-permute-done.10.refs_3_.refs_1_
  190.2 0.0 collective-permute-done.9.refs_2_
  190.2 1.6 passed_on.4
  191.8 0.1 collective-permute-start.11
  191.8 2.7 %collective-permute-start.12 = (bf16[256,768]{1,0:T(8,128)(2,1)S(1)}, bf16[256,768]{1,0:T(8,128)(2,1)S(1)}, u32[]{:S(2)}, u32[]{:S(2)}) collective-permute-start(bf16[256,768]{1,0:T(8,128)(2,1)S(1)} %get-tuple-element.58.refs_5_), channel_id=1, source_target_pairs={{0,96},{16,112},{32,0},{48,16},{64,32},{80,48},{96,64},{112,80},{1... | collective-permute-start | bytes 1179656 | tf_op jit(solution)/shard_map/ppermute | solution.py:464
  194.5 13.9 %collective-permute-done.7.refs_2_ = bf16[2,256,768]{2,1,0:T(8,128)(2,1)S(1)} collective-permute-done((bf16[2,256,768]{2,1,0:T(8,128)(2,1)S(1)}, bf16[2,256,768]{2,1,0:T(8,128)(2,1)S(1)}, u32[]{:S(2)}, u32[]{:S(2)}) %collective-permute-start.7) | collective-permute-done | bytes 786464 | tf_op jit(solution)/shard_map/ppermute | solution.py:464
  208.4 0.0 collective-permute-done.8.refs_3_.refs_1_
  208.4 0.9 passed_on.5
  209.3 0.0 collective-permute-start.13
  209.3 2.7 %collective-permute-start.14 = (bf16[256,768]{1,0:T(8,128)(2,1)}, bf16[256,768]{1,0:T(8,128)(2,1)}, u32[]{:S(2)}, u32[]{:S(2)}) collective-permute-start(bf16[256,768]{1,0:T(8,128)(2,1)} %get-tuple-element.60.refs_3_), channel_id=1, source_target_pairs={{0,96},{16,112},{32,0},{48,16},{64,32},{80,48},{96,64},{112,80},{1... | collective-permute-start | bytes 1179656 | tf_op jit(solution)/shard_map/ppermute | solution.py:464
  212.0 1.0 all-to-all-done.1
  213.0 4.6 %combine.1.refs_5_ = bf16[128,4096]{1,0:T(8,128)(2,1)} custom-call(bf16[512,128]{1,0:T(8,128)(2,1)} %copy-done.4, bf16[512,4096]{1,0:T(8,128)(2,1)} %bitcast.7.refs_1_, bf16[256,768]{1,0:T(8,128)(2,1)} %get-tuple-element.59.refs_2_, bf16[256,768]{1,0:T(8,128)(2,1)} %get-tuple-element.60.refs_3_), custom_call_target="tpu_custom_call" | custom-call | flops 5750000128 | bytes 1000000 | tf_op jit(solution)/shard_map/combine/pallas_call | solution.py:424
  217.6 0.0 collective-permute-done.11.refs_3_
  217.6 0.0 collective-permute-done.12.refs_4_
  217.6 2.4 %finished.4.refs_5_ = bf16[512,768]{1,0:T(8,128)(2,1)} custom-call(bf16[512,768]{1,0:T(8,128)(2,1)} %get-tuple-element.52.refs_7_.refs_0_, bf16[2,256,768]{2,1,0:T(8,128)(2,1)} %collective-permute-done.10.refs_3_.refs_1_, bf16[2,256,768]{2,1,0:T(8,128)(2,1)} %collective-permute-done.9.refs_2_, bf16[256,768]{1,0:T(8,128)(2,1)S(1)} %collective-permute-done.11.refs_3_, ...), custom_call_target="tpu_custom_call" | custom-call | flops 115000000512 | bytes 1000000 | tf_op jit(solution)/shard_map/finished/pallas_call | solution.py:404
  220.0 5.1 %collective-permute-done.13.refs_3_ = bf16[256,768]{1,0:T(8,128)(2,1)S(1)} collective-permute-done((bf16[256,768]{1,0:T(8,128)(2,1)}, bf16[256,768]{1,0:T(8,128)(2,1)S(1)}, u32[]{:S(2)}, u32[]{:S(2)}) %collective-permute-start.13) | collective-permute-done | bytes 393248 | tf_op jit(solution)/shard_map/ppermute | solution.py:464
  225.2 0.0 collective-permute-done.14.refs_4_
  225.2 2.3 finished.5
  (1 shorter events, 0.0 us)
Async XLA Ops:
  6.2 102.5 %copy-start.4 = (bf16[512,128]{1,0:T(8,128)(2,1)}, bf16[512,128]{1,0:T(8,128)(2,1)S(1)}, u32[]{:S(2)}) copy-start(bf16[512,128]{1,0:T(8,128)(2,1)S(1)} %get-tuple-element.33.refs_0_) | copy-start | bytes 393220
  6.2 102.5 %copy-start = (bf16[1,4096,768]{2,1,0:T(8,128)(2,1)S(1)}, bf16[1,4096,768]{2,1,0:T(8,128)(2,1)}, u32[]{:S(2)}) copy-start(bf16[1,4096,768]{2,1,0:T(8,128)(2,1)} %refs_2_.1) | copy-start | bytes 18874372
  6.3 102.5 %copy-start.1 = (bf16[1,4096,768]{2,1,0:T(8,128)(2,1)S(1)}, bf16[1,4096,768]{2,1,0:T(8,128)(2,1)}, u32[]{:S(2)}) copy-start(bf16[1,4096,768]{2,1,0:T(8,128)(2,1)} %refs_3_.3) | copy-start | bytes 18874372
  6.3 117.6 %slice-start = ((s8[6291456]{0:T(1024)(128)(4,1)}), s8[4194304]{0:T(1024)(128)(4,1)S(1)}, s32[]{:S(2)}) async-start(s8[6291456]{0:T(1024)(128)(4,1)} %bitcast.12), calls=%async_computation.2 | async-start | bytes 8388608
  108.7 15.2 %slice-start.1 = ((s8[6291456]{0:T(1024)(128)(4,1)}), s8[2097152]{0:T(1024)(128)(4,1)S(1)}, s32[]{:S(2)}) async-start(s8[6291456]{0:T(1024)(128)(4,1)} %bitcast.12), calls=%async_computation.3 | async-start | bytes 4194304
  121.2 9.0 %collective-permute-start = (bf16[4,768,512]{2,1,0:T(8,128)(2,1)S(1)}, bf16[4,768,512]{2,1,0:T(8,128)(2,1)S(1)}, u32[]{:S(2)}, u32[]{:S(2)}) collective-permute-start(bf16[4,768,512]{2,1,0:T(8,128)(2,1)S(1)} %get-tuple-element.37.refs_4_), channel_id=1, source_target_pairs={{0,16},{16,0},{32,48},{48,32},{64,80},{80,64},{96,112},{112,96},{1... | collective-permute-start | bytes 9437192 | tf_op jit(solution)/shard_map/ppermute | solution.py:461
  130.2 15.4 %copy-start.2 = (bf16[512,768]{1,0:T(8,128)(2,1)}, bf16[512,768]{1,0:T(8,128)(2,1)S(1)}, u32[]{:S(2)}) copy-start(bf16[512,768]{1,0:T(8,128)(2,1)S(1)} %get-tuple-element.39.refs_1_.refs_2_) | copy-start | bytes 2359300
  136.3 22.2 %collective-permute-start.2 = (bf16[2,384,512]{2,1,0:T(8,128)(2,1)}, bf16[2,384,512]{2,1,0:T(8,128)(2,1)}, u32[]{:S(2)}, u32[]{:S(2)}) collective-permute-start(bf16[2,384,512]{2,1,0:T(8,128)(2,1)} %get-tuple-element.41.refs_3_), channel_id=1, source_target_pairs={{0,32},{16,48},{32,64},{48,80},{64,96},{80,112},{96,0},{112,16},{1... | collective-permute-start | bytes 2359304 | tf_op jit(solution)/shard_map/ppermute | solution.py:464
  138.0 20.6 %collective-permute-start.3 = (bf16[2,384,512]{2,1,0:T(8,128)(2,1)}, bf16[2,384,512]{2,1,0:T(8,128)(2,1)}, u32[]{:S(2)}, u32[]{:S(2)}) collective-permute-start(bf16[2,384,512]{2,1,0:T(8,128)(2,1)} %get-tuple-element.42.refs_4_), channel_id=1, source_target_pairs={{0,96},{16,112},{32,0},{48,16},{64,32},{80,48},{96,64},{112,80},{1... | collective-permute-start | bytes 2359304 | tf_op jit(solution)/shard_map/ppermute | solution.py:464
  145.3 18.3 %collective-permute-start.1 = (bf16[4,512,768]{2,1,0:T(8,128)(2,1)}, bf16[4,512,768]{2,1,0:T(8,128)(2,1)}, u32[]{:S(2)}, u32[]{:S(2)}) collective-permute-start(bf16[4,512,768]{2,1,0:T(8,128)(2,1)} %weight_part.6.refs_4_), channel_id=1, source_target_pairs={{0,16},{16,0},{32,48},{48,32},{64,80},{80,64},{96,112},{112,96},{1... | collective-permute-start | bytes 9437192 | tf_op jit(solution)/shard_map/ppermute | solution.py:461
  154.0 59.0 %all-to-all-start.1 = ((bf16[16,32,4096]{2,1,0:T(8,128)(2,1)}), bf16[16,32,4096]{2,1,0:T(8,128)(2,1)}, u32[]{:S(2)}, u32[]{:S(2)}) async-start(bf16[16,32,4096]{2,1,0:T(8,128)(2,1)} %bitcast.22), calls=%async_computation.1 | async-start | bytes 8388608 | tf_op jit(solution)/shard_map/all_to_all | solution.py:454
  160.9 16.1 %collective-permute-start.5 = (bf16[384,512]{1,0:T(8,128)(2,1)}, bf16[384,512]{1,0:T(8,128)(2,1)}, u32[]{:S(2)}, u32[]{:S(2)}) collective-permute-start(bf16[384,512]{1,0:T(8,128)(2,1)} %get-tuple-element.46.refs_4_), channel_id=1, source_target_pairs={{0,32},{16,48},{32,64},{48,80},{64,96},{80,112},{96,0},{112,16},{1... | collective-permute-start | bytes 1179656 | tf_op jit(solution)/shard_map/ppermute | solution.py:464
  161.0 10.4 %copy-start.3 = (bf16[512,768]{1,0:T(8,128)(2,1)S(1)}, bf16[512,768]{1,0:T(8,128)(2,1)}, u32[]{:S(2)}) copy-start(bf16[512,768]{1,0:T(8,128)(2,1)} %copy-done.2) | copy-start | bytes 2359300
  161.0 16.0 %collective-permute-start.6 = (bf16[384,512]{1,0:T(8,128)(2,1)}, bf16[384,512]{1,0:T(8,128)(2,1)}, u32[]{:S(2)}, u32[]{:S(2)}) collective-permute-start(bf16[384,512]{1,0:T(8,128)(2,1)} %get-tuple-element.47.refs_5_), channel_id=1, source_target_pairs={{0,96},{16,112},{32,0},{48,16},{64,32},{80,48},{96,64},{112,80},{1... | collective-permute-start | bytes 1179656 | tf_op jit(solution)/shard_map/ppermute | solution.py:464
  169.9 20.2 %collective-permute-start.10 = (bf16[2,256,768]{2,1,0:T(8,128)(2,1)}, bf16[2,256,768]{2,1,0:T(8,128)(2,1)}, u32[]{:S(2)}, u32[]{:S(2)}) collective-permute-start(bf16[2,256,768]{2,1,0:T(8,128)(2,1)} %get-tuple-element.49.refs_4_), channel_id=1, source_target_pairs={{0,96},{16,112},{32,0},{48,16},{64,32},{80,48},{96,64},{112,80},{1... | collective-permute-start | bytes 2359304 | tf_op jit(solution)/shard_map/ppermute | solution.py:464
  170.9 19.3 %collective-permute-start.9 = (bf16[2,256,768]{2,1,0:T(8,128)(2,1)}, bf16[2,256,768]{2,1,0:T(8,128)(2,1)}, u32[]{:S(2)}, u32[]{:S(2)}) collective-permute-start(bf16[2,256,768]{2,1,0:T(8,128)(2,1)} %get-tuple-element.48.refs_3_), channel_id=1, source_target_pairs={{0,32},{16,48},{32,64},{48,80},{64,96},{80,112},{96,0},{112,16},{1... | collective-permute-start | bytes 2359304 | tf_op jit(solution)/shard_map/ppermute | solution.py:464
  175.5 6.8 %collective-permute-start.4 = (bf16[4,512,768]{2,1,0:T(8,128)(2,1)S(1)}, bf16[4,512,768]{2,1,0:T(8,128)(2,1)S(1)}, u32[]{:S(2)}, u32[]{:S(2)}) collective-permute-start(bf16[4,512,768]{2,1,0:T(8,128)(2,1)S(1)} %weight_part.8.refs_5_), channel_id=1, source_target_pairs={{0,16},{16,0},{32,48},{48,32},{64,80},{80,64},{96,112},{112,96},{1... | collective-permute-start | bytes 9437192 | tf_op jit(solution)/shard_map/ppermute | solution.py:461
  187.5 20.9 %collective-permute-start.7 = (bf16[2,256,768]{2,1,0:T(8,128)(2,1)S(1)}, bf16[2,256,768]{2,1,0:T(8,128)(2,1)S(1)}, u32[]{:S(2)}, u32[]{:S(2)}) collective-permute-start(bf16[2,256,768]{2,1,0:T(8,128)(2,1)S(1)} %get-tuple-element.55.refs_4_), channel_id=1, source_target_pairs={{0,32},{16,48},{32,64},{48,80},{64,96},{80,112},{96,0},{112,16},{1... | collective-permute-start | bytes 2359304 | tf_op jit(solution)/shard_map/ppermute | solution.py:464
  187.5 20.9 %collective-permute-start.8 = (bf16[2,256,768]{2,1,0:T(8,128)(2,1)S(1)}, bf16[2,256,768]{2,1,0:T(8,128)(2,1)S(1)}, u32[]{:S(2)}, u32[]{:S(2)}) collective-permute-start(bf16[2,256,768]{2,1,0:T(8,128)(2,1)S(1)} %get-tuple-element.56.refs_5_), channel_id=1, source_target_pairs={{0,96},{16,112},{32,0},{48,16},{64,32},{80,48},{96,64},{112,80},{1... | collective-permute-start | bytes 2359304 | tf_op jit(solution)/shard_map/ppermute | solution.py:464
  191.8 25.9 %collective-permute-start.11 = (bf16[256,768]{1,0:T(8,128)(2,1)S(1)}, bf16[256,768]{1,0:T(8,128)(2,1)S(1)}, u32[]{:S(2)}, u32[]{:S(2)}) collective-permute-start(bf16[256,768]{1,0:T(8,128)(2,1)S(1)} %get-tuple-element.57.refs_4_), channel_id=1, source_target_pairs={{0,32},{16,48},{32,64},{48,80},{64,96},{80,112},{96,0},{112,16},{1... | collective-permute-start | bytes 1179656 | tf_op jit(solution)/shard_map/ppermute | solution.py:464
  191.8 25.8 %collective-permute-start.12 = (bf16[256,768]{1,0:T(8,128)(2,1)S(1)}, bf16[256,768]{1,0:T(8,128)(2,1)S(1)}, u32[]{:S(2)}, u32[]{:S(2)}) collective-permute-start(bf16[256,768]{1,0:T(8,128)(2,1)S(1)} %get-tuple-element.58.refs_5_), channel_id=1, source_target_pairs={{0,96},{16,112},{32,0},{48,16},{64,32},{80,48},{96,64},{112,80},{1... | collective-permute-start | bytes 1179656 | tf_op jit(solution)/shard_map/ppermute | solution.py:464
  209.3 15.8 %collective-permute-start.13 = (bf16[256,768]{1,0:T(8,128)(2,1)}, bf16[256,768]{1,0:T(8,128)(2,1)S(1)}, u32[]{:S(2)}, u32[]{:S(2)}) collective-permute-start(bf16[256,768]{1,0:T(8,128)(2,1)} %get-tuple-element.59.refs_2_), channel_id=1, source_target_pairs={{0,32},{16,48},{32,64},{48,80},{64,96},{80,112},{96,0},{112,16},{1... | collective-permute-start | bytes 1179656 | tf_op jit(solution)/shard_map/ppermute | solution.py:464
  209.3 15.8 %collective-permute-start.14 = (bf16[256,768]{1,0:T(8,128)(2,1)}, bf16[256,768]{1,0:T(8,128)(2,1)}, u32[]{:S(2)}, u32[]{:S(2)}) collective-permute-start(bf16[256,768]{1,0:T(8,128)(2,1)} %get-tuple-element.60.refs_3_), channel_id=1, source_target_pairs={{0,96},{16,112},{32,0},{48,16},{64,32},{80,48},{96,64},{112,80},{1... | collective-permute-start | bytes 1179656 | tf_op jit(solution)/shard_map/ppermute | solution.py:464

commit v6 on v5

--- a/solution.py
+++ b/solution.py
@@ -416,7 +416,7 @@
 def combine(select, returned, after=()):
     slots, tok = select.shape
     width = returned.shape[1]
-    block = 1024
+    block = 2048
 
     def body(sel_ref, in_ref, out_ref):
         out_ref[...] = dot_tn(sel_ref[...], in_ref[...]).astype(jnp.bfloat16)
@@ -431,7 +431,7 @@
         + [ANY] * len(after),
         out_specs=pl.BlockSpec((tok, block), lambda j: (0, j)),
         out_shape=jax.ShapeDtypeStruct((tok, width), jnp.bfloat16),
-        compiler_params=params(12),
+        compiler_params=params(16),
         cost_estimate=takes(5),
         name="combine",
     )(in_hbm(select), in_hbm(returned), *after)

time: 229 us -> 228 us (level)
  transfers between devices with their start and end apart: 16 -> 16, of which waited for: 4 -> 5; matrix products, arithmetic and copies ran while one was open for 0% -> 0% of each run, Pallas kernels for 22% -> 21%
where the time goes in v6:
time: 228 us; the launch traced here: 227 us
  blocking collectives  102 us (45%)
  Pallas kernels  75.3 us (33%)
  starting transfers between devices  25.1 us (11%)
  waiting for transfers between devices  23.8 us (10%)
    all_to_all x1, blocking collectives, exchange(): lax.all_to_all(blocks, 'expert', split_axis=0, concat_axis=0, tiled=True)  102 us
    pallas_call x5, Pallas kernels, weight_part(): pl.pallas_call(ordered(body, 1 + len(args), len(after)), grid_spec=pltpu....  26.9 us
    ppermute x12, waiting for transfers between devices, one_hop(): return (lax.ppermute(fwd, 'dp', ahead), lax.ppermute(bwd, 'dp', behind))  20.2 us
    ppermute x12, starting transfers between devices, one_hop(): return (lax.ppermute(fwd, 'dp', ahead), lax.ppermute(bwd, 'dp', behind))  16 us
    pallas_call x1, Pallas kernels, forward(): pl.pallas_call(body, grid_spec=pltpu.PrefetchScalarGridSpec(num_scalar_pr...  12.5 us
    pallas_call x1, Pallas kernels, input_rows(): pl.pallas_call(ordered(body, 4, len(after)), grid=(width // block,), in_s...  8.34 us
    pallas_call x3, Pallas kernels, finished(): pl.pallas_call(ordered(body, 5, len(after)), grid=(2,), in_specs=[tile, s...  7.31 us
    pallas_call x1, Pallas kernels, hidden_grad(): pl.pallas_call(ordered(body, 4, len(after)), grid=(steps,), in_specs=[pl....  6.33 us
  transfers between devices with their start and end apart: 16, of which 5 were waited for; matrix products, arithmetic and copies ran while one was open for 0% of the time, Pallas kernels for 21%

profile of v6, /device:TPU:1, one launch (start us, length us, event | category | flops | bytes accessed | tf_op | source)
XLA Modules:
  0.0 227.4 jit_solution(3077335766065299568)
XLA Ops:
  0.6 5.6 %pack.1 = (bf16[512,8192]{1,0:T(8,128)(2,1)S(1)}, bf16[512,128]{1,0:T(8,128)(2,1)S(1)}) custom-call(s32[2,128]{1,0:T(2,128)} %bitcast.24, s32[2,128]{1,0:T(2,128)} %bitcast.25, s32[4,16]{1,0:T(4,128)} %bitcast.23, bf16[128,4096]{1,0:T(8,128)(2,1)} %refs_3_.2, bf16[128,4096]{1,0:T(8,128)(2,1)} %refs_4_.1, s32[1]{0:T(128)} %bitcast.3.refs_5_.place_ref.refs_0_), custom_call_target="tpu_custom_call" | custom-call | flops 11500000256 | bytes 1000000 | tf_op jit(solution)/shard_map/pack/pallas_call | solution.py:120
  6.2 0.0 copy-start.4
  6.2 0.0 copy-start
  6.3 0.0 copy-start.1
  6.3 0.0 slice-start
  6.3 102.4 %all_to_all.10 = bf16[16,32,8192]{2,1,0:T(8,128)(2,1)} all-to-all(bf16[16,32,8192]{2,1,0:T(8,128)(2,1)S(1)} %bitcast.11), channel_id=1, replica_groups=mesh['dp'=8,'expert'=16] {'expert'}, dimensions={0} | all-to-all | bytes 16777216 | tf_op jit(solution)/shard_map/all_to_all | solution.py:454
  108.7 0.0 copy-done.4
  108.7 0.0 copy-done
  108.7 0.0 copy-done.1
  108.7 0.0 slice-start.1
  108.7 12.5 %forward.1 = (bf16[512,768]{1,0:T(8,128)(2,1)S(1)}, f32[512,768]{1,0:T(8,128)S(1)}, f32[512,768]{1,0:T(8,128)S(1)}, bf16[4,768,512]{2,1,0:T(8,128)(2,1)S(1)}) custom-call(s32[1]{0:T(128)} %bitcast.3.refs_5_.place_ref.refs_0_, bf16[512,8192]{1,0:T(8,128)(2,1)} %bitcast.14, bf16[512,8192]{1,0:T(8,128)(2,1)} %bitcast.15, bf16[1,4096,768]{2,1,0:T(8,128)(2,1)S(1)} %copy-done, ...), custom_call_target="tpu_custom_call" | custom-call | flops 11500000256 | bytes 1000000 | tf_op jit(solution)/shard_map/forward/pallas_call | solution.py:185
  121.2 2.7 %collective-permute-start = (bf16[4,768,512]{2,1,0:T(8,128)(2,1)S(1)}, bf16[4,768,512]{2,1,0:T(8,128)(2,1)S(1)}, u32[]{:S(2)}, u32[]{:S(2)}) collective-permute-start(bf16[4,768,512]{2,1,0:T(8,128)(2,1)S(1)} %get-tuple-element.37.refs_4_), channel_id=1, source_target_pairs={{0,16},{16,0},{32,48},{48,32},{64,80},{80,64},{96,112},{112,96},{1... | collective-permute-start | bytes 9437192 | tf_op jit(solution)/shard_map/ppermute | solution.py:461
  123.9 0.0 slice-done
  123.9 0.0 slice-done.1
  123.9 6.3 %hidden_grad.1 = (bf16[512,768]{1,0:T(8,128)(2,1)S(1)}, bf16[512,768]{1,0:T(8,128)(2,1)S(1)}) custom-call(bf16[512,8192]{1,0:T(8,128)(2,1)} %bitcast.16, bf16[1,768,4096]{2,1,0:T(8,128)(2,1)S(1)} %bitcast.13, f32[512,768]{1,0:T(8,128)S(1)} %get-tuple-element.35.refs_2_, f32[512,768]{1,0:T(8,128)S(1)} %get-tuple-element.36.refs_3_, ...), custom_call_target="tpu_custom_call" | custom-call | flops 5750000128 | bytes 1000000 | tf_op jit(solution)/shard_map/hidden_grad/pallas_call | solution.py:240
  130.2 0.0 copy-start.2
  130.3 0.0 collective-permute-done.refs_3_
  130.3 6.1 %weight_part.5 = (bf16[2,384,512]{2,1,0:T(8,128)(2,1)}, bf16[2,384,512]{2,1,0:T(8,128)(2,1)}, bf16[384,512]{1,0:T(8,128)(2,1)}, bf16[384,512]{1,0:T(8,128)(2,1)}, bf16[768,512]{1,0:T(8,128)(2,1)}) custom-call(s32[1]{0:T(128)} %bitcast.3.refs_5_.place_ref.refs_0_, bf16[512,8192]{1,0:T(8,128)(2,1)} %bitcast.17, ...), custom_call_target="tpu_custom_call" | custom-call | flops 5750000128 | bytes 1000000 | tf_op jit(solution)/shard_map/weight_part/pallas_call | solution.py:324
  136.3 1.7 collective-permute-start.2
  138.0 2.1 collective-permute-start.3
  140.1 5.2 %weight_part.6.refs_4_ = bf16[4,512,768]{2,1,0:T(8,128)(2,1)} custom-call(s32[1]{0:T(128)} %bitcast.3.refs_5_.place_ref.refs_0_, bf16[512,8192]{1,0:T(8,128)(2,1)} %bitcast.18, bf16[512,768]{1,0:T(8,128)(2,1)S(1)} %get-tuple-element.38.refs_4_.refs_2_.refs_0_, bf16[2,384,512]{2,1,0:T(8,128)(2,1)} %get-tuple-element.41.refs_3_, ...), custom_call_target="tpu_custom_call" | custom-call | flops 115000000512 | bytes 1000000 | tf_op jit(solution)/shard_map/weight_part/pallas_call | solution.py:324
  145.3 0.3 collective-permute-start.1
  145.7 0.0 copy-done.2
  145.7 8.3 %input_rows.1.refs_4_ = bf16[512,4096]{1,0:T(8,128)(2,1)} custom-call(bf16[512,768]{1,0:T(8,128)(2,1)S(1)} %get-tuple-element.38.refs_4_.refs_2_.refs_0_, bf16[512,768]{1,0:T(8,128)(2,1)S(1)} %get-tuple-element.39.refs_1_.refs_2_, bf16[1,4096,768]{2,1,0:T(8,128)(2,1)S(1)} %copy-done, bf16[1,4096,768]{2,1,0:T(8,128)(2,1)S(1)} %copy-done.1, ...), custom_call_target="tpu_custom_call" | custom-call | flops 115000000512 | bytes 1000000 | tf_op jit(solution)/shard_map/input_rows/pallas_call | solution.py:347
  154.0 4.6 %all-to-all-start.1 = ((bf16[16,32,4096]{2,1,0:T(8,128)(2,1)}), bf16[16,32,4096]{2,1,0:T(8,128)(2,1)}, u32[]{:S(2)}, u32[]{:S(2)}) async-start(bf16[16,32,4096]{2,1,0:T(8,128)(2,1)} %bitcast.22), calls=%async_computation.1 | async-start | bytes 8388608 | tf_op jit(solution)/shard_map/all_to_all | solution.py:454
  158.6 0.0 collective-permute-done.2.refs_2_
  158.6 0.0 collective-permute-done.3.refs_3_.refs_1_
  158.6 2.3 %passed_on.3 = (bf16[384,512]{1,0:T(8,128)(2,1)}, bf16[384,512]{1,0:T(8,128)(2,1)}) custom-call(bf16[384,512]{1,0:T(8,128)(2,1)} %get-tuple-element.43.refs_5_.refs_0_, bf16[384,512]{1,0:T(8,128)(2,1)} %get-tuple-element.44.refs_6_.refs_1_, bf16[2,384,512]{2,1,0:T(8,128)(2,1)} %collective-permute-done.2.refs_2_, ...), custom_call_target="tpu_custom_call" | custom-call | flops 115000000512 | bytes 1000000 | tf_op jit(solution)/shard_map/passed_on/pallas_call | solution.py:371
  160.9 0.1 collective-permute-start.5
  161.0 0.0 copy-start.3
  161.0 2.5 %collective-permute-start.6 = (bf16[384,512]{1,0:T(8,128)(2,1)}, bf16[384,512]{1,0:T(8,128)(2,1)}, u32[]{:S(2)}, u32[]{:S(2)}) collective-permute-start(bf16[384,512]{1,0:T(8,128)(2,1)} %get-tuple-element.47.refs_5_), channel_id=1, source_target_pairs={{0,96},{16,112},{32,0},{48,16},{64,32},{80,48},{96,64},{112,80},{1... | collective-permute-start | bytes 1179656 | tf_op jit(solution)/shard_map/ppermute | solution.py:464
  163.6 0.0 collective-permute-done.1.refs_3_
  163.6 6.4 %weight_part.7 = (bf16[2,256,768]{2,1,0:T(8,128)(2,1)}, bf16[2,256,768]{2,1,0:T(8,128)(2,1)}, bf16[256,768]{1,0:T(8,128)(2,1)}, bf16[256,768]{1,0:T(8,128)(2,1)}, bf16[512,768]{1,0:T(8,128)(2,1)}) custom-call(s32[1]{0:T(128)} %bitcast.3.refs_5_.place_ref.refs_0_, bf16[512,8192]{1,0:T(8,128)(2,1)} %bitcast.19, ...), custom_call_target="tpu_custom_call" | custom-call | flops 115000000512 | bytes 1000000 | tf_op jit(solution)/shard_map/weight_part/pallas_call | solution.py:324
  169.9 0.9 collective-permute-start.10
  170.9 0.5 collective-permute-start.9
  171.4 0.0 copy-done.3
  171.4 4.1 %weight_part.8.refs_5_ = bf16[4,512,768]{2,1,0:T(8,128)(2,1)S(1)} custom-call(s32[1]{0:T(128)} %bitcast.3.refs_5_.place_ref.refs_0_, bf16[512,8192]{1,0:T(8,128)(2,1)} %bitcast.20, bf16[512,768]{1,0:T(8,128)(2,1)S(1)} %copy-done.3, bf16[2,256,768]{2,1,0:T(8,128)(2,1)} %get-tuple-element.48.refs_3_, bf16[2,256,768]{2,1,0:T(8,128)(2,1)} %get-tuple-element.49.refs_4_, ...), custom_call_target="tpu_custom_call" | custom-call | flops 115000000512 | bytes 1000000 | tf_op jit(solution)/shard_map/weight_part/pallas_call | solution.py:324
  175.5 1.5 collective-permute-start.4
  177.0 0.0 collective-permute-done.5.refs_3_
  177.0 0.0 collective-permute-done.6.refs_4_
  177.0 2.6 %finished.3.refs_4_ = bf16[768,512]{1,0:T(8,128)(2,1)} custom-call(bf16[768,512]{1,0:T(8,128)(2,1)} %get-tuple-element.45.refs_7_.refs_0_, bf16[2,384,512]{2,1,0:T(8,128)(2,1)} %collective-permute-done.3.refs_3_.refs_1_, bf16[2,384,512]{2,1,0:T(8,128)(2,1)} %collective-permute-done.2.refs_2_, bf16[384,512]{1,0:T(8,128)(2,1)} %collective-permute-done.5.refs_3_, ...), custom_call_target="tpu_custom_call" | custom-call | flops 115000000512 | bytes 1000000 | tf_op jit(solution)/shard_map/finished/pallas_call | solution.py:404
  179.7 2.6 %collective-permute-done.4.refs_3_ = bf16[4,512,768]{2,1,0:T(8,128)(2,1)S(1)} collective-permute-done((bf16[4,512,768]{2,1,0:T(8,128)(2,1)S(1)}, bf16[4,512,768]{2,1,0:T(8,128)(2,1)S(1)}, u32[]{:S(2)}, u32[]{:S(2)}) %collective-permute-start.4) | collective-permute-done | bytes 3145760 | tf_op jit(solution)/shard_map/ppermute | solution.py:461
  182.3 5.2 %weight_part.9 = (bf16[2,256,768]{2,1,0:T(8,128)(2,1)S(1)}, bf16[2,256,768]{2,1,0:T(8,128)(2,1)S(1)}, bf16[256,768]{1,0:T(8,128)(2,1)S(1)}, bf16[256,768]{1,0:T(8,128)(2,1)S(1)}, bf16[512,768]{1,0:T(8,128)(2,1)}) custom-call(s32[1]{0:T(128)} %bitcast.3.refs_5_.place_ref.refs_0_, bf16[512,8192]{1,0:T(8,128)(2,1)} %bitcast.21, bf16[512,768]{1,0:T(8,128)(2,1)S(1)} %copy-done.3, ...), custom_call_target="tpu_custom_call" | custom-call | flops 115000000512 | bytes 1000000 | tf_op jit(solution)/shard_map/weight_part/pallas_call | solution.py:324
  187.5 0.0 collective-permute-start.7
  187.5 2.7 %collective-permute-start.8 = (bf16[2,256,768]{2,1,0:T(8,128)(2,1)S(1)}, bf16[2,256,768]{2,1,0:T(8,128)(2,1)S(1)}, u32[]{:S(2)}, u32[]{:S(2)}) collective-permute-start(bf16[2,256,768]{2,1,0:T(8,128)(2,1)S(1)} %get-tuple-element.56.refs_5_), channel_id=1, source_target_pairs={{0,96},{16,112},{32,0},{48,16},{64,32},{80,48},{96,64},{112,80},{1... | collective-permute-start | bytes 2359304 | tf_op jit(solution)/shard_map/ppermute | solution.py:464
  190.2 0.0 collective-permute-done.10.refs_3_.refs_1_
  190.2 0.0 collective-permute-done.9.refs_2_
  190.2 1.6 passed_on.4
  191.8 0.1 collective-permute-start.11
  191.8 2.7 %collective-permute-start.12 = (bf16[256,768]{1,0:T(8,128)(2,1)S(1)}, bf16[256,768]{1,0:T(8,128)(2,1)S(1)}, u32[]{:S(2)}, u32[]{:S(2)}) collective-permute-start(bf16[256,768]{1,0:T(8,128)(2,1)S(1)} %get-tuple-element.58.refs_5_), channel_id=1, source_target_pairs={{0,96},{16,112},{32,0},{48,16},{64,32},{80,48},{96,64},{112,80},{1... | collective-permute-start | bytes 1179656 | tf_op jit(solution)/shard_map/ppermute | solution.py:464
  194.5 13.9 %collective-permute-done.7.refs_2_ = bf16[2,256,768]{2,1,0:T(8,128)(2,1)S(1)} collective-permute-done((bf16[2,256,768]{2,1,0:T(8,128)(2,1)S(1)}, bf16[2,256,768]{2,1,0:T(8,128)(2,1)S(1)}, u32[]{:S(2)}, u32[]{:S(2)}) %collective-permute-start.7) | collective-permute-done | bytes 786464 | tf_op jit(solution)/shard_map/ppermute | solution.py:464
  208.4 0.0 collective-permute-done.8.refs_3_.refs_1_
  208.4 0.9 passed_on.5
  209.3 0.0 collective-permute-start.13
  209.3 2.7 %collective-permute-start.14 = (bf16[256,768]{1,0:T(8,128)(2,1)}, bf16[256,768]{1,0:T(8,128)(2,1)}, u32[]{:S(2)}, u32[]{:S(2)}) collective-permute-start(bf16[256,768]{1,0:T(8,128)(2,1)} %get-tuple-element.60.refs_3_), channel_id=1, source_target_pairs={{0,96},{16,112},{32,0},{48,16},{64,32},{80,48},{96,64},{112,80},{1... | collective-permute-start | bytes 1179656 | tf_op jit(solution)/shard_map/ppermute | solution.py:464
  212.0 1.0 all-to-all-done.1
  213.0 3.5 %combine.1.refs_5_ = bf16[128,4096]{1,0:T(8,128)(2,1)} custom-call(bf16[512,128]{1,0:T(8,128)(2,1)} %copy-done.4, bf16[512,4096]{1,0:T(8,128)(2,1)} %bitcast.7.refs_1_, bf16[256,768]{1,0:T(8,128)(2,1)} %get-tuple-element.59.refs_2_, bf16[256,768]{1,0:T(8,128)(2,1)} %get-tuple-element.60.refs_3_), custom_call_target="tpu_custom_call" | custom-call | flops 5750000128 | bytes 1000000 | tf_op jit(solution)/shard_map/combine/pallas_call | solution.py:424
  216.5 0.2 collective-permute-done.11.refs_3_
  216.7 0.0 collective-permute-done.12.refs_4_
  216.7 2.4 %finished.4.refs_5_ = bf16[512,768]{1,0:T(8,128)(2,1)} custom-call(bf16[512,768]{1,0:T(8,128)(2,1)} %get-tuple-element.52.refs_7_.refs_0_, bf16[2,256,768]{2,1,0:T(8,128)(2,1)} %collective-permute-done.10.refs_3_.refs_1_, bf16[2,256,768]{2,1,0:T(8,128)(2,1)} %collective-permute-done.9.refs_2_, bf16[256,768]{1,0:T(8,128)(2,1)S(1)} %collective-permute-done.11.refs_3_, ...), custom_call_target="tpu_custom_call" | custom-call | flops 115000000512 | bytes 1000000 | tf_op jit(solution)/shard_map/finished/pallas_call | solution.py:404
  219.1 6.0 %collective-permute-done.13.refs_3_ = bf16[256,768]{1,0:T(8,128)(2,1)S(1)} collective-permute-done((bf16[256,768]{1,0:T(8,128)(2,1)}, bf16[256,768]{1,0:T(8,128)(2,1)S(1)}, u32[]{:S(2)}, u32[]{:S(2)}) %collective-permute-start.13) | collective-permute-done | bytes 393248 | tf_op jit(solution)/shard_map/ppermute | solution.py:464
  225.2 0.0 collective-permute-done.14.refs_4_
  225.2 2.3 finished.5
  (1 shorter events, 0.0 us)
Async XLA Ops:
  6.2 102.5 %copy-start.4 = (bf16[512,128]{1,0:T(8,128)(2,1)}, bf16[512,128]{1,0:T(8,128)(2,1)S(1)}, u32[]{:S(2)}) copy-start(bf16[512,128]{1,0:T(8,128)(2,1)S(1)} %get-tuple-element.33.refs_0_) | copy-start | bytes 393220
  6.2 102.5 %copy-start = (bf16[1,4096,768]{2,1,0:T(8,128)(2,1)S(1)}, bf16[1,4096,768]{2,1,0:T(8,128)(2,1)}, u32[]{:S(2)}) copy-start(bf16[1,4096,768]{2,1,0:T(8,128)(2,1)} %refs_2_.1) | copy-start | bytes 18874372
  6.3 102.5 %copy-start.1 = (bf16[1,4096,768]{2,1,0:T(8,128)(2,1)S(1)}, bf16[1,4096,768]{2,1,0:T(8,128)(2,1)}, u32[]{:S(2)}) copy-start(bf16[1,4096,768]{2,1,0:T(8,128)(2,1)} %refs_3_.3) | copy-start | bytes 18874372
  6.3 117.6 %slice-start = ((s8[6291456]{0:T(1024)(128)(4,1)}), s8[4194304]{0:T(1024)(128)(4,1)S(1)}, s32[]{:S(2)}) async-start(s8[6291456]{0:T(1024)(128)(4,1)} %bitcast.12), calls=%async_computation.2 | async-start | bytes 8388608
  108.7 15.2 %slice-start.1 = ((s8[6291456]{0:T(1024)(128)(4,1)}), s8[2097152]{0:T(1024)(128)(4,1)S(1)}, s32[]{:S(2)}) async-start(s8[6291456]{0:T(1024)(128)(4,1)} %bitcast.12), calls=%async_computation.3 | async-start | bytes 4194304
  121.2 9.0 %collective-permute-start = (bf16[4,768,512]{2,1,0:T(8,128)(2,1)S(1)}, bf16[4,768,512]{2,1,0:T(8,128)(2,1)S(1)}, u32[]{:S(2)}, u32[]{:S(2)}) collective-permute-start(bf16[4,768,512]{2,1,0:T(8,128)(2,1)S(1)} %get-tuple-element.37.refs_4_), channel_id=1, source_target_pairs={{0,16},{16,0},{32,48},{48,32},{64,80},{80,64},{96,112},{112,96},{1... | collective-permute-start | bytes 9437192 | tf_op jit(solution)/shard_map/ppermute | solution.py:461
  130.2 15.4 %copy-start.2 = (bf16[512,768]{1,0:T(8,128)(2,1)}, bf16[512,768]{1,0:T(8,128)(2,1)S(1)}, u32[]{:S(2)}) copy-start(bf16[512,768]{1,0:T(8,128)(2,1)S(1)} %get-tuple-element.39.refs_1_.refs_2_) | copy-start | bytes 2359300
  136.3 22.2 %collective-permute-start.2 = (bf16[2,384,512]{2,1,0:T(8,128)(2,1)}, bf16[2,384,512]{2,1,0:T(8,128)(2,1)}, u32[]{:S(2)}, u32[]{:S(2)}) collective-permute-start(bf16[2,384,512]{2,1,0:T(8,128)(2,1)} %get-tuple-element.41.refs_3_), channel_id=1, source_target_pairs={{0,32},{16,48},{32,64},{48,80},{64,96},{80,112},{96,0},{112,16},{1... | collective-permute-start | bytes 2359304 | tf_op jit(solution)/shard_map/ppermute | solution.py:464
  138.0 20.6 %collective-permute-start.3 = (bf16[2,384,512]{2,1,0:T(8,128)(2,1)}, bf16[2,384,512]{2,1,0:T(8,128)(2,1)}, u32[]{:S(2)}, u32[]{:S(2)}) collective-permute-start(bf16[2,384,512]{2,1,0:T(8,128)(2,1)} %get-tuple-element.42.refs_4_), channel_id=1, source_target_pairs={{0,96},{16,112},{32,0},{48,16},{64,32},{80,48},{96,64},{112,80},{1... | collective-permute-start | bytes 2359304 | tf_op jit(solution)/shard_map/ppermute | solution.py:464
  145.3 18.3 %collective-permute-start.1 = (bf16[4,512,768]{2,1,0:T(8,128)(2,1)}, bf16[4,512,768]{2,1,0:T(8,128)(2,1)}, u32[]{:S(2)}, u32[]{:S(2)}) collective-permute-start(bf16[4,512,768]{2,1,0:T(8,128)(2,1)} %weight_part.6.refs_4_), channel_id=1, source_target_pairs={{0,16},{16,0},{32,48},{48,32},{64,80},{80,64},{96,112},{112,96},{1... | collective-permute-start | bytes 9437192 | tf_op jit(solution)/shard_map/ppermute | solution.py:461
  154.0 59.0 %all-to-all-start.1 = ((bf16[16,32,4096]{2,1,0:T(8,128)(2,1)}), bf16[16,32,4096]{2,1,0:T(8,128)(2,1)}, u32[]{:S(2)}, u32[]{:S(2)}) async-start(bf16[16,32,4096]{2,1,0:T(8,128)(2,1)} %bitcast.22), calls=%async_computation.1 | async-start | bytes 8388608 | tf_op jit(solution)/shard_map/all_to_all | solution.py:454
  160.9 16.1 %collective-permute-start.5 = (bf16[384,512]{1,0:T(8,128)(2,1)}, bf16[384,512]{1,0:T(8,128)(2,1)}, u32[]{:S(2)}, u32[]{:S(2)}) collective-permute-start(bf16[384,512]{1,0:T(8,128)(2,1)} %get-tuple-element.46.refs_4_), channel_id=1, source_target_pairs={{0,32},{16,48},{32,64},{48,80},{64,96},{80,112},{96,0},{112,16},{1... | collective-permute-start | bytes 1179656 | tf_op jit(solution)/shard_map/ppermute | solution.py:464
  161.0 10.4 %copy-start.3 = (bf16[512,768]{1,0:T(8,128)(2,1)S(1)}, bf16[512,768]{1,0:T(8,128)(2,1)}, u32[]{:S(2)}) copy-start(bf16[512,768]{1,0:T(8,128)(2,1)} %copy-done.2) | copy-start | bytes 2359300
  161.0 16.0 %collective-permute-start.6 = (bf16[384,512]{1,0:T(8,128)(2,1)}, bf16[384,512]{1,0:T(8,128)(2,1)}, u32[]{:S(2)}, u32[]{:S(2)}) collective-permute-start(bf16[384,512]{1,0:T(8,128)(2,1)} %get-tuple-element.47.refs_5_), channel_id=1, source_target_pairs={{0,96},{16,112},{32,0},{48,16},{64,32},{80,48},{96,64},{112,80},{1... | collective-permute-start | bytes 1179656 | tf_op jit(solution)/shard_map/ppermute | solution.py:464
  169.9 20.2 %collective-permute-start.10 = (bf16[2,256,768]{2,1,0:T(8,128)(2,1)}, bf16[2,256,768]{2,1,0:T(8,128)(2,1)}, u32[]{:S(2)}, u32[]{:S(2)}) collective-permute-start(bf16[2,256,768]{2,1,0:T(8,128)(2,1)} %get-tuple-element.49.refs_4_), channel_id=1, source_target_pairs={{0,96},{16,112},{32,0},{48,16},{64,32},{80,48},{96,64},{112,80},{1... | collective-permute-start | bytes 2359304 | tf_op jit(solution)/shard_map/ppermute | solution.py:464
  170.9 19.3 %collective-permute-start.9 = (bf16[2,256,768]{2,1,0:T(8,128)(2,1)}, bf16[2,256,768]{2,1,0:T(8,128)(2,1)}, u32[]{:S(2)}, u32[]{:S(2)}) collective-permute-start(bf16[2,256,768]{2,1,0:T(8,128)(2,1)} %get-tuple-element.48.refs_3_), channel_id=1, source_target_pairs={{0,32},{16,48},{32,64},{48,80},{64,96},{80,112},{96,0},{112,16},{1... | collective-permute-start | bytes 2359304 | tf_op jit(solution)/shard_map/ppermute | solution.py:464
  175.5 6.8 %collective-permute-start.4 = (bf16[4,512,768]{2,1,0:T(8,128)(2,1)S(1)}, bf16[4,512,768]{2,1,0:T(8,128)(2,1)S(1)}, u32[]{:S(2)}, u32[]{:S(2)}) collective-permute-start(bf16[4,512,768]{2,1,0:T(8,128)(2,1)S(1)} %weight_part.8.refs_5_), channel_id=1, source_target_pairs={{0,16},{16,0},{32,48},{48,32},{64,80},{80,64},{96,112},{112,96},{1... | collective-permute-start | bytes 9437192 | tf_op jit(solution)/shard_map/ppermute | solution.py:461
  187.5 20.9 %collective-permute-start.7 = (bf16[2,256,768]{2,1,0:T(8,128)(2,1)S(1)}, bf16[2,256,768]{2,1,0:T(8,128)(2,1)S(1)}, u32[]{:S(2)}, u32[]{:S(2)}) collective-permute-start(bf16[2,256,768]{2,1,0:T(8,128)(2,1)S(1)} %get-tuple-element.55.refs_4_), channel_id=1, source_target_pairs={{0,32},{16,48},{32,64},{48,80},{64,96},{80,112},{96,0},{112,16},{1... | collective-permute-start | bytes 2359304 | tf_op jit(solution)/shard_map/ppermute | solution.py:464
  187.5 20.9 %collective-permute-start.8 = (bf16[2,256,768]{2,1,0:T(8,128)(2,1)S(1)}, bf16[2,256,768]{2,1,0:T(8,128)(2,1)S(1)}, u32[]{:S(2)}, u32[]{:S(2)}) collective-permute-start(bf16[2,256,768]{2,1,0:T(8,128)(2,1)S(1)} %get-tuple-element.56.refs_5_), channel_id=1, source_target_pairs={{0,96},{16,112},{32,0},{48,16},{64,32},{80,48},{96,64},{112,80},{1... | collective-permute-start | bytes 2359304 | tf_op jit(solution)/shard_map/ppermute | solution.py:464
  191.8 25.0 %collective-permute-start.11 = (bf16[256,768]{1,0:T(8,128)(2,1)S(1)}, bf16[256,768]{1,0:T(8,128)(2,1)S(1)}, u32[]{:S(2)}, u32[]{:S(2)}) collective-permute-start(bf16[256,768]{1,0:T(8,128)(2,1)S(1)} %get-tuple-element.57.refs_4_), channel_id=1, source_target_pairs={{0,32},{16,48},{32,64},{48,80},{64,96},{80,112},{96,0},{112,16},{1... | collective-permute-start | bytes 1179656 | tf_op jit(solution)/shard_map/ppermute | solution.py:464
  191.8 24.9 %collective-permute-start.12 = (bf16[256,768]{1,0:T(8,128)(2,1)S(1)}, bf16[256,768]{1,0:T(8,128)(2,1)S(1)}, u32[]{:S(2)}, u32[]{:S(2)}) collective-permute-start(bf16[256,768]{1,0:T(8,128)(2,1)S(1)} %get-tuple-element.58.refs_5_), channel_id=1, source_target_pairs={{0,96},{16,112},{32,0},{48,16},{64,32},{80,48},{96,64},{112,80},{1... | collective-permute-start | bytes 1179656 | tf_op jit(solution)/shard_map/ppermute | solution.py:464
  209.3 15.8 %collective-permute-start.13 = (bf16[256,768]{1,0:T(8,128)(2,1)}, bf16[256,768]{1,0:T(8,128)(2,1)S(1)}, u32[]{:S(2)}, u32[]{:S(2)}) collective-permute-start(bf16[256,768]{1,0:T(8,128)(2,1)} %get-tuple-element.59.refs_2_), channel_id=1, source_target_pairs={{0,32},{16,48},{32,64},{48,80},{64,96},{80,112},{96,0},{112,16},{1... | collective-permute-start | bytes 1179656 | tf_op jit(solution)/shard_map/ppermute | solution.py:464
  209.3 15.8 %collective-permute-start.14 = (bf16[256,768]{1,0:T(8,128)(2,1)}, bf16[256,768]{1,0:T(8,128)(2,1)}, u32[]{:S(2)}, u32[]{:S(2)}) collective-permute-start(bf16[256,768]{1,0:T(8,128)(2,1)} %get-tuple-element.60.refs_3_), channel_id=1, source_target_pairs={{0,96},{16,112},{32,0},{48,16},{64,32},{80,48},{96,64},{112,80},{1... | collective-permute-start | bytes 1179656 | tf_op jit(solution)/shard_map/ppermute | solution.py:464
